TPU v7x, 32 devices: a whole 2x2x4 slice. The times are simulated.
32 devices in a mesh: dp: 8 (over y, x, core), tensor: 4 (over z).
Axes of the slice: x: 2, y: 2, z: 4, core: 2. Of those that a mesh axis runs over, the one named last changes fastest.
Arguments:
- tokens: bfloat16 [4096, 6144], P('dp', 'tensor'), may hold values from -6 to 6
- block_mask: int32 [16, 4, 4], P('dp'), may hold values from 0 to 1
- norm_gain: float32 [6144], replicated, may hold values from 0.25 to 1.75
- w_query: bfloat16 [6144, 3072], P('dp', 'tensor'), may hold values from -0.078125 to 0.078125
- w_key: bfloat16 [6144, 3072], P('dp', 'tensor'), may hold values from -0.078125 to 0.078125
- w_value: bfloat16 [6144, 3072], P('dp', 'tensor'), may hold values from -0.078125 to 0.078125
- query_gain: float32 [128], replicated, may hold values from 0.1 to 1.9
- key_gain: float32 [128], replicated, may hold values from 0.1 to 1.9
Outputs:
- attended: bfloat16 [4096, 3072], P('dp', 'tensor')
All inputs are finite; a program needn't handle non-finite values.
Results may differ from a plain program's by a relative error of at most 0.0085.
Values may be sent and summed in bfloat16 or wider, within the bound.
No kernel may reach another device: no remote copies, remote signals or barrier semaphores. Data moves between devices by JAX's collectives and lax.ppermute only.
A program may use at most 192 MiB of HBM per device.

v0:
```python
import jax
import jax.numpy as jnp
from jax import lax
from jax.sharding import PartitionSpec as P

DH = 128
TPD = 256
BLOCK = 64


EPS = 1e-06


def layer_norm(rows, gain):
    values = rows.astype(jnp.float32)
    mean = jnp.mean(values, axis=-1, keepdims=True)
    mean_sq = jnp.mean(values * values, axis=-1, keepdims=True)
    return (values - mean) * lax.rsqrt(mean_sq - mean * mean + EPS) * gain


def head_norm(values, gain):
    mean_sq = jnp.mean(values * values, axis=-1, keepdims=True)
    return values * lax.rsqrt(mean_sq + EPS) * gain


def add_rows(normed, piece):
    return jnp.dot(normed, piece, preferred_element_type=jnp.float32)


def per_device(tokens, block_mask, norm_gain, w_query, w_key, w_value, query_gain, key_gain):
    whole = lax.all_gather(tokens, "tensor", axis=1, tiled=True)
    normed = layer_norm(whole, norm_gain).astype(jnp.bfloat16)

    def add_one(piece):
        return add_rows(normed, piece)

    query = add_one(lax.all_gather(w_query, "dp", axis=0, tiled=True))
    key = add_one(lax.all_gather(w_key, "dp", axis=0, tiled=True))
    value = add_one(lax.all_gather(w_value, "dp", axis=0, tiled=True))
    draws_here = tokens.shape[0] // TPD
    heads_here = w_query.shape[1] // DH
    query_n = head_norm(query.reshape(draws_here, TPD, heads_here, DH), query_gain).astype(
        jnp.bfloat16
    )
    key_n = head_norm(key.reshape(draws_here, TPD, heads_here, DH), key_gain).astype(jnp.bfloat16)
    value = value.astype(jnp.bfloat16).reshape(draws_here, TPD, heads_here, DH)
    blocks = block_mask.shape[-1]
    allowed = (block_mask > 0) | (jnp.arange(blocks)[:, None] == jnp.arange(blocks)[None, :])[None]
    allowed = jnp.repeat(jnp.repeat(allowed, BLOCK, axis=1), BLOCK, axis=2)
    scores = jnp.einsum(
        "bqhe,bkhe->bhqk", query_n, key_n, preferred_element_type=jnp.float32
    ) / jnp.sqrt(jnp.float32(DH))
    scores = jnp.where(allowed[:, None], scores, jnp.float32(-1e30))
    top = jnp.max(scores, axis=-1, keepdims=True)
    weights = jnp.exp(scores - top)
    probs = (weights / jnp.sum(weights, axis=-1, keepdims=True)).astype(jnp.bfloat16)
    out = jnp.einsum("bhqk,bkhe->bqhe", probs, value, preferred_element_type=jnp.float32)
    return out.astype(jnp.bfloat16).reshape(tokens.shape[0], heads_here * DH)


def solution(mesh):
    return jax.shard_map(
        per_device,
        mesh=mesh,
        in_specs=(
            P("dp", "tensor"),
            P("dp", None, None),
            P(),
            P("dp", "tensor"),
            P("dp", "tensor"),
            P("dp", "tensor"),
            P(),
            P(),
        ),
        out_specs=P("dp", "tensor"),
        check_vma=False,
    )
```

profile of v0, /device:TPU:0, one launch (start us, length us, event | category | flops | bytes accessed | tf_op | source)
XLA Modules:
  0.0 333.0 jit_solution(2809300179781047278)
XLA Ops:
  6.5 0.7 all-gather.5.cloned.1.call-update
  7.3 0.0 all-gather.11.cloned.1.call-start
  7.3 0.7 all-gather.11.cloned.1.call-update
  8.0 0.0 all-gather.9.cloned.1.call-start
  8.1 0.7 all-gather.9.cloned.1.call-update
  8.7 0.0 all-gather.7.cloned.1.call-start
  8.8 0.5 all-gather.7.cloned.1.call-update
  9.4 0.1 copy.15
  9.5 0.1 broadcast_in_dim.14
  9.6 0.1 reshape.68
  9.6 117.4 %all-gather.5.cloned.1.call-done = bf16[512,6144]{1,0:T(8,128)(2,1)} async-done(((bf16[512,1536]{1,0:T(8,128)(2,1)}), bf16[512,6144]{1,0:T(8,128)(2,1)}) %all-gather.5.cloned.1.call-update) | async-done | bytes 6291472 | tf_op jit(solution)/shard_map/all_gather | solution.py:31
  127.0 5.0 %convert_reduce_fusion = (f32[512]{0:T(512)S(1)}, f32[512]{0:T(512)S(1)}) fusion(bf16[512,6144]{1,0:T(8,128)(2,1)} %all-gather.5.cloned.1.call-done), kind=kLoop, calls=%fused_computation.3 | loop fusion | flops 12581888 | bytes 6295552 | tf_op jit(solution)/shard_map/reduce_sum | solution.py:16
  132.0 6.2 %fusion.3 = bf16[512,6144]{1,0:T(8,128)(2,1)} fusion(bf16[512,6144]{1,0:T(8,128)(2,1)S(1)} %copy-done, f32[6144]{0:T(1024)S(1)} %copy-done.2, f32[512]{0:T(512)S(1)} %get-tuple-element.8, f32[512]{0:T(512)S(1)} %get-tuple-element.7), kind=kLoop, calls=%fused_computation.6 | loop fusion | flops 15728640 | bytes 12611584 | tf_op jit(solution)/shard_map/convert_element_type | solution.py:32
  138.2 47.7 %all-gather.11.cloned.1.call-done = bf16[6144,768]{1,0:T(8,128)(2,1)} async-done(((bf16[768,768]{1,0:T(8,128)(2,1)}), bf16[6144,768]{1,0:T(8,128)(2,1)}) %all-gather.11.cloned.1.call-update) | async-done | bytes 9437200 | tf_op jit(solution)/shard_map/all_gather | solution.py:38
  185.9 9.5 %fusion.20 = f32[512,768]{0,1:T(8,128)S(1)} fusion(bf16[512,6144]{1,0:T(8,128)(2,1)} %fusion.3, bf16[6144,768]{1,0:T(8,128)(2,1)} %all-gather.11.cloned.1.call-done), kind=kOutput, calls=%fused_computation.38 | convolution fusion | flops 4831838208 | bytes 17301504 | tf_op jit(solution)/shard_map/dot_general | solution.py:27
  195.5 1.0 reshape.70
  196.5 50.2 %all-gather.9.cloned.1.call-done = bf16[6144,768]{1,0:T(8,128)(2,1)} async-done(((bf16[768,768]{1,0:T(8,128)(2,1)}), bf16[6144,768]{1,0:T(8,128)(2,1)}) %all-gather.9.cloned.1.call-update) | async-done | bytes 9437200 | tf_op jit(solution)/shard_map/all_gather | solution.py:37
  246.7 13.3 %fusion.19 = f32[512,768]{0,1:T(8,128)} fusion(bf16[512,6144]{1,0:T(8,128)(2,1)} %fusion.3, bf16[6144,768]{1,0:T(8,128)(2,1)} %all-gather.9.cloned.1.call-done), kind=kOutput, calls=%fused_computation.37 | convolution fusion | flops 4831838208 | bytes 17301504 | tf_op jit(solution)/shard_map/dot_general | solution.py:27
  260.0 2.3 reshape.69
  262.2 0.6 multiply_reduce_fusion
  262.9 0.6 multiply_reduce_fusion.1
  263.5 0.0 copy-start.4
  263.5 43.8 %all-gather.7.cloned.1.call-done = bf16[6144,768]{1,0:T(8,128)(2,1)} async-done(((bf16[768,768]{1,0:T(8,128)(2,1)}), bf16[6144,768]{1,0:T(8,128)(2,1)}) %all-gather.7.cloned.1.call-update) | async-done | bytes 9437200 | tf_op jit(solution)/shard_map/all_gather | solution.py:39
  307.3 10.6 %convolution_convert_fusion = bf16[512,768]{1,0:T(8,128)(2,1)} fusion(bf16[512,6144]{1,0:T(8,128)(2,1)} %fusion.3, bf16[6144,768]{1,0:T(8,128)(2,1)} %all-gather.7.cloned.1.call-done), kind=kOutput, calls=%fused_computation.21 | convolution fusion | flops 4832231424 | bytes 16515072 | tf_op jit(solution)/shard_map/dot_general | solution.py:27
  317.9 2.7 reshape.72
  320.6 1.6 multiply_convert_fusion
  322.3 0.6 fusion.13
  322.9 1.1 fusion.18
  324.0 0.1 copy-done.1
  324.2 0.5 fusion.11
  324.7 0.8 copy.29
  325.4 1.0 copy.39
  (17 shorter events, 0.1 us)
Async XLA Ops:
  6.5 2.8 copy-start.3
  6.5 120.5 %all-gather.5.cloned.1.call-start = ((), (), s32[]{:S(2)}) async-start(), calls=%async_computation | async-start | bytes 7864320 | tf_op jit(solution)/shard_map/all_gather | solution.py:31
  7.3 178.7 %all-gather.11.cloned.1.call-start = ((), (), s32[]{:S(2)}) async-start(), calls=%async_computation.3 | async-start | bytes 10616832 | tf_op jit(solution)/shard_map/all_gather | solution.py:38
  8.0 238.7 %all-gather.9.cloned.1.call-start = ((), (), s32[]{:S(2)}) async-start(), calls=%async_computation.2 | async-start | bytes 10616832 | tf_op jit(solution)/shard_map/all_gather | solution.py:37
  8.7 298.6 %all-gather.7.cloned.1.call-start = ((), (), s32[]{:S(2)}) async-start(), calls=%async_computation.1 | async-start | bytes 10616832 | tf_op jit(solution)/shard_map/all_gather | solution.py:39
  9.5 122.5 %copy-start.2 = (f32[6144]{0:T(1024)S(1)}, f32[6144]{0:T(1024)}, u32[]{:S(2)}) copy-start(f32[6144]{0:T(1024)} %param.10) | copy-start | bytes 73732
  127.0 5.0 %copy-start = (bf16[512,6144]{1,0:T(8,128)(2,1)S(1)}, bf16[512,6144]{1,0:T(8,128)(2,1)}, u32[]{:S(2)}) copy-start(bf16[512,6144]{1,0:T(8,128)(2,1)} %all-gather.5.cloned.1.call-done) | copy-start | bytes 18874372
  263.5 57.1 %copy-start.4 = (f32[128]{0:T(128)S(1)}, f32[128]{0:T(128)}, u32[]{:S(2)}) copy-start(f32[128]{0:T(128)} %param.15) | copy-start | bytes 1540
  263.5 57.1 %copy-start.5 = (f32[128]{0:T(128)S(1)}, f32[128]{0:T(128)}, u32[]{:S(2)}) copy-start(f32[128]{0:T(128)} %param.14) | copy-start | bytes 1540
  322.9 1.2 copy-start.1
Sparse Core Ops, SparseCore 0:
  8.9 118.0 all-gather.4
  128.9 57.0 all-gather.10
  187.8 58.8 all-gather.8
  248.4 58.8 all-gather.6
where the time goes:
time: 333 us
  waiting for transfers between devices  262 us (79%)
  matrix products  34.5 us (10%)
  other arithmetic  15.2 us (5%)
  between operations  13.3 us (4%)
  local copies, waits for them, and re-layouts  8.22 us (2%)
    all_gather x1, waiting for transfers between devices, per_device(): whole = lax.all_gather(tokens, 'tensor', axis=1, tiled=True)  117 us
    all_gather x1, waiting for transfers between devices, per_device(): query = add_one(lax.all_gather(w_query, 'dp', axis=0, tiled=True))  50.2 us
    all_gather x1, waiting for transfers between devices, per_device(): key = add_one(lax.all_gather(w_key, 'dp', axis=0, tiled=True))  47.7 us
    all_gather x1, waiting for transfers between devices, per_device(): value = add_one(lax.all_gather(w_value, 'dp', axis=0, tiled=True))  43.8 us
    dot_general x3, matrix products, add_rows(): return jnp.dot(normed, piece, preferred_element_type=jnp.float32)  33.4 us
  transfers between devices with their start and end apart: 4, of which 4 were waited for; matrix products, arithmetic and copies ran while one was open for 12% of the time, Pallas kernels for 0%

commit v1 on v0

--- a/solution.py
+++ b/solution.py
@@ -1,6 +1,10 @@
+import functools
+
 import jax
 import jax.numpy as jnp
 from jax import lax
+from jax.experimental import pallas as pl
+from jax.experimental.pallas import tpu as pltpu
 from jax.sharding import PartitionSpec as P
 
 DH = 128
@@ -25,6 +29,12 @@
 
 def add_rows(normed, piece):
     return jnp.dot(normed, piece, preferred_element_type=jnp.float32)
+
+
+def allowed_pairs(block_mask):
+    blocks = block_mask.shape[-1]
+    allowed = (block_mask > 0) | (jnp.arange(blocks)[:, None] == jnp.arange(blocks)[None, :])[None]
+    return jnp.repeat(jnp.repeat(allowed, BLOCK, axis=1), BLOCK, axis=2)
 
 
 def per_device(tokens, block_mask, norm_gain, w_query, w_key, w_value, query_gain, key_gain):
@@ -44,9 +54,7 @@
     )
     key_n = head_norm(key.reshape(draws_here, TPD, heads_here, DH), key_gain).astype(jnp.bfloat16)
     value = value.astype(jnp.bfloat16).reshape(draws_here, TPD, heads_here, DH)
-    blocks = block_mask.shape[-1]
-    allowed = (block_mask > 0) | (jnp.arange(blocks)[:, None] == jnp.arange(blocks)[None, :])[None]
-    allowed = jnp.repeat(jnp.repeat(allowed, BLOCK, axis=1), BLOCK, axis=2)
+    allowed = allowed_pairs(block_mask)
     scores = jnp.einsum(
         "bqhe,bkhe->bhqk", query_n, key_n, preferred_element_type=jnp.float32
     ) / jnp.sqrt(jnp.float32(DH))
@@ -58,9 +66,402 @@
     return out.astype(jnp.bfloat16).reshape(tokens.shape[0], heads_here * DH)
 
 
+CORE, X, Y = 1, 2, 4
+
+PLACES = ((0, 1, 2, 3), (1, 0, 2, 3), (2, 3, 1, 0), (3, 2, 1, 0))
+
+
+def arrival(z, place):
+    return z - place if place <= z else 3 + place - z
+
+
+def plan(z, chip):
+    diagonal = chip ^ 3
+    order = [place for place in PLACES[z] if place != diagonal] + [diagonal]
+    pairs = [number for place in order for number in (PLACES[z].index(place), place ^ chip)]
+    return pairs + list(PLACES[z]) + [arrival(z, place) for place in PLACES[z]]
+
+
+PLAN = [[plan(z, chip) for chip in range(4)] for z in range(4)]
+PLACE, ARRIVAL, CORE_AT = 8, 12, 16
+
+HBM = pl.BlockSpec(memory_space=pltpu.HBM)
+ANY = pl.BlockSpec(memory_space=pl.ANY)
+VMEM = pl.BlockSpec(memory_space=pltpu.VMEM)
+SMEM = pl.BlockSpec(memory_space=pltpu.SMEM)
+FREE = pl.CostEstimate(flops=0, bytes_accessed=0, transcendentals=0)
+PARAMS = pltpu.CompilerParams(vmem_limit_bytes=56 * 2**20)
+
+
+def swap(array, bits):
+    return lax.ppermute(array, "dp", [(i, i ^ bits) for i in range(8)])
+
+
+def gate(arrays, others):
+    return pl.pallas_call(
+        lambda *refs: None,
+        in_specs=[ANY] * (len(arrays) + len(others)),
+        out_specs=[ANY] * len(arrays),
+        out_shape=[jax.ShapeDtypeStruct(array.shape, array.dtype) for array in arrays],
+        input_output_aliases={number: number for number in range(len(arrays))},
+        compiler_params=PARAMS,
+        cost_estimate=FREE,
+    )(*arrays, *others)
+
+
+def pack_kernel(plan_ref, *refs):
+    weights, outs, held, packed, in_sems, out_sems = refs[:3], refs[3:5], refs[5], refs[6], refs[7], refs[8]
+    core = plan_ref[CORE_AT]
+    _, heads, _, _ = packed.shape
+    width = heads * DH
+
+    def load(number, kind):
+        first = pl.multiple_of((core if number == 0 else 1 - core) * width, DH)
+        return pltpu.make_async_copy(
+            weights[kind].at[:, pl.ds(first, width)], held.at[number, kind], in_sems.at[number, kind]
+        )
+
+    def store(number, h):
+        return pltpu.make_async_copy(packed.at[number, h], outs[number].at[h], out_sems.at[number, h])
+
+    for number in range(2):
+        for kind in range(3):
+            load(number, kind).start()
+    for number in range(2):
+        for kind in range(3):
+            load(number, kind).wait()
+        for h in range(heads):
+            for kind in range(3):
+                packed[number, h, :, kind * DH : (kind + 1) * DH] = held[
+                    number, kind, :, h * DH : (h + 1) * DH
+                ]
+            store(number, h).start()
+    for number in range(2):
+        for h in range(heads):
+            store(number, h).wait()
+
+
+def pack(plan_here, *weights):
+    rows, columns = weights[0].shape
+    heads = columns // (2 * DH)
+    packed = jax.ShapeDtypeStruct((heads, rows, 3 * DH), jnp.bfloat16)
+    return pl.pallas_call(
+        pack_kernel,
+        in_specs=[SMEM] + [HBM] * 3,
+        out_specs=[HBM] * 2,
+        out_shape=[packed] * 2,
+        scratch_shapes=[
+            pltpu.VMEM((2, 3, rows, heads * DH), jnp.bfloat16),
+            pltpu.VMEM((2, heads, rows, 3 * DH), jnp.bfloat16),
+            pltpu.SemaphoreType.DMA((2, 3)),
+            pltpu.SemaphoreType.DMA((2, heads)),
+        ],
+        compiler_params=PARAMS,
+        cost_estimate=FREE,
+    )(plan_here, *weights)
+
+
+def fetch(chosen, choices, target, sem):
+    for number, choice in choices.items():
+
+        @pl.when(chosen == number)
+        def _():
+            pltpu.make_async_copy(choice, target, sem).start()
+
+
+def norm_kernel(slots, numbers, plan_ref, mean_ref, scale_ref, gains_ref, *refs):
+    arrays = dict(zip(numbers, refs))
+    outs, (raw, normed, in_sems, out_sems) = refs[-4 - len(slots) : -4], refs[-4:]
+    rows = raw.shape[1]
+    step = 64
+    for n, slot in enumerate(slots):
+        fetch(plan_ref[ARRIVAL + slot], arrays, raw.at[n], in_sems.at[n])
+    for n, slot in enumerate(slots):
+        pltpu.make_async_copy(refs[0], raw.at[n], in_sems.at[n]).wait()
+        gain = gains_ref[pl.ds(plan_ref[PLACE + slot], 1), :]
+
+        @pl.loop(0, rows // step)
+        def _(tile):
+            at = pl.ds(pl.multiple_of(tile * step, step), step)
+            values = raw[n, at, :].astype(jnp.float32)
+            normed[n, at, :] = ((values - mean_ref[at, :]) * scale_ref[at, :] * gain).astype(jnp.bfloat16)
+
+        pltpu.make_async_copy(normed.at[n], outs[n], out_sems.at[n]).start()
+    for n, slot in enumerate(slots):
+        pltpu.make_async_copy(normed.at[n], outs[n], out_sems.at[n]).wait()
+
+
+def norm(plan_here, slots, mean, scale, gains, arrays, *others):
+    rows, features = next(iter(arrays.values())).shape
+    shape = (len(slots), rows, features)
+    return pl.pallas_call(
+        functools.partial(norm_kernel, slots, tuple(arrays)),
+        in_specs=[SMEM] + [VMEM] * 3 + [ANY] * (len(arrays) + len(others)),
+        out_specs=[HBM] * len(slots),
+        out_shape=[jax.ShapeDtypeStruct(shape[1:], jnp.bfloat16)] * len(slots),
+        scratch_shapes=[
+            pltpu.VMEM(shape, jnp.bfloat16),
+            pltpu.VMEM(shape, jnp.bfloat16),
+            pltpu.SemaphoreType.DMA((len(slots),)),
+            pltpu.SemaphoreType.DMA((len(slots),)),
+        ],
+        compiler_params=PARAMS,
+        cost_estimate=FREE,
+    )(plan_here, mean, scale, gains, *arrays.values(), *others)
+
+
+def project_kernel(count, first, size, has_acc, plan_ref, *refs):
+    here, there = dict(enumerate(refs[:size])), dict(enumerate(refs[size : 2 * size]))
+    same, cross = dict(enumerate(refs[2 * size : 2 * size + 3])), dict(enumerate(refs[2 * size + 3 : 2 * size + 6]))
+    rest = refs[2 * size + 6 :]
+    if has_acc:
+        acc_in, rest = rest[0], rest[1:]
+    acc_ref, tokens, weights, total, token_sems, weight_sems, acc_sems = rest
+    core = plan_ref[CORE_AT]
+    heads, depth, _ = same[0].shape
+    rows = here[0].shape[0]
+
+    def weight_copy(n, part, h):
+        return pltpu.make_async_copy(same[0].at[h], weights.at[n, part, h], weight_sems.at[n, part, h])
+
+    def token_copy(n, side):
+        at = pl.ds(side * rows, rows)
+        return pltpu.make_async_copy(here[0], tokens.at[n, at], token_sems.at[n, side])
+
+    def store(h):
+        return pltpu.make_async_copy(total.at[h], acc_ref.at[h], acc_sems.at[1, h])
+
+    def load(h):
+        return pltpu.make_async_copy(acc_in.at[h], total.at[h], acc_sems.at[0, h])
+
+    for n in range(count):
+        slot, bits = plan_ref[2 * (first + n)], plan_ref[2 * (first + n) + 1]
+        for h in range(heads):
+            for part, choices in enumerate((same, cross)):
+                views = {number: choice.at[h] for number, choice in choices.items()}
+                fetch(bits, views, weights.at[n, part, h], weight_sems.at[n, part, h])
+            if h == 0:
+                for side, choices in enumerate((here, there)):
+                    fetch(slot, choices, tokens.at[n, pl.ds(side * rows, rows)], token_sems.at[n, side])
+            if has_acc and n == 0:
+                load(h).start()
+    for n in range(count):
+        for side in range(2):
+            token_copy(n, side).wait()
+
+        @pl.loop(0, heads)
+        def _(h):
+            update = None
+            for part in range(2):
+                weight_copy(n, part, h).wait()
+                offset = pl.multiple_of((core if part == 0 else 1 - core) * depth, depth)
+                product = jnp.dot(
+                    tokens[n, :, pl.ds(offset, depth)],
+                    weights[n, part, h],
+                    preferred_element_type=jnp.float32,
+                )
+                update = product if update is None else update + product
+            if has_acc and n == 0:
+                load(h).wait()
+            if has_acc or n > 0:
+                update = update + total[h]
+            total[h] = update
+            if n == count - 1:
+                store(h).start()
+
+    for h in range(heads):
+        store(h).wait()
+
+
+def project(plan_here, count, first, here, there, same, cross, acc=None):
+    heads, depth, width = same[0].shape
+    rows, features = here[0].shape
+    operands = [*here, *there, *same, *cross] + ([] if acc is None else [acc])
+    return pl.pallas_call(
+        functools.partial(project_kernel, count, first, len(here), acc is not None),
+        in_specs=[SMEM] + [ANY] * len(operands),
+        out_specs=HBM,
+        out_shape=jax.ShapeDtypeStruct((heads, 2 * rows, width), jnp.float32),
+        scratch_shapes=[
+            pltpu.VMEM((count, 2 * rows, features), jnp.bfloat16),
+            pltpu.VMEM((count, 2, heads, depth, width), jnp.bfloat16),
+            pltpu.VMEM((heads, 2 * rows, width), jnp.float32),
+            pltpu.SemaphoreType.DMA((count, 2)),
+            pltpu.SemaphoreType.DMA((count, 2, heads)),
+            pltpu.SemaphoreType.DMA((2, heads)),
+        ],
+        compiler_params=PARAMS,
+        cost_estimate=FREE,
+    )(plan_here, *operands)
+
+
+def attend(query, key, value, mask_ref, draw):
+    scores = lax.dot_general(
+        query, key, (((1,), (1,)), ((), ())), preferred_element_type=jnp.float32
+    ) / jnp.sqrt(jnp.float32(DH))
+    blocks = TPD // BLOCK
+    column = lax.broadcasted_iota(jnp.int32, (1, TPD), 1) // BLOCK
+    bands = []
+    for i in range(blocks):
+        allowed = column == i
+        for j in range(blocks):
+            allowed = allowed | ((column == j) & (mask_ref[(draw * blocks + i) * blocks + j] > 0))
+        bands.append(
+            jnp.where(allowed, scores[i * BLOCK : (i + 1) * BLOCK], jnp.float32(-1e30))
+        )
+    scores = jnp.concatenate(bands, axis=0)
+    top = jnp.max(scores, axis=-1, keepdims=True)
+    weights = jnp.exp(scores - top)
+    probs = (weights / jnp.sum(weights, axis=-1, keepdims=True)).astype(jnp.bfloat16)
+    return jnp.dot(probs, value, preferred_element_type=jnp.float32).astype(jnp.bfloat16)
+
+
+def head_kernel(size, plan_ref, mask_ref, *refs):
+    sides = dict(enumerate(refs[:size])), dict(enumerate(refs[size : 2 * size]))
+    same, cross, acc, query_gain, key_gain, out_ref = refs[2 * size : 2 * size + 6]
+    tokens, weights, total, out, token_sems, weight_sems, acc_sems, out_sems = refs[2 * size + 6 :]
+    core = plan_ref[CORE_AT]
+    heads, depth, _ = same.shape
+    rows = sides[0][0].shape[0]
+
+    def token_copy(side):
+        return pltpu.make_async_copy(sides[0][0], tokens.at[side], token_sems.at[side])
+
+    def weight_copy(part, h):
+        return pltpu.make_async_copy((same, cross)[part].at[h], weights.at[part, h], weight_sems.at[part, h])
+
+    def acc_copy(side, h):
+        return pltpu.make_async_copy(acc.at[h, pl.ds(side * rows, rows)], total.at[side, h], acc_sems.at[side, h])
+
+    def out_copy(side, h):
+        whose = core if side == 0 else 1 - core
+        return pltpu.make_async_copy(out.at[side, h], out_ref.at[whose, h], out_sems.at[side, h])
+
+    for h in range(heads):
+        weight_copy(0, h).start()
+        weight_copy(1, h).start()
+        for side in range(2):
+            if h == 0:
+                fetch(plan_ref[6], sides[side], tokens.at[side], token_sems.at[side])
+            acc_copy(side, h).start()
+    for h in range(heads):
+        weight_copy(0, h).wait()
+        weight_copy(1, h).wait()
+        for side in range(2):
+            if h == 0:
+                token_copy(side).wait()
+            acc_copy(side, h).wait()
+            sums = total[side, h]
+            for part in range(2):
+                offset = pl.multiple_of((core if part == 0 else 1 - core) * depth, depth)
+                sums = sums + jnp.dot(
+                    tokens[side, :, pl.ds(offset, depth)],
+                    weights[part, h],
+                    preferred_element_type=jnp.float32,
+                )
+            query = head_norm(sums[:, :DH], query_gain[...]).astype(jnp.bfloat16)
+            key = head_norm(sums[:, DH : 2 * DH], key_gain[...]).astype(jnp.bfloat16)
+            value = sums[:, 2 * DH :].astype(jnp.bfloat16)
+            draws = rows // TPD
+            for draw in range(draws):
+                at = slice(draw * TPD, (draw + 1) * TPD)
+                out[side, h, at, :] = attend(query[at], key[at], value[at], mask_ref, side * draws + draw)
+            out_copy(side, h).start()
+    for side in range(2):
+        for h in range(heads):
+            out_copy(side, h).wait()
+
+
+def attend_heads(plan_here, mask, here, there, same, cross, acc, query_gain, key_gain):
+    heads, depth, width = same.shape
+    rows, features = here[0].shape
+    return pl.pallas_call(
+        functools.partial(head_kernel, len(here)),
+        in_specs=[SMEM] * 2 + [ANY] * (2 * len(here) + 3) + [VMEM] * 2,
+        out_specs=HBM,
+        out_shape=jax.ShapeDtypeStruct((2, heads, rows, DH), jnp.bfloat16),
+        scratch_shapes=[
+            pltpu.VMEM((2, rows, features), jnp.bfloat16),
+            pltpu.VMEM((2, heads, depth, width), jnp.bfloat16),
+            pltpu.VMEM((2, heads, rows, width), jnp.float32),
+            pltpu.VMEM((2, heads, rows, DH), jnp.bfloat16),
+            pltpu.SemaphoreType.DMA((2,)),
+            pltpu.SemaphoreType.DMA((2, heads)),
+            pltpu.SemaphoreType.DMA((2, heads)),
+            pltpu.SemaphoreType.DMA((2, heads)),
+        ],
+        compiler_params=PARAMS,
+        cost_estimate=FREE,
+    )(plan_here, mask, *here, *there, same, cross, acc, query_gain, key_gain)
+
+
+def per_device_8x4(tokens, block_mask, norm_gain, w_query, w_key, w_value, query_gain, key_gain):
+    features = tokens.shape[1]
+    heads = w_query.shape[1] // (2 * DH)
+    dp, z = lax.axis_index("dp"), lax.axis_index("tensor")
+    core = (dp % 2).astype(jnp.int32)
+    plan_here = jnp.asarray(PLAN, jnp.int32)[z, dp // 2]
+    plan_here = jnp.concatenate([plan_here, core[None]])
+
+    def up(array, first):
+        return lax.ppermute(array, "tensor", [(i, i + 1) for i in range(first, 3)])
+
+    def down(array, last):
+        return lax.ppermute(array, "tensor", [(i + 1, i) for i in range(last)])
+
+    values = tokens.astype(jnp.float32)
+    stats = jnp.stack([jnp.sum(values, axis=1), jnp.sum(values * values, axis=1)])
+    mine, other = pack(plan_here, w_query, w_key, w_value)
+
+    x_same, y_cross = swap(mine, X), swap(other, Y | CORE)
+    up1, down1 = up(tokens, 0), down(tokens, 3)
+    (stats,) = gate((stats,), ())
+    stats = stats + lax.ppermute(stats, "tensor", [(i, i ^ 1) for i in range(4)])
+    mask = block_mask.astype(jnp.float32).reshape(-1)
+    mask = jnp.concatenate([mask, swap(mask, CORE)])
+
+    mine, other = gate((mine, other), (x_same, y_cross, mask))
+    x_cross, y_same = swap(other, X | CORE), swap(mine, Y)
+    own_cross = swap(other, CORE)
+    stats = stats + lax.ppermute(stats, "tensor", [(i, i ^ 2) for i in range(4)])
+    up1, down1 = gate((up1, down1), (stats,))
+    up2, down2 = up(up1, 1), down(down1, 2)
+
+    total = stats / (4 * features)
+    mean = total[0][:, None]
+    scale = lax.rsqrt(total[1] - total[0] * total[0] + EPS)[:, None]
+    gains = norm_gain.reshape(4, features)
+    arrived = {0: tokens, 1: up1, 4: down1}
+    here = list(norm(plan_here, (0, 1), mean, scale, gains, arrived))
+    there = [swap(chunk, CORE) for chunk in here]
+
+    x_same, y_cross = gate(
+        (x_same, y_cross), (x_cross, y_same, own_cross)
+    )
+    diag_same, diag_cross = swap(x_same, Y), swap(y_cross, X)
+    up3, down3 = up(up2, 2), down(down2, 1)
+    arrived = {1: up1, 2: up2, 4: down1, 5: down2}
+    here += norm(plan_here, (2,), mean, scale, gains, arrived)
+    there.append(swap(here[2], CORE))
+    same, cross = [mine, x_same, y_same], [own_cross, x_cross, y_cross]
+    acc = project(plan_here, 2, 0, here, there, same, cross)
+
+    arrived = {2: up2, 3: up3, 5: down2, 6: down3}
+    here += norm(plan_here, (3,), mean, scale, gains, arrived, acc)
+    there.append(swap(here[3], CORE))
+    acc = project(plan_here, 1, 2, here, there, same, cross, acc)
+
+    out = attend_heads(
+        plan_here, mask, here, there, diag_same, diag_cross, acc, query_gain[None, :], key_gain[None, :]
+    )
+    out = lax.all_to_all(out, "dp", 0, 0, axis_index_groups=[[i, i + 1] for i in range(0, 8, 2)])
+    return jnp.concatenate([out[i // heads, i % heads] for i in range(2 * heads)], axis=1)
+
+
 def solution(mesh):
+    eight_by_four = dict(mesh.shape) == {"dp": 8, "tensor": 4}
     return jax.shard_map(
-        per_device,
+        per_device_8x4 if eight_by_four else per_device,
         mesh=mesh,
         in_specs=(
             P("dp", "tensor"),

time: 333 us -> 195 us (0.59)
  waiting for transfers between devices: 262 us -> 82.6 us
  Pallas kernels: 0 us -> 61.4 us
  matrix products: 34.5 us -> 0 us
  starting transfers between devices: 0.12 us -> 24.5 us
  between operations: 13.3 us -> 0.29 us
  other arithmetic: 15.2 us -> 6.94 us
  blocking collectives: 0 us -> 5.46 us
  local copies, waits for them, and re-layouts: 8.22 us -> 13.2 us
    all_gather x4 -> x0, waiting for transfers between devices: 259 us -> none  [the longest x1 117 us: per_device(): whole = lax.all_gather(tokens, 'tensor', axis=1, tiled=True)]
    ppermute x0 -> x20, waiting for transfers between devices: none -> 82.6 us  [the longest x3 43.4 us: down(): return lax.ppermute(array, 'tensor', [(i + 1, i) for i in range(last)])]
    pallas_call x0 -> x11, Pallas kernels: none -> 61.4 us  [the longest x2 28.8 us: project(): pl.pallas_call(functools.partial(project_kernel, count, first, len(here),...]
    dot_general x5 -> x0, matrix products: 34.5 us -> none  [the longest x3 33.4 us: add_rows(): return jnp.dot(normed, piece, preferred_element_type=jnp.float32)]
    ppermute x0 -> x20, starting transfers between devices: none -> 24.5 us  [the longest x3 8.28 us: up(): return lax.ppermute(array, 'tensor', [(i, i + 1) for i in range(first, 3)])]
    convert_element_type x2 -> x1, other arithmetic: 7.83 us -> 0.01 us  [per_device_8x4(): mask = block_mask.astype(jnp.float32).reshape(-1)]
    unnamed x13 -> x29, local copies, waits for them, and re-layouts: 1.15 us -> 7.78 us
    all_to_all x0 -> x1, blocking collectives: none -> 5.46 us  [per_device_8x4(): lax.all_to_all(out, 'dp', 0, 0, axis_index_groups=[[i, i + 1] for i in ra...]
  transfers between devices with their start and end apart: 4 -> 20, of which waited for: 4 -> 6; matrix products, arithmetic and copies ran while one was open for 12% -> 5% of each run, Pallas kernels for 0% -> 23%
where the time goes in v1:
time: 195 us; the launch traced here: 194 us
  waiting for transfers between devices  82.6 us (42%)
  Pallas kernels  61.4 us (31%)
  starting transfers between devices  24.5 us (13%)
  local copies, waits for them, and re-layouts  13.2 us (7%)
  other arithmetic  6.94 us (4%)
  blocking collectives  5.46 us (3%)
    ppermute x3, waiting for transfers between devices, down(): return lax.ppermute(array, 'tensor', [(i + 1, i) for i in range(last)])  43.4 us
    ppermute x1, waiting for transfers between devices, per_device_8x4(): lax.ppermute(stats, 'tensor', [(i, i ^ 1) for i in range(4)])  32.6 us
    pallas_call x2, Pallas kernels, project(): pl.pallas_call(functools.partial(project_kernel, count, first, len(here),...  28.8 us
    pallas_call x3, Pallas kernels, norm(): pl.pallas_call(functools.partial(norm_kernel, slots, tuple(arrays)), in_s...  14.9 us
    pallas_call x1, Pallas kernels, attend_heads(): pl.pallas_call(functools.partial(head_kernel, len(here)), in_specs=[SMEM]...  13.6 us
    ppermute x3, starting transfers between devices, up(): return lax.ppermute(array, 'tensor', [(i, i + 1) for i in range(first, 3)])  8.28 us
    ppermute x12, starting transfers between devices, swap(): return lax.ppermute(array, 'dp', [(i, i ^ bits) for i in range(8)])  8.06 us
    unnamed x29, local copies, waits for them, and re-layouts  7.78 us
  transfers between devices with their start and end apart: 20, of which 6 were waited for; matrix products, arithmetic and copies ran while one was open for 5% of the time, Pallas kernels for 23%

profile of v1, /device:TPU:0, one launch (start us, length us, event | category | flops | bytes accessed | tf_op | source)
XLA Modules:
  0.0 194.3 jit_solution(8795420328816313562)
XLA Ops:
  1.4 4.1 %shard_map.95 = (bf16[3,768,384]{2,1,0:T(8,128)(2,1)}, bf16[3,768,384]{2,1,0:T(8,128)(2,1)}) custom-call(s32[17]{0:T(128)} %pad_add_fusion.plan_ref, bf16[768,768]{1,0:T(8,128)(2,1)} %refs_0_.3, bf16[768,768]{1,0:T(8,128)(2,1)} %refs_1_.1, bf16[768,768]{1,0:T(8,128)(2,1)} %refs_2_.1), custom_call_target="tpu_custom_call" | custom-call | tf_op jit(solution)/shard_map/pallas_call | solution.py:148
  5.4 3.0 %collective-permute-start.12 = (bf16[3,768,384]{2,1,0:T(8,128)(2,1)}, bf16[3,768,384]{2,1,0:T(8,128)(2,1)S(1)}, u32[]{:S(2)}, u32[]{:S(2)}) collective-permute-start(bf16[3,768,384]{2,1,0:T(8,128)(2,1)} %get-tuple-element.19.refs_0_), channel_id=1, source_target_pairs={{0,8},{4,12},{8,0},{12,4},{16,24},{20,28},{24,16},{28,20},{1,9},{5... | collective-permute-start | bytes 5308424 | tf_op jit(solution)/shard_map/ppermute | solution.py:97
  9.1 4.6 %collective-permute-start.3 = (bf16[512,1536]{1,0:T(8,128)(2,1)}, bf16[512,1536]{1,0:T(8,128)(2,1)}, u32[]{:S(2)}, u32[]{:S(2)}) collective-permute-start(bf16[512,1536]{1,0:T(8,128)(2,1)} %refs_0_.2), channel_id=1, source_target_pairs={{0,1},{1,2},{2,3},{4,5},{5,6},{6,7},{8,9},{9,10},{10,11},{12,13},{... | collective-permute-start | bytes 4718600 | tf_op jit(solution)/shard_map/ppermute | solution.py:407
  13.8 1.3 collective-permute-start.4
  15.1 2.0 %convert_reduce_fusion = (f32[512]{0:T(512)S(1)}, f32[512]{0:T(512)S(1)}) fusion(bf16[512,1536]{1,0:T(8,128)(2,1)} %refs_0_.2), kind=kLoop, calls=%fused_computation.1 | loop fusion | flops 3144704 | bytes 1576960 | tf_op jit(solution)/shard_map/reduce_sum | solution.py:413
  17.6 2.7 %collective-permute-start.1 = (f32[2,512]{1,0:T(2,128)}, f32[2,512]{1,0:T(2,128)S(1)}, u32[]{:S(2)}, u32[]{:S(2)}) collective-permute-start(f32[2,512]{1,0:T(2,128)} %shard_map.91), channel_id=1, source_target_pairs={{0,1},{1,0},{2,3},{3,2},{4,5},{5,4},{6,7},{7,6},{8,9},{9,8},{10,11... | collective-permute-start | bytes 12296 | tf_op jit(solution)/shard_map/ppermute | solution.py:419
  20.4 32.6 %collective-permute-done.1 = f32[2,512]{1,0:T(2,128)S(1)} collective-permute-done((f32[2,512]{1,0:T(2,128)}, f32[2,512]{1,0:T(2,128)S(1)}, u32[]{:S(2)}, u32[]{:S(2)}) %collective-permute-start.1) | collective-permute-done | bytes 4128 | tf_op jit(solution)/shard_map/ppermute | solution.py:419
  54.1 1.4 collective-permute-start.2
  56.1 2.5 %collective-permute-done.2 = f32[2,512]{1,0:T(2,128)S(1)} collective-permute-done((f32[2,512]{1,0:T(2,128)S(1)}, f32[2,512]{1,0:T(2,128)S(1)}, u32[]{:S(2)}, u32[]{:S(2)}) %collective-permute-start.2) | collective-permute-done | bytes 4128 | tf_op jit(solution)/shard_map/ppermute | solution.py:426
  59.2 1.3 copy-done
  60.5 1.2 copy-done.1
  62.3 1.8 collective-permute-start.5
  64.5 1.3 collective-permute-start.6
  65.7 1.4 reshape.33.gains_ref
  69.7 1.8 add_rsqrt_fusion.scale_ref
  71.5 5.7 %shard_map.93 = (bf16[512,1536]{1,0:T(8,128)(2,1)}, bf16[512,1536]{1,0:T(8,128)(2,1)}) custom-call(s32[17]{0:T(128)} %pad_add_fusion.plan_ref, f32[512,1]{1,0:T(8,128)} %copy.25.mean_ref, f32[512,1]{1,0:T(8,128)} %add_rsqrt_fusion.scale_ref, f32[4,1536]{1,0:T(4,128)} %reshape.33.gains_ref, bf16[512,1536]{1,0:T(8,128)(2,1)} %refs_0_.2, ...), custom_call_target="tpu_custom_call" | custom-call | tf_op jit(solution)/shard_map/pallas_call | solution.py:197
  77.4 27.2 %collective-permute-done.6.refs_3_.refs_2_ = bf16[512,1536]{1,0:T(8,128)(2,1)} collective-permute-done((bf16[512,1536]{1,0:T(8,128)(2,1)}, bf16[512,1536]{1,0:T(8,128)(2,1)}, u32[]{:S(2)}, u32[]{:S(2)}) %collective-permute-start.6) | collective-permute-done | bytes 1572896 | tf_op jit(solution)/shard_map/ppermute | solution.py:410
  104.6 4.6 %shard_map.94.refs_2_ = bf16[512,1536]{1,0:T(8,128)(2,1)} custom-call(s32[17]{0:T(128)} %pad_add_fusion.plan_ref, f32[512,1]{1,0:T(8,128)} %copy.25.mean_ref, f32[512,1]{1,0:T(8,128)} %add_rsqrt_fusion.scale_ref, f32[4,1536]{1,0:T(4,128)} %reshape.33.gains_ref, bf16[512,1536]{1,0:T(8,128)(2,1)} %get-tuple-element.15.refs_1_.refs_0_, ...), custom_call_target="tpu_custom_call" | custom-call | tf_op jit(solution)/shard_map/pallas_call | solution.py:197
  109.9 1.8 collective-permute-start.7
  111.7 1.5 collective-permute-start.8
  113.2 1.6 collective-permute-start.18
  114.8 1.1 collective-permute-start.19
  115.9 1.2 copy-done.6
  117.1 17.3 %shard_map.98.refs_4_.refs_14_ = f32[3,1024,384]{2,1,0:T(8,128)} custom-call(s32[17]{0:T(128)} %pad_add_fusion.plan_ref, bf16[512,1536]{1,0:T(8,128)(2,1)} %get-tuple-element.17.refs_0_, bf16[512,1536]{1,0:T(8,128)(2,1)} %get-tuple-element.18.refs_1_, bf16[512,1536]{1,0:T(8,128)(2,1)} %shard_map.94.refs_2_, bf16[512,1536]{1,0:T(8,128)(2,1)} %copy-done.5, ...), custom_call_target="tpu_custom_call" | custom-call | tf_op jit(solution)/shard_map/pallas_call | solution.py:280
  134.4 16.2 %collective-permute-done.8.refs_3_ = bf16[512,1536]{1,0:T(8,128)(2,1)} collective-permute-done((bf16[512,1536]{1,0:T(8,128)(2,1)}, bf16[512,1536]{1,0:T(8,128)(2,1)}, u32[]{:S(2)}, u32[]{:S(2)}) %collective-permute-start.8) | collective-permute-done | bytes 1572896 | tf_op jit(solution)/shard_map/ppermute | solution.py:410
  150.6 4.6 %shard_map.99.refs_3_ = bf16[512,1536]{1,0:T(8,128)(2,1)} custom-call(s32[17]{0:T(128)} %pad_add_fusion.plan_ref, f32[512,1]{1,0:T(8,128)} %copy.25.mean_ref, f32[512,1]{1,0:T(8,128)} %add_rsqrt_fusion.scale_ref, f32[4,1536]{1,0:T(4,128)} %reshape.33.gains_ref, bf16[512,1536]{1,0:T(8,128)(2,1)} %collective-permute-done.5.refs_1_.refs_0_, ...), custom_call_target="tpu_custom_call" | custom-call | tf_op jit(solution)/shard_map/pallas_call | solution.py:197
  155.3 3.6 %collective-permute-done.17.refs_7_ = bf16[512,1536]{1,0:T(8,128)(2,1)S(1)} collective-permute-done((bf16[512,1536]{1,0:T(8,128)(2,1)}, bf16[512,1536]{1,0:T(8,128)(2,1)S(1)}, u32[]{:S(2)}, u32[]{:S(2)}) %collective-permute-start.17) | collective-permute-done | bytes 1572896 | tf_op jit(solution)/shard_map/ppermute | solution.py:97
  158.9 1.2 copy-done.7
  160.1 11.5 %shard_map.100.refs_10_ = f32[3,1024,384]{2,1,0:T(8,128)} custom-call(s32[17]{0:T(128)} %pad_add_fusion.plan_ref, bf16[512,1536]{1,0:T(8,128)(2,1)} %get-tuple-element.17.refs_0_, bf16[512,1536]{1,0:T(8,128)(2,1)} %get-tuple-element.18.refs_1_, bf16[512,1536]{1,0:T(8,128)(2,1)} %shard_map.94.refs_2_, bf16[512,1536]{1,0:T(8,128)(2,1)} %shard_map.99.refs_3_, ...), custom_call_target="tpu_custom_call" | custom-call | tf_op jit(solution)/shard_map/pallas_call | solution.py:280
  171.7 1.2 copy-done.8
  173.5 13.6 %shard_map.101 = bf16[2,3,512,128]{3,2,1,0:T(8,128)(2,1)} custom-call(s32[17]{0:T(128)} %pad_add_fusion.plan_ref, f32[64]{0:T(128)} %pad_maximum_fusion.1.refs_4_.mask_ref, bf16[512,1536]{1,0:T(8,128)(2,1)} %get-tuple-element.17.refs_0_, bf16[512,1536]{1,0:T(8,128)(2,1)} %get-tuple-element.18.refs_1_, bf16[512,1536]{1,0:T(8,128)(2,1)} %shard_map.94.refs_2_, ...), custom_call_target="tpu_custom_call" | custom-call | tf_op jit(solution)/shard_map/pallas_call | solution.py:378
  187.1 5.5 %all_to_all.5 = bf16[2,3,512,128]{3,2,1,0:T(8,128)(2,1)S(1)} all-to-all(bf16[2,3,512,128]{3,2,1,0:T(8,128)(2,1)} %shard_map.101), channel_id=1, replica_groups={{0,4},{8,12},{16,20},{24,28},{1,5},{9,13},{17,21},{25,29},{2,6},{10,14}..., dimensions={0} | all-to-all | bytes 1572864 | tf_op jit(solution)/shard_map/all_to_all | solution.py:457
  (66 shorter events, 11.8 us)
Async XLA Ops:
  5.4 14.9 %copy-start.11 = (s32[2,4,4]{2,1,0:T(4,128)S(1)}, s32[2,4,4]{2,1,0:T(4,128)}, u32[]{:S(2)}) copy-start(s32[2,4,4]{2,1,0:T(4,128)} %param.10) | copy-start | bytes 388
  5.4 53.8 %collective-permute-start.12 = (bf16[3,768,384]{2,1,0:T(8,128)(2,1)}, bf16[3,768,384]{2,1,0:T(8,128)(2,1)S(1)}, u32[]{:S(2)}, u32[]{:S(2)}) collective-permute-start(bf16[3,768,384]{2,1,0:T(8,128)(2,1)} %get-tuple-element.19.refs_0_), channel_id=1, source_target_pairs={{0,8},{4,12},{8,0},{12,4},{16,24},{20,28},{24,16},{28,20},{1,9},{5... | collective-permute-start | bytes 5308424 | tf_op jit(solution)/shard_map/ppermute | solution.py:97
  8.4 50.8 %collective-permute-start.13 = (bf16[3,768,384]{2,1,0:T(8,128)(2,1)}, bf16[3,768,384]{2,1,0:T(8,128)(2,1)S(1)}, u32[]{:S(2)}, u32[]{:S(2)}) collective-permute-start(bf16[3,768,384]{2,1,0:T(8,128)(2,1)} %get-tuple-element.20.refs_1_), channel_id=1, source_target_pairs={{0,20},{4,16},{8,28},{12,24},{16,4},{20,0},{24,12},{28,8},{1,21},{... | collective-permute-start | bytes 5308424 | tf_op jit(solution)/shard_map/ppermute | solution.py:97
  9.1 50.1 %collective-permute-start.3 = (bf16[512,1536]{1,0:T(8,128)(2,1)}, bf16[512,1536]{1,0:T(8,128)(2,1)}, u32[]{:S(2)}, u32[]{:S(2)}) collective-permute-start(bf16[512,1536]{1,0:T(8,128)(2,1)} %refs_0_.2), channel_id=1, source_target_pairs={{0,1},{1,2},{2,3},{4,5},{5,6},{6,7},{8,9},{9,10},{10,11},{12,13},{... | collective-permute-start | bytes 4718600 | tf_op jit(solution)/shard_map/ppermute | solution.py:407
  13.8 45.5 %collective-permute-start.4 = (bf16[512,1536]{1,0:T(8,128)(2,1)}, bf16[512,1536]{1,0:T(8,128)(2,1)}, u32[]{:S(2)}, u32[]{:S(2)}) collective-permute-start(bf16[512,1536]{1,0:T(8,128)(2,1)} %refs_0_.2), channel_id=1, source_target_pairs={{1,0},{2,1},{3,2},{5,4},{6,5},{7,6},{9,8},{10,9},{11,10},{13,12},{... | collective-permute-start | bytes 4718600 | tf_op jit(solution)/shard_map/ppermute | solution.py:410
  17.6 35.3 %collective-permute-start.1 = (f32[2,512]{1,0:T(2,128)}, f32[2,512]{1,0:T(2,128)S(1)}, u32[]{:S(2)}, u32[]{:S(2)}) collective-permute-start(f32[2,512]{1,0:T(2,128)} %shard_map.91), channel_id=1, source_target_pairs={{0,1},{1,0},{2,3},{3,2},{4,5},{5,4},{6,7},{7,6},{8,9},{9,8},{10,11... | collective-permute-start | bytes 12296 | tf_op jit(solution)/shard_map/ppermute | solution.py:419
  53.0 1.1 collective-permute-start
  54.1 4.5 %collective-permute-start.2 = (f32[2,512]{1,0:T(2,128)S(1)}, f32[2,512]{1,0:T(2,128)S(1)}, u32[]{:S(2)}, u32[]{:S(2)}) collective-permute-start(f32[2,512]{1,0:T(2,128)S(1)} %add.33), channel_id=1, source_target_pairs={{0,2},{1,3},{2,0},{3,1},{4,6},{5,7},{6,4},{7,5},{8,10},{9,11},{10,... | collective-permute-start | bytes 12296 | tf_op jit(solution)/shard_map/ppermute | solution.py:426
  59.2 1.3 copy-start
  60.5 1.2 copy-start.1
  61.7 47.5 %collective-permute-start.14 = (bf16[3,768,384]{2,1,0:T(8,128)(2,1)}, bf16[3,768,384]{2,1,0:T(8,128)(2,1)S(1)}, u32[]{:S(2)}, u32[]{:S(2)}) collective-permute-start(bf16[3,768,384]{2,1,0:T(8,128)(2,1)} %get-tuple-element.22), channel_id=1, source_target_pairs={{0,12},{4,8},{8,4},{12,0},{16,28},{20,24},{24,20},{28,16},{1,13},{... | collective-permute-start | bytes 5308424 | tf_op jit(solution)/shard_map/ppermute | solution.py:97
  61.8 48.1 %collective-permute-start.15 = (bf16[3,768,384]{2,1,0:T(8,128)(2,1)}, bf16[3,768,384]{2,1,0:T(8,128)(2,1)S(1)}, u32[]{:S(2)}, u32[]{:S(2)}) collective-permute-start(bf16[3,768,384]{2,1,0:T(8,128)(2,1)} %get-tuple-element.21.refs_6_.refs_8_), channel_id=1, source_target_pairs={{0,16},{4,20},{8,24},{12,28},{16,0},{20,4},{24,8},{28,12},{1,17},{... | collective-permute-start | bytes 5308424 | tf_op jit(solution)/shard_map/ppermute | solution.py:97
  62.3 14.9 %collective-permute-start.5 = (bf16[512,1536]{1,0:T(8,128)(2,1)}, bf16[512,1536]{1,0:T(8,128)(2,1)}, u32[]{:S(2)}, u32[]{:S(2)}) collective-permute-start(bf16[512,1536]{1,0:T(8,128)(2,1)} %get-tuple-element.15.refs_1_.refs_0_), channel_id=1, source_target_pairs={{1,2},{2,3},{5,6},{6,7},{9,10},{10,11},{13,14},{14,15},{17,18},{18... | collective-permute-start | bytes 4718600 | tf_op jit(solution)/shard_map/ppermute | solution.py:407
  64.1 47.6 %collective-permute-start.16 = (bf16[3,768,384]{2,1,0:T(8,128)(2,1)}, bf16[3,768,384]{2,1,0:T(8,128)(2,1)}, u32[]{:S(2)}, u32[]{:S(2)}) collective-permute-start(bf16[3,768,384]{2,1,0:T(8,128)(2,1)} %get-tuple-element.22), channel_id=1, source_target_pairs={{0,4},{4,0},{8,12},{12,8},{16,20},{20,16},{24,28},{28,24},{1,5},{5... | collective-permute-start | bytes 5308424 | tf_op jit(solution)/shard_map/ppermute | solution.py:97
  64.5 40.2 %collective-permute-start.6 = (bf16[512,1536]{1,0:T(8,128)(2,1)}, bf16[512,1536]{1,0:T(8,128)(2,1)}, u32[]{:S(2)}, u32[]{:S(2)}) collective-permute-start(bf16[512,1536]{1,0:T(8,128)(2,1)} %get-tuple-element.16.refs_2_), channel_id=1, source_target_pairs={{1,0},{2,1},{5,4},{6,5},{9,8},{10,9},{13,12},{14,13},{17,16},{18,1... | collective-permute-start | bytes 4718600 | tf_op jit(solution)/shard_map/ppermute | solution.py:410
  77.2 36.0 %collective-permute-start.10 = (bf16[512,1536]{1,0:T(8,128)(2,1)}, bf16[512,1536]{1,0:T(8,128)(2,1)S(1)}, u32[]{:S(2)}, u32[]{:S(2)}) collective-permute-start(bf16[512,1536]{1,0:T(8,128)(2,1)} %get-tuple-element.18.refs_1_), channel_id=1, source_target_pairs={{0,4},{4,0},{8,12},{12,8},{16,20},{20,16},{24,28},{28,24},{1,5},{5... | collective-permute-start | bytes 4718600 | tf_op jit(solution)/shard_map/ppermute | solution.py:97
  104.6 10.2 %collective-permute-start.9 = (bf16[512,1536]{1,0:T(8,128)(2,1)}, bf16[512,1536]{1,0:T(8,128)(2,1)S(1)}, u32[]{:S(2)}, u32[]{:S(2)}) collective-permute-start(bf16[512,1536]{1,0:T(8,128)(2,1)} %get-tuple-element.17.refs_0_), channel_id=1, source_target_pairs={{0,4},{4,0},{8,12},{12,8},{16,20},{20,16},{24,28},{28,24},{1,5},{5... | collective-permute-start | bytes 4718600 | tf_op jit(solution)/shard_map/ppermute | solution.py:97
  109.3 3.9 %copy-start.2 = (bf16[3,768,384]{2,1,0:T(8,128)(2,1)}, bf16[3,768,384]{2,1,0:T(8,128)(2,1)S(1)}, u32[]{:S(2)}) copy-start(bf16[3,768,384]{2,1,0:T(8,128)(2,1)S(1)} %collective-permute-done.14.refs_2_.refs_10_.refs_12_) | copy-start | bytes 5308420
  109.3 6.6 %collective-permute-start.11 = (bf16[512,1536]{1,0:T(8,128)(2,1)}, bf16[512,1536]{1,0:T(8,128)(2,1)S(1)}, u32[]{:S(2)}, u32[]{:S(2)}) collective-permute-start(bf16[512,1536]{1,0:T(8,128)(2,1)} %shard_map.94.refs_2_), channel_id=1, source_target_pairs={{0,4},{4,0},{8,12},{12,8},{16,20},{20,16},{24,28},{28,24},{1,5},{5... | collective-permute-start | bytes 4718600 | tf_op jit(solution)/shard_map/ppermute | solution.py:97
  109.9 3.3 %copy-start.3 = (bf16[3,768,384]{2,1,0:T(8,128)(2,1)}, bf16[3,768,384]{2,1,0:T(8,128)(2,1)S(1)}, u32[]{:S(2)}) copy-start(bf16[3,768,384]{2,1,0:T(8,128)(2,1)S(1)} %collective-permute-done.15.refs_3_.refs_8_.refs_10_) | copy-start | bytes 5308420
  109.9 24.5 %collective-permute-start.7 = (bf16[512,1536]{1,0:T(8,128)(2,1)}, bf16[512,1536]{1,0:T(8,128)(2,1)}, u32[]{:S(2)}, u32[]{:S(2)}) collective-permute-start(bf16[512,1536]{1,0:T(8,128)(2,1)} %collective-permute-done.5.refs_1_.refs_0_), channel_id=1, source_target_pairs={{2,3},{6,7},{10,11},{14,15},{18,19},{22,23},{26,27},{30,31}} | collective-permute-start | bytes 4718600 | tf_op jit(solution)/shard_map/ppermute | solution.py:407
  111.7 38.9 %collective-permute-start.8 = (bf16[512,1536]{1,0:T(8,128)(2,1)}, bf16[512,1536]{1,0:T(8,128)(2,1)}, u32[]{:S(2)}, u32[]{:S(2)}) collective-permute-start(bf16[512,1536]{1,0:T(8,128)(2,1)} %collective-permute-done.6.refs_3_.refs_2_), channel_id=1, source_target_pairs={{1,0},{5,4},{9,8},{13,12},{17,16},{21,20},{25,24},{29,28}} | collective-permute-start | bytes 4718600 | tf_op jit(solution)/shard_map/ppermute | solution.py:410
  113.2 2.7 %copy-start.4 = (bf16[512,1536]{1,0:T(8,128)(2,1)}, bf16[512,1536]{1,0:T(8,128)(2,1)S(1)}, u32[]{:S(2)}) copy-start(bf16[512,1536]{1,0:T(8,128)(2,1)S(1)} %collective-permute-done.10.refs_4_.refs_5_) | copy-start | bytes 4718596
  113.2 58.5 %collective-permute-start.18 = (bf16[3,768,384]{2,1,0:T(8,128)(2,1)}, bf16[3,768,384]{2,1,0:T(8,128)(2,1)S(1)}, u32[]{:S(2)}, u32[]{:S(2)}) collective-permute-start(bf16[3,768,384]{2,1,0:T(8,128)(2,1)} %get-tuple-element.23.refs_7_.refs_9_), channel_id=1, source_target_pairs={{0,16},{4,20},{8,24},{12,28},{16,0},{20,4},{24,8},{28,12},{1,17},{... | collective-permute-start | bytes 5308424 | tf_op jit(solution)/shard_map/ppermute | solution.py:97
  114.8 1.1 copy-start.5
  114.8 56.9 %collective-permute-start.19 = (bf16[3,768,384]{2,1,0:T(8,128)(2,1)}, bf16[3,768,384]{2,1,0:T(8,128)(2,1)S(1)}, u32[]{:S(2)}, u32[]{:S(2)}) collective-permute-start(bf16[3,768,384]{2,1,0:T(8,128)(2,1)} %get-tuple-element.24.refs_11_.refs_13_), channel_id=1, source_target_pairs={{0,8},{4,12},{8,0},{12,4},{16,24},{20,28},{24,16},{28,20},{1,9},{5... | collective-permute-start | bytes 5308424 | tf_op jit(solution)/shard_map/ppermute | solution.py:97
  115.9 1.2 copy-start.6
  155.3 3.7 %collective-permute-start.17 = (bf16[512,1536]{1,0:T(8,128)(2,1)}, bf16[512,1536]{1,0:T(8,128)(2,1)S(1)}, u32[]{:S(2)}, u32[]{:S(2)}) collective-permute-start(bf16[512,1536]{1,0:T(8,128)(2,1)} %shard_map.99.refs_3_), channel_id=1, source_target_pairs={{0,4},{4,0},{8,12},{12,8},{16,20},{20,16},{24,28},{28,24},{1,5},{5... | collective-permute-start | bytes 4718600 | tf_op jit(solution)/shard_map/ppermute | solution.py:97
  158.9 1.2 copy-start.7
  171.7 1.3 copy-start.8
  171.7 1.8 copy-start.9
  192.7 0.9 copy-start.10

commit v2 on v0

--- a/solution.py
+++ b/solution.py
@@ -1,6 +1,10 @@
+import functools
+
 import jax
 import jax.numpy as jnp
 from jax import lax
+from jax.experimental import pallas as pl
+from jax.experimental.pallas import tpu as pltpu
 from jax.sharding import PartitionSpec as P
 
 DH = 128
@@ -25,6 +29,12 @@
 
 def add_rows(normed, piece):
     return jnp.dot(normed, piece, preferred_element_type=jnp.float32)
+
+
+def allowed_pairs(block_mask):
+    blocks = block_mask.shape[-1]
+    allowed = (block_mask > 0) | (jnp.arange(blocks)[:, None] == jnp.arange(blocks)[None, :])[None]
+    return jnp.repeat(jnp.repeat(allowed, BLOCK, axis=1), BLOCK, axis=2)
 
 
 def per_device(tokens, block_mask, norm_gain, w_query, w_key, w_value, query_gain, key_gain):
@@ -44,9 +54,7 @@
     )
     key_n = head_norm(key.reshape(draws_here, TPD, heads_here, DH), key_gain).astype(jnp.bfloat16)
     value = value.astype(jnp.bfloat16).reshape(draws_here, TPD, heads_here, DH)
-    blocks = block_mask.shape[-1]
-    allowed = (block_mask > 0) | (jnp.arange(blocks)[:, None] == jnp.arange(blocks)[None, :])[None]
-    allowed = jnp.repeat(jnp.repeat(allowed, BLOCK, axis=1), BLOCK, axis=2)
+    allowed = allowed_pairs(block_mask)
     scores = jnp.einsum(
         "bqhe,bkhe->bhqk", query_n, key_n, preferred_element_type=jnp.float32
     ) / jnp.sqrt(jnp.float32(DH))
@@ -58,9 +66,470 @@
     return out.astype(jnp.bfloat16).reshape(tokens.shape[0], heads_here * DH)
 
 
+CORE, X, Y = 1, 2, 4
+
+PLACES = ((0, 1, 2, 3), (1, 0, 2, 3), (2, 3, 1, 0), (3, 2, 1, 0))
+
+
+def arrival(z, place):
+    return z - place if place <= z else 3 + place - z
+
+
+def plan(z, chip):
+    diagonal = chip ^ 3
+    order = [place for place in PLACES[z] if place != diagonal] + [diagonal]
+    pairs = [number for place in order for number in (PLACES[z].index(place), place ^ chip)]
+    return pairs + list(PLACES[z]) + [arrival(z, place) for place in PLACES[z]]
+
+
+PLAN = [[plan(z, chip) for chip in range(4)] for z in range(4)]
+PLACE, ARRIVAL, CORE_AT = 8, 12, 16
+
+HBM = pl.BlockSpec(memory_space=pltpu.HBM)
+ANY = pl.BlockSpec(memory_space=pl.ANY)
+VMEM = pl.BlockSpec(memory_space=pltpu.VMEM)
+SMEM = pl.BlockSpec(memory_space=pltpu.SMEM)
+FREE = pl.CostEstimate(flops=0, bytes_accessed=0, transcendentals=0)
+
+
+def params(mib):
+    return pltpu.CompilerParams(vmem_limit_bytes=mib * 2**20)
+
+
+def swap(array, bits):
+    return lax.ppermute(array, "dp", [(i, i ^ bits) for i in range(8)])
+
+
+def trade(array):
+    return lax.all_to_all(array, "dp", 0, 0, axis_index_groups=[[i, i + 1] for i in range(0, 8, 2)])
+
+
+def gate(arrays, others):
+    return pl.pallas_call(
+        lambda *refs: None,
+        in_specs=[ANY] * (len(arrays) + len(others)),
+        out_specs=[ANY] * len(arrays),
+        out_shape=[jax.ShapeDtypeStruct(array.shape, array.dtype) for array in arrays],
+        input_output_aliases={number: number for number in range(len(arrays))},
+        compiler_params=params(1),
+        cost_estimate=FREE,
+    )(*arrays, *others)
+
+
+def columns_of(heads):
+    query = [h * 2 * DH for h in range(heads)]
+    value = [heads * 2 * DH + h * DH for h in range(heads)]
+    return query, [first + DH for first in query], value
+
+
+def column_groups(width):
+    return [(first, min(first + 2 * DH, width)) for first in range(0, width, 2 * DH)]
+
+
+def pack_kernel(*refs):
+    weights, outs, (held, packed, in_sems, out_sems) = refs[:3], refs[3:5], refs[5:]
+    core = lax.axis_index("dp") % 2
+    _, _, _, width = held.shape
+    heads = width // DH
+
+    def load(number, kind):
+        first = pl.multiple_of((core if number == 0 else 1 - core) * width, DH)
+        return pltpu.make_async_copy(
+            weights[kind].at[:, pl.ds(first, width)], held.at[number, kind], in_sems.at[number, kind]
+        )
+
+    def store(number):
+        return pltpu.make_async_copy(packed.at[number], outs[number], out_sems.at[number])
+
+    for number in range(2):
+        for kind in range(3):
+            load(number, kind).start()
+    for number in range(2):
+        for kind, firsts in enumerate(columns_of(heads)):
+            load(number, kind).wait()
+            for h, first in enumerate(firsts):
+                packed[number, :, first : first + DH] = held[number, kind, :, h * DH : (h + 1) * DH]
+        store(number).start()
+    for number in range(2):
+        store(number).wait()
+
+
+def pack(*weights):
+    rows, columns = weights[0].shape
+    shape = (rows, 3 * columns // 2)
+    return pl.pallas_call(
+        pack_kernel,
+        in_specs=[HBM] * 3,
+        out_specs=[HBM] * 2,
+        out_shape=[jax.ShapeDtypeStruct(shape, jnp.bfloat16)] * 2,
+        scratch_shapes=[
+            pltpu.VMEM((2, 3, rows, columns // 2), jnp.bfloat16),
+            pltpu.VMEM((2, *shape), jnp.bfloat16),
+            pltpu.SemaphoreType.DMA((2, 3)),
+            pltpu.SemaphoreType.DMA((2,)),
+        ],
+        compiler_params=params(56),
+        cost_estimate=FREE,
+    )(*weights)
+
+
+def fetch(chosen, choices, target, sem):
+    for number, choice in choices.items():
+
+        @pl.when(chosen == number)
+        def _():
+            pltpu.make_async_copy(choice, target, sem).start()
+
+
+def norm_kernel(slots, numbers, plan_ref, mean_ref, scale_ref, gains_ref, *refs):
+    arrays = dict(zip(numbers, refs))
+    out_ref, raw, normed, in_sems, out_sems = refs[-5:]
+    rows = raw.shape[1]
+    step = 64
+
+    for n, slot in enumerate(slots):
+        fetch(plan_ref[ARRIVAL + slot], arrays, raw.at[n], in_sems.at[n])
+    for n, slot in enumerate(slots):
+        gain = gains_ref[pl.ds(plan_ref[PLACE + slot], 1), :]
+        pltpu.make_async_copy(refs[0], raw.at[n], in_sems.at[n]).wait()
+
+        @pl.loop(0, rows // step)
+        def _(tile):
+            at = pl.ds(pl.multiple_of(tile * step, step), step)
+            values = raw[n, at, :].astype(jnp.float32)
+            normed[n, at, :] = ((values - mean_ref[at, :]) * scale_ref[at, :] * gain).astype(jnp.bfloat16)
+
+        for copy in range(out_ref.shape[0]):
+            pltpu.make_async_copy(normed.at[n], out_ref.at[copy, n], out_sems.at[copy, n]).start()
+    for n in range(len(slots)):
+        for copy in range(out_ref.shape[0]):
+            pltpu.make_async_copy(normed.at[n], out_ref.at[copy, n], out_sems.at[copy, n]).wait()
+
+
+def norm(plan_here, slots, copies, mean, scale, gains, arrays, *others):
+    rows, features = next(iter(arrays.values())).shape
+    shape = (len(slots), rows, features)
+    return pl.pallas_call(
+        functools.partial(norm_kernel, slots, tuple(arrays)),
+        in_specs=[SMEM] + [VMEM] * 3 + [ANY] * len(arrays) + [ANY] * len(others),
+        out_specs=HBM,
+        out_shape=jax.ShapeDtypeStruct((copies, *shape), jnp.bfloat16),
+        scratch_shapes=[
+            pltpu.VMEM(shape, jnp.bfloat16),
+            pltpu.VMEM(shape, jnp.bfloat16),
+            pltpu.SemaphoreType.DMA((len(slots),)),
+            pltpu.SemaphoreType.DMA((copies, len(slots))),
+        ],
+        compiler_params=params(16),
+        cost_estimate=FREE,
+    )(plan_here, mean, scale, gains, *arrays.values(), *others)
+
+
+class Tokens:
+    def __init__(self, arrays):
+        self.arrays = arrays
+        _, _, self.rows, self.features = self.arrays[0].shape
+        self.tiles_here = self.rows // TPD
+        self.count = 2 * self.tiles_here
+
+    def tiles(self, core, refs):
+        found = [{} for _ in range(self.count)]
+        slot = 0
+        for ref, array in zip(refs, self.arrays):
+            for n in range(array.shape[1]):
+                for tile, choices in enumerate(found):
+                    whose = core if tile < self.tiles_here else 1 - core
+                    choices[slot] = ref.at[whose, n, pl.ds(tile % self.tiles_here * TPD, TPD)]
+                slot += 1
+        return found, refs[len(self.arrays) :]
+
+
+def weight_copies(core, pair, columns, target, sems):
+    copies = []
+    for part, source in enumerate(pair):
+        depth = source.shape[0]
+        first = pl.multiple_of((core if part == 0 else 1 - core) * depth, depth)
+        at = pl.ds(columns[0], columns[1] - columns[0])
+        copies.append(
+            pltpu.make_async_copy(source.at[:, at], target.at[pl.ds(first, depth), at], sems.at[part])
+        )
+    return copies
+
+
+def weight_group(core, chosen, choices, columns, target, sems):
+    def start():
+        for number, pair in choices.items():
+
+            @pl.when(chosen == number)
+            def _():
+                for copy in weight_copies(core, pair, columns, target, sems):
+                    copy.start()
+
+    def wait():
+        for copy in weight_copies(core, choices[0], columns, target, sems):
+            copy.wait()
+
+    return [(start, wait)]
+
+
+def token_group(chosen, views, target, sem):
+    return [(functools.partial(fetch, chosen, views, target, sem), pltpu.make_async_copy(views[0], target, sem).wait)]
+
+
+def run(groups, steps, ahead):
+    started = waited = 0
+    for need, step in steps:
+        while started < min(need + 1 + ahead, len(groups)):
+            for start, _ in groups[started]:
+                start()
+            started += 1
+        while waited <= need:
+            for _, wait in groups[waited]:
+                wait()
+            waited += 1
+        step()
+
+
+def project_kernel(tokens_of, plan_ref, *refs):
+    core = plan_ref[CORE_AT]
+    tiles, refs = tokens_of.tiles(core, refs)
+    choices = {0: (refs[0].at[core], refs[0].at[1 - core]), 1: (refs[1], refs[2]), 2: (refs[3], refs[4])}
+    total, next_tokens, next_weights, tokens, weights, token_sems, weight_sems, next_sems = refs[5:]
+    count, _, width = weights.shape
+    cuts = [0, 2 * DH, 4 * DH, 6 * DH, width]
+
+    def add(n, first, last, tile):
+        update = jnp.dot(tokens[n, tile], weights[n, :, first:last], preferred_element_type=jnp.float32)
+        if n > 0:
+            update = update + total[tile, :, first:last]
+        total[tile, :, first:last] = update
+
+    groups, steps = [], []
+    for n in range(count):
+        slot, bits = plan_ref[2 * n], plan_ref[2 * n + 1]
+        for piece, columns in enumerate(zip(cuts, cuts[1:])):
+            group = weight_group(core, bits, choices, columns, weights.at[n], weight_sems.at[n, piece])
+            if piece > 0:
+                groups.append(group)
+            for tile, views in enumerate(tiles):
+                if piece == 0:
+                    tile_group = token_group(slot, views, tokens.at[n, tile], token_sems.at[n, tile])
+                    groups.append(group + tile_group if tile == 0 else tile_group)
+                for first, last in column_groups(width):
+                    if columns[0] <= first < columns[1]:
+                        steps.append((len(groups) - 1, functools.partial(add, n, first, last, tile)))
+    slot = jnp.where(plan_ref[4] == 3, plan_ref[6], plan_ref[4])
+    for tile, views in enumerate(tiles):
+        groups.append(token_group(slot, views, next_tokens.at[tile], token_sems.at[count, tile]))
+    groups.append(weight_group(core, plan_ref[5], choices, (0, width), next_weights, next_sems))
+    steps.append((len(groups) - 1, lambda: None))
+    run(groups, steps, 5)
+
+
+def project(plan_here, arrays, near):
+    tokens = Tokens(arrays)
+    depth, width = near[1].shape
+    count = 2
+    shape = (tokens.count, TPD, tokens.features)
+    return pl.pallas_call(
+        functools.partial(project_kernel, tokens),
+        in_specs=[SMEM] + [HBM] * (len(arrays) + len(near)),
+        out_specs=[VMEM] * 3,
+        out_shape=[
+            jax.ShapeDtypeStruct((tokens.count, TPD, width), jnp.float32),
+            jax.ShapeDtypeStruct(shape, jnp.bfloat16),
+            jax.ShapeDtypeStruct((tokens.features, width), jnp.bfloat16),
+        ],
+        scratch_shapes=[
+            pltpu.VMEM((count, *shape), jnp.bfloat16),
+            pltpu.VMEM((count, tokens.features, width), jnp.bfloat16),
+            pltpu.SemaphoreType.DMA((count + 1, tokens.count)),
+            pltpu.SemaphoreType.DMA((count, 4, 2)),
+            pltpu.SemaphoreType.DMA((2,)),
+        ],
+        compiler_params=params(18),
+        cost_estimate=FREE,
+    )(plan_here, *arrays, *near)
+
+
+def attend(query, key, value, mask_ref, draw):
+    scores = lax.dot_general(
+        query, key, (((1,), (1,)), ((), ())), preferred_element_type=jnp.float32
+    )
+    weights = jnp.exp(scores * (DH**-0.5))
+    blocks = TPD // BLOCK
+    column = lax.broadcasted_iota(jnp.int32, (1, TPD), 1) // BLOCK
+    bands = []
+    for i in range(blocks):
+        allowed = column == i
+        for j in range(blocks):
+            allowed = allowed | ((column == j) & (mask_ref[(draw * blocks + i) * blocks + j] > 0))
+        bands.append(jnp.where(allowed, weights[i * BLOCK : (i + 1) * BLOCK], 0.0))
+    weights = jnp.concatenate(bands, axis=0).astype(jnp.bfloat16)
+    both = jnp.dot(
+        weights,
+        jnp.concatenate([value, jnp.ones_like(value)], axis=1),
+        preferred_element_type=jnp.float32,
+    )
+    return (both[:, :DH] / both[:, DH:]).astype(jnp.bfloat16)
+
+
+def finish_kernel(
+    plan_ref,
+    mask_ref,
+    total_ref,
+    next_tokens,
+    next_weights,
+    last_here,
+    last_there,
+    diag_same,
+    diag_cross,
+    query_gain,
+    key_gain,
+    out_ref,
+    near_tokens,
+    diag_tokens,
+):
+    core = plan_ref[CORE_AT]
+    tiles, _, width = total_ref.shape
+    heads = width // (3 * DH)
+    half = tiles // 2
+    depth = diag_same.shape[0]
+
+    def place(tile, near, diag):
+        near_tokens[tile] = near(slice(None))
+        for part in range(2):
+            first = pl.multiple_of((core if part == 0 else 1 - core) * depth, depth)
+            diag_tokens[part, tile] = diag(pl.ds(first, depth))
+
+    for tile in range(tiles):
+        at = pl.ds(tile % half * TPD, TPD)
+
+        def last(features, at=at, ref=last_here if tile < half else last_there):
+            return ref[0, 0, at, features]
+
+        def early(features, tile=tile):
+            return next_tokens[tile, :, features]
+
+        @pl.when(plan_ref[4] == 3)
+        def _():
+            place(tile, last, early)
+
+        @pl.when(plan_ref[4] != 3)
+        def _():
+            place(tile, early, last)
+
+    query_first, key_first, value_first = columns_of(heads)
+    for tile in range(tiles):
+        sums = []
+        for first, end in column_groups(width):
+            part = total_ref[tile, :, first:end]
+            for tokens, weights in (
+                (near_tokens[tile], next_weights),
+                (diag_tokens[0, tile], diag_same),
+                (diag_tokens[1, tile], diag_cross),
+            ):
+                part = part + jnp.dot(tokens, weights[:, first:end], preferred_element_type=jnp.float32)
+            sums += [part[:, at : at + DH] for at in range(0, end - first, DH)]
+        whose = core if tile < half else 1 - core
+        for h in range(heads):
+            query = head_norm(sums[query_first[h] // DH], query_gain[...]).astype(jnp.bfloat16)
+            key = head_norm(sums[key_first[h] // DH], key_gain[...]).astype(jnp.bfloat16)
+            value = sums[value_first[h] // DH].astype(jnp.bfloat16)
+            out_ref[whose, h, pl.ds(tile % half * TPD, TPD), :] = attend(
+                query, key, value, mask_ref, whose * half + tile % half
+            )
+
+
+def finish(plan_here, mask, total, next_tokens, next_weights, last, diag, query_gain, key_gain):
+    tiles, _, width = total.shape
+    depth = diag[0].shape[0]
+    heads = width // (3 * DH)
+    return pl.pallas_call(
+        finish_kernel,
+        in_specs=[SMEM] * 2 + [VMEM] * 9,
+        out_specs=VMEM,
+        out_shape=jax.ShapeDtypeStruct((2, heads, tiles // 2 * TPD, DH), jnp.bfloat16),
+        scratch_shapes=[
+            pltpu.VMEM((tiles, TPD, 2 * depth), jnp.bfloat16),
+            pltpu.VMEM((2, tiles, TPD, depth), jnp.bfloat16),
+        ],
+        compiler_params=params(18),
+        cost_estimate=FREE,
+    )(plan_here, mask, total, next_tokens, next_weights, *last, *diag, query_gain, key_gain)
+
+
+def per_device_8x4(tokens, block_mask, norm_gain, w_query, w_key, w_value, query_gain, key_gain):
+    features = tokens.shape[1]
+    heads = w_query.shape[1] // (2 * DH)
+    dp, z = lax.axis_index("dp"), lax.axis_index("tensor")
+    core = (dp % 2).astype(jnp.int32)
+    plan_here = jnp.asarray(PLAN, jnp.int32)[z, dp // 2]
+    plan_here = jnp.concatenate([plan_here, core[None]])
+
+    def up(array, first):
+        return lax.ppermute(array, "tensor", [(i, i + 1) for i in range(first, 3)])
+
+    def down(array, last):
+        return lax.ppermute(array, "tensor", [(i + 1, i) for i in range(last)])
+
+    mine, other = pack(w_query, w_key, w_value)
+    values = tokens.astype(jnp.float32)
+    stats = jnp.stack([jnp.sum(values, axis=1), jnp.sum(values * values, axis=1)])
+    stats = stats + lax.ppermute(stats, "tensor", [(i, i ^ 1) for i in range(4)])
+
+    x_same, y_cross = swap(mine, X), swap(other, Y | CORE)
+    (sent,) = gate((tokens,), (stats, mine))
+    up1, down1 = up(sent, 0), down(sent, 3)
+    own = trade(jnp.where(core == 0, jnp.stack([mine, other]), jnp.stack([other, mine])))
+    mask = block_mask.astype(jnp.float32).reshape(1, -1)
+    mask = trade(jnp.concatenate([mask, mask])).reshape(-1)
+    (stats,) = gate((stats,), (own, mask))
+    stats = stats + lax.ppermute(stats, "tensor", [(i, i ^ 2) for i in range(4)])
+
+    mine, other, up1, down1 = gate((mine, other, up1, down1), (x_same, y_cross, stats))
+    x_cross, y_same = swap(other, X | CORE), swap(mine, Y)
+    up2, down2 = up(up1, 1), down(down1, 2)
+
+    means = stats / (4 * features)
+    mean = means[0][:, None]
+    scale = lax.rsqrt(means[1] - means[0] * means[0] + EPS)[:, None]
+    gains = norm_gain.reshape(4, features)
+    arrived = {0: tokens, 1: up1, 4: down1}
+    normed = [trade(norm(plan_here, (0, 1), 2, mean, scale, gains, arrived))]
+
+    x_same, y_cross, up2, down2 = gate(
+        (x_same, y_cross, up2, down2), (x_cross, y_same, normed[0])
+    )
+    diag_same, diag_cross = swap(x_same, Y), swap(y_cross, X)
+    up3, down3 = up(up2, 2), down(down2, 1)
+    arrived = {1: up1, 2: up2, 4: down1, 5: down2}
+    normed.append(trade(norm(plan_here, (2,), 2, mean, scale, gains, arrived)))
+    near = [own, x_same, x_cross, y_same, y_cross]
+    total, next_tokens, next_weights = project(plan_here, normed, near)
+
+    arrived = {2: up2, 3: up3, 5: down2, 6: down3}
+    last = norm(plan_here, (3,), 1, mean, scale, gains, arrived, total)
+    last = (last, swap(last, CORE))
+    out = finish(
+        plan_here,
+        mask,
+        total,
+        next_tokens,
+        next_weights,
+        last,
+        (diag_same, diag_cross),
+        query_gain[None, :],
+        key_gain[None, :],
+    )
+    out = trade(out)
+    return jnp.concatenate([out[i // heads, i % heads] for i in range(2 * heads)], axis=1)
+
+
 def solution(mesh):
+    eight_by_four = dict(mesh.shape) == {"dp": 8, "tensor": 4}
     return jax.shard_map(
-        per_device,
+        per_device_8x4 if eight_by_four else per_device,
         mesh=mesh,
         in_specs=(
             P("dp", "tensor"),

time: 333 us -> 159 us (0.48)
  waiting for transfers between devices: 262 us -> 49.1 us
  Pallas kernels: 0 us -> 36.2 us
  matrix products: 34.5 us -> 0 us
  starting transfers between devices: 0.12 us -> 31 us
  blocking collectives: 0 us -> 19.4 us
  between operations: 13.3 us -> 0.3 us
  other arithmetic: 15.2 us -> 9.32 us
  local copies, waits for them, and re-layouts: 8.22 us -> 12.5 us
    all_gather x4 -> x0, waiting for transfers between devices: 259 us -> none  [the longest x1 117 us: per_device(): whole = lax.all_gather(tokens, 'tensor', axis=1, tiled=True)]
    ppermute x0 -> x15, waiting for transfers between devices: none -> 46.5 us  [the longest x3 28.9 us: down(): return lax.ppermute(array, 'tensor', [(i + 1, i) for i in range(last)])]
    pallas_call x0 -> x10, Pallas kernels: none -> 36.2 us  [the longest x1 13.7 us: project(): pl.pallas_call(functools.partial(project_kernel, tokens), in_specs=[SMEM]...]
    dot_general x5 -> x0, matrix products: 34.5 us -> none  [the longest x3 33.4 us: add_rows(): return jnp.dot(normed, piece, preferred_element_type=jnp.float32)]
    ppermute x0 -> x15, starting transfers between devices: none -> 23.8 us  [the longest x3 8.26 us: up(): return lax.ppermute(array, 'tensor', [(i, i + 1) for i in range(first, 3)])]
    all_to_all x0 -> x3, blocking collectives: none -> 19.4 us  [trade(): lax.all_to_all(array, 'dp', 0, 0, axis_index_groups=[[i, i + 1] for i in...]
    convert_element_type x2 -> x1, other arithmetic: 7.83 us -> 0.01 us  [per_device_8x4(): mask = block_mask.astype(jnp.float32).reshape(1, -1)]
    all_to_all x0 -> x2, starting transfers between devices: none -> 7.21 us  [trade(): lax.all_to_all(array, 'dp', 0, 0, axis_index_groups=[[i, i + 1] for i in...]
  transfers between devices with their start and end apart: 4 -> 17, of which waited for: 4 -> 7; matrix products, arithmetic and copies ran while one was open for 12% -> 10% of each run, Pallas kernels for 0% -> 16%
where the time goes in v2:
time: 159 us; the launch traced here: 158 us
  waiting for transfers between devices  49.1 us (31%)
  Pallas kernels  36.2 us (23%)
  starting transfers between devices  31 us (19%)
  blocking collectives  19.4 us (12%)
  local copies, waits for them, and re-layouts  12.5 us (8%)
  other arithmetic  9.32 us (6%)
    ppermute x3, waiting for transfers between devices, down(): return lax.ppermute(array, 'tensor', [(i + 1, i) for i in range(last)])  28.9 us
    all_to_all x3, blocking collectives, trade(): lax.all_to_all(array, 'dp', 0, 0, axis_index_groups=[[i, i + 1] for i in...  19.4 us
    ppermute x1, waiting for transfers between devices, per_device_8x4(): lax.ppermute(stats, 'tensor', [(i, i ^ 2) for i in range(4)])  14.1 us
    pallas_call x1, Pallas kernels, project(): pl.pallas_call(functools.partial(project_kernel, tokens), in_specs=[SMEM]...  13.7 us
    pallas_call x1, Pallas kernels, finish(): pl.pallas_call(finish_kernel, in_specs=[SMEM] * 2 + [VMEM] * 9, out_specs...  10.7 us
    pallas_call x3, Pallas kernels, norm(): pl.pallas_call(functools.partial(norm_kernel, slots, tuple(arrays)), in_s...  8.37 us
    ppermute x3, starting transfers between devices, up(): return lax.ppermute(array, 'tensor', [(i, i + 1) for i in range(first, 3)])  8.26 us
    all_to_all x2, starting transfers between devices, trade(): lax.all_to_all(array, 'dp', 0, 0, axis_index_groups=[[i, i + 1] for i in...  7.21 us
  transfers between devices with their start and end apart: 17, of which 7 were waited for; matrix products, arithmetic and copies ran while one was open for 10% of the time, Pallas kernels for 16%

profile of v2, /device:TPU:0, one launch (start us, length us, event | category | flops | bytes accessed | tf_op | source)
XLA Modules:
  0.0 157.9 jit_solution(3360365312534661071)
XLA Ops:
  0.0 2.0 %convert_reduce_fusion = (f32[512]{0:T(512)S(1)}, f32[512]{0:T(512)S(1)}) fusion(bf16[512,1536]{1,0:T(8,128)(2,1)} %refs_0_.4), kind=kLoop, calls=%fused_computation.1 | loop fusion | flops 3144704 | bytes 1576960 | tf_op jit(solution)/shard_map/reduce_sum | solution.py:478
  2.0 3.1 %collective-permute-start = (f32[2,512]{1,0:T(2,128)S(1)}, f32[2,512]{1,0:T(2,128)S(1)}, u32[]{:S(2)}, u32[]{:S(2)}) collective-permute-start(f32[2,512]{1,0:T(2,128)S(1)} %pad_maximum_fusion), channel_id=1, source_target_pairs={{0,1},{1,0},{2,3},{3,2},{4,5},{5,4},{6,7},{7,6},{8,9},{9,8},{10,11... | collective-permute-start | bytes 12296 | tf_op jit(solution)/shard_map/ppermute | solution.py:479
  5.1 3.4 %shard_map.91 = (bf16[768,1152]{1,0:T(8,128)(2,1)}, bf16[768,1152]{1,0:T(8,128)(2,1)}) custom-call(bf16[768,768]{1,0:T(8,128)(2,1)} %refs_0_.3, bf16[768,768]{1,0:T(8,128)(2,1)} %refs_1_.1, bf16[768,768]{1,0:T(8,128)(2,1)} %refs_2_.1), custom_call_target="tpu_custom_call" | custom-call | tf_op jit(solution)/shard_map/pallas_call | solution.py:160
  9.3 1.5 collective-permute-start.4
  11.9 1.3 collective-permute-start.3
  13.2 5.7 %collective-permute-start.2 = (bf16[512,1536]{1,0:T(8,128)(2,1)}, bf16[512,1536]{1,0:T(8,128)(2,1)}, u32[]{:S(2)}, u32[]{:S(2)}) collective-permute-start(bf16[512,1536]{1,0:T(8,128)(2,1)} %shard_map.93), channel_id=1, source_target_pairs={{0,1},{1,2},{2,3},{4,5},{5,6},{6,7},{8,9},{9,10},{10,11},{12,13},{... | collective-permute-start | bytes 4718600 | tf_op jit(solution)/shard_map/ppermute | solution.py:471
  19.6 3.2 %all-to-all-start = ((f32[2,1,32]{2,1,0:T(1,128)}), f32[2,1,32]{2,1,0:T(1,128)S(1)}, u32[]{:S(2)}, u32[]{:S(2)}) async-start(f32[2,1,32]{2,1,0:T(1,128)} %bitcast.3), calls=%async_computation | async-start | bytes 2048 | tf_op jit(solution)/shard_map/all_to_all | solution.py:104
  22.8 4.9 %maximum_select_fusion = bf16[2,768,1152]{2,1,0:T(8,128)(2,1)} fusion(bf16[1,768,1152]{2,1,0:T(8,128)(2,1)} %bitcast.7, bf16[1,768,1152]{2,1,0:T(8,128)(2,1)} %bitcast.6, pred[]{:T(512)S(6)} %eq.5), kind=kLoop, calls=%fused_computation.2 | loop fusion | flops 5308416 | bytes 7077889 | tf_op jit(solution)/shard_map/jit(_where)/select_n | solution.py:484
  27.7 4.0 %all-to-all-start.1 = ((bf16[2,768,1152]{2,1,0:T(8,128)(2,1)}), bf16[2,768,1152]{2,1,0:T(8,128)(2,1)S(1)}, u32[]{:S(2)}, u32[]{:S(2)}) async-start(bf16[2,768,1152]{2,1,0:T(8,128)(2,1)} %maximum_select_fusion), calls=%async_computation.1 | async-start | bytes 7077888 | tf_op jit(solution)/shard_map/all_to_all | solution.py:104
  33.0 2.6 %all-to-all-done.1.refs_1_.refs_2_ = bf16[2,768,1152]{2,1,0:T(8,128)(2,1)S(1)} async-done(((bf16[2,768,1152]{2,1,0:T(8,128)(2,1)}), bf16[2,768,1152]{2,1,0:T(8,128)(2,1)S(1)}, u32[]{:S(2)}, u32[]{:S(2)}) %all-to-all-start.1) | async-done | bytes 3538976 | tf_op jit(solution)/shard_map/all_to_all | solution.py:104
  35.6 2.6 %collective-permute-start.1 = (f32[2,512]{1,0:T(2,128)S(1)}, f32[2,512]{1,0:T(2,128)S(1)}, u32[]{:S(2)}, u32[]{:S(2)}) collective-permute-start(f32[2,512]{1,0:T(2,128)S(1)} %shard_map.92), channel_id=1, source_target_pairs={{0,2},{1,3},{2,0},{3,1},{4,6},{5,7},{6,4},{7,5},{8,10},{9,11},{10,... | collective-permute-start | bytes 12296 | tf_op jit(solution)/shard_map/ppermute | solution.py:488
  38.2 14.1 %collective-permute-done.1 = f32[2,512]{1,0:T(2,128)S(1)} collective-permute-done((f32[2,512]{1,0:T(2,128)S(1)}, f32[2,512]{1,0:T(2,128)S(1)}, u32[]{:S(2)}, u32[]{:S(2)}) %collective-permute-start.1) | collective-permute-done | bytes 4128 | tf_op jit(solution)/shard_map/ppermute | solution.py:488
  53.0 1.8 %collective-permute-start.6 = (bf16[512,1536]{1,0:T(8,128)(2,1)}, bf16[512,1536]{1,0:T(8,128)(2,1)}, u32[]{:S(2)}, u32[]{:S(2)}) collective-permute-start(bf16[512,1536]{1,0:T(8,128)(2,1)} %get-tuple-element.20.refs_1_.refs_0_), channel_id=1, source_target_pairs={{1,2},{2,3},{5,6},{6,7},{9,10},{10,11},{13,14},{14,15},{17,18},{18... | collective-permute-start | bytes 4718600 | tf_op jit(solution)/shard_map/ppermute | solution.py:471
  54.8 1.3 collective-permute-start.7
  56.1 1.4 reshape.40.gains_ref
  60.6 1.5 copy.36.mean_ref
  63.2 1.4 copy-done.1
  66.3 3.4 %shard_map.95 = bf16[2,2,512,1536]{3,2,1,0:T(8,128)(2,1)S(1)} custom-call(s32[17]{0:T(128)S(1)} %pad_add_fusion.plan_ref, f32[512,1]{1,0:T(8,128)S(1)} %copy-done.2, f32[512,1]{1,0:T(8,128)S(1)} %add_rsqrt_fusion.scale_ref, f32[4,1536]{1,0:T(4,128)S(1)} %copy-done.3, bf16[512,1536]{1,0:T(8,128)(2,1)S(1)} %copy-done.1, ...), custom_call_target="tpu_custom_call" | custom-call | tf_op jit(solution)/shard_map/pallas_call | solution.py:212
  69.6 8.8 %all_to_all.29.refs_6_.refs_0_ = bf16[2,2,512,1536]{3,2,1,0:T(8,128)(2,1)S(1)} all-to-all(bf16[2,2,512,1536]{3,2,1,0:T(8,128)(2,1)S(1)} %shard_map.95), channel_id=1, replica_groups={{0,4},{8,12},{16,20},{24,28},{1,5},{9,13},{17,21},{25,29},{2,6},{10,14}..., dimensions={0} | all-to-all | bytes 12582912 | tf_op jit(solution)/shard_map/all_to_all | solution.py:104
  78.4 18.6 %collective-permute-done.7.refs_3_ = bf16[512,1536]{1,0:T(8,128)(2,1)} collective-permute-done((bf16[512,1536]{1,0:T(8,128)(2,1)}, bf16[512,1536]{1,0:T(8,128)(2,1)}, u32[]{:S(2)}, u32[]{:S(2)}) %collective-permute-start.7) | collective-permute-done | bytes 1572896 | tf_op jit(solution)/shard_map/ppermute | solution.py:474
  97.8 1.3 collective-permute-start.11
  99.1 1.6 %collective-permute-start.13 = (bf16[768,1152]{1,0:T(8,128)(2,1)}, bf16[768,1152]{1,0:T(8,128)(2,1)S(1)}, u32[]{:S(2)}, u32[]{:S(2)}) collective-permute-start(bf16[768,1152]{1,0:T(8,128)(2,1)} %get-tuple-element.26.refs_3_), channel_id=1, source_target_pairs={{0,16},{4,20},{8,24},{12,28},{16,0},{20,4},{24,8},{28,12},{1,17},{... | collective-permute-start | bytes 5308424 | tf_op jit(solution)/shard_map/ppermute | solution.py:100
  100.8 1.5 collective-permute-start.14
  102.3 3.2 %shard_map.97 = bf16[2,1,512,1536]{3,2,1,0:T(8,128)(2,1)S(1)} custom-call(s32[17]{0:T(128)S(1)} %pad_add_fusion.plan_ref, f32[512,1]{1,0:T(8,128)S(1)} %copy-done.2, f32[512,1]{1,0:T(8,128)S(1)} %add_rsqrt_fusion.scale_ref, f32[4,1536]{1,0:T(4,128)S(1)} %copy-done.3, bf16[512,1536]{1,0:T(8,128)(2,1)} %get-tuple-element.20.refs_1_.refs_0_, ...), custom_call_target="tpu_custom_call" | custom-call | tf_op jit(solution)/shard_map/pallas_call | solution.py:212
  105.5 6.3 %all_to_all.30.refs_1_ = bf16[2,1,512,1536]{3,2,1,0:T(8,128)(2,1)S(1)} all-to-all(bf16[2,1,512,1536]{3,2,1,0:T(8,128)(2,1)S(1)} %shard_map.97), channel_id=1, replica_groups={{0,4},{8,12},{16,20},{24,28},{1,5},{9,13},{17,21},{25,29},{2,6},{10,14}..., dimensions={0} | all-to-all | bytes 6291456 | tf_op jit(solution)/shard_map/all_to_all | solution.py:104
  111.7 13.7 %shard_map.98 = (f32[4,256,1152]{2,1,0:T(8,128)S(1)}, bf16[4,256,1536]{2,1,0:T(8,128)(2,1)S(1)}, bf16[1536,1152]{1,0:T(8,128)(2,1)S(1)}) custom-call(s32[17]{0:T(128)S(1)} %pad_add_fusion.plan_ref, bf16[2,2,512,1536]{3,2,1,0:T(8,128)(2,1)S(1)} %all_to_all.29.refs_6_.refs_0_, bf16[2,1,512,1536]{3,2,1,0:T(8,128)(2,1)S(1)} %all_to_all.30.refs_1_, ...), custom_call_target="tpu_custom_call" | custom-call | tf_op jit(solution)/shard_map/pallas_call | solution.py:334
  125.4 10.3 %collective-permute-done.11.refs_3_ = bf16[512,1536]{1,0:T(8,128)(2,1)S(1)} collective-permute-done((bf16[512,1536]{1,0:T(8,128)(2,1)}, bf16[512,1536]{1,0:T(8,128)(2,1)S(1)}, u32[]{:S(2)}, u32[]{:S(2)}) %collective-permute-start.11) | collective-permute-done | bytes 1572896 | tf_op jit(solution)/shard_map/ppermute | solution.py:474
  135.7 1.8 %shard_map.99.last_here = bf16[1,1,512,1536]{3,2,1,0:T(8,128)(2,1)S(1)} custom-call(s32[17]{0:T(128)S(1)} %pad_add_fusion.plan_ref, f32[512,1]{1,0:T(8,128)S(1)} %copy-done.2, f32[512,1]{1,0:T(8,128)S(1)} %add_rsqrt_fusion.scale_ref, f32[4,1536]{1,0:T(4,128)S(1)} %copy-done.3, bf16[512,1536]{1,0:T(8,128)(2,1)} %get-tuple-element.24.refs_1_.refs_0_, ...), custom_call_target="tpu_custom_call" | custom-call | tf_op jit(solution)/shard_map/pallas_call | solution.py:212
  137.6 1.8 %collective-permute-done.13.diag_same = bf16[768,1152]{1,0:T(8,128)(2,1)S(1)} collective-permute-done((bf16[768,1152]{1,0:T(8,128)(2,1)}, bf16[768,1152]{1,0:T(8,128)(2,1)S(1)}, u32[]{:S(2)}, u32[]{:S(2)}) %collective-permute-start.13) | collective-permute-done | bytes 1769504 | tf_op jit(solution)/shard_map/ppermute | solution.py:100
  139.4 1.4 collective-permute-done.14.diag_cross
  141.0 10.7 %shard_map.100 = bf16[2,3,512,128]{3,2,1,0:T(8,128)(2,1)S(1)} custom-call(s32[17]{0:T(128)S(1)} %pad_add_fusion.plan_ref, f32[64]{0:T(128)S(1)} %reshape.39.refs_2_.mask_ref, f32[4,256,1152]{2,1,0:T(8,128)S(1)} %get-tuple-element.28.refs_4_.total_ref, bf16[4,256,1536]{2,1,0:T(8,128)(2,1)S(1)} %get-tuple-element.29.next_tokens, ...), custom_call_target="tpu_custom_call" | custom-call | tf_op jit(solution)/shard_map/pallas_call | solution.py:448
  151.8 4.4 %all_to_all.31 = bf16[2,3,512,128]{3,2,1,0:T(8,128)(2,1)S(1)} all-to-all(bf16[2,3,512,128]{3,2,1,0:T(8,128)(2,1)S(1)} %shard_map.100), channel_id=1, replica_groups={{0,4},{8,12},{16,20},{24,28},{1,5},{9,13},{17,21},{25,29},{2,6},{10,14}..., dimensions={0} | all-to-all | bytes 1572864 | tf_op jit(solution)/shard_map/all_to_all | solution.py:104
  (58 shorter events, 13.1 us)
Async XLA Ops:
  2.0 8.7 %copy-start = (bf16[512,1536]{1,0:T(8,128)(2,1)S(1)}, bf16[512,1536]{1,0:T(8,128)(2,1)}, u32[]{:S(2)}) copy-start(bf16[512,1536]{1,0:T(8,128)(2,1)} %refs_0_.4) | copy-start | bytes 4718596
  2.0 9.9 %collective-permute-start = (f32[2,512]{1,0:T(2,128)S(1)}, f32[2,512]{1,0:T(2,128)S(1)}, u32[]{:S(2)}, u32[]{:S(2)}) collective-permute-start(f32[2,512]{1,0:T(2,128)S(1)} %pad_maximum_fusion), channel_id=1, source_target_pairs={{0,1},{1,0},{2,3},{3,2},{4,5},{5,4},{6,7},{7,6},{8,9},{9,8},{10,11... | collective-permute-start | bytes 12296 | tf_op jit(solution)/shard_map/ppermute | solution.py:479
  8.5 43.9 %collective-permute-start.5 = (bf16[768,1152]{1,0:T(8,128)(2,1)}, bf16[768,1152]{1,0:T(8,128)(2,1)}, u32[]{:S(2)}, u32[]{:S(2)}) collective-permute-start(bf16[768,1152]{1,0:T(8,128)(2,1)} %get-tuple-element.19.refs_1_), channel_id=1, source_target_pairs={{0,20},{4,16},{8,28},{12,24},{16,4},{20,0},{24,12},{28,8},{1,21},{... | collective-permute-start | bytes 5308424 | tf_op jit(solution)/shard_map/ppermute | solution.py:100
  9.3 43.2 %collective-permute-start.4 = (bf16[768,1152]{1,0:T(8,128)(2,1)}, bf16[768,1152]{1,0:T(8,128)(2,1)}, u32[]{:S(2)}, u32[]{:S(2)}) collective-permute-start(bf16[768,1152]{1,0:T(8,128)(2,1)} %get-tuple-element.18.refs_2_.refs_0_), channel_id=1, source_target_pairs={{0,8},{4,12},{8,0},{12,4},{16,24},{20,28},{24,16},{28,20},{1,9},{5... | collective-permute-start | bytes 5308424 | tf_op jit(solution)/shard_map/ppermute | solution.py:100
  11.9 7.0 %copy-start.7 = (s32[2,4,4]{2,1,0:T(4,128)S(1)}, s32[2,4,4]{2,1,0:T(4,128)}, u32[]{:S(2)}) copy-start(s32[2,4,4]{2,1,0:T(4,128)} %param.10) | copy-start | bytes 388
  11.9 40.5 %collective-permute-start.3 = (bf16[512,1536]{1,0:T(8,128)(2,1)}, bf16[512,1536]{1,0:T(8,128)(2,1)}, u32[]{:S(2)}, u32[]{:S(2)}) collective-permute-start(bf16[512,1536]{1,0:T(8,128)(2,1)} %shard_map.93), channel_id=1, source_target_pairs={{1,0},{2,1},{3,2},{5,4},{6,5},{7,6},{9,8},{10,9},{11,10},{13,12},{... | collective-permute-start | bytes 4718600 | tf_op jit(solution)/shard_map/ppermute | solution.py:474
  13.2 39.2 %collective-permute-start.2 = (bf16[512,1536]{1,0:T(8,128)(2,1)}, bf16[512,1536]{1,0:T(8,128)(2,1)}, u32[]{:S(2)}, u32[]{:S(2)}) collective-permute-start(bf16[512,1536]{1,0:T(8,128)(2,1)} %shard_map.93), channel_id=1, source_target_pairs={{0,1},{1,2},{2,3},{4,5},{5,6},{6,7},{8,9},{9,10},{10,11},{12,13},{... | collective-permute-start | bytes 4718600 | tf_op jit(solution)/shard_map/ppermute | solution.py:471
  19.6 8.1 %all-to-all-start = ((f32[2,1,32]{2,1,0:T(1,128)}), f32[2,1,32]{2,1,0:T(1,128)S(1)}, u32[]{:S(2)}, u32[]{:S(2)}) async-start(f32[2,1,32]{2,1,0:T(1,128)} %bitcast.3), calls=%async_computation | async-start | bytes 2048 | tf_op jit(solution)/shard_map/all_to_all | solution.py:104
  27.7 7.9 %all-to-all-start.1 = ((bf16[2,768,1152]{2,1,0:T(8,128)(2,1)}), bf16[2,768,1152]{2,1,0:T(8,128)(2,1)S(1)}, u32[]{:S(2)}, u32[]{:S(2)}) async-start(bf16[2,768,1152]{2,1,0:T(8,128)(2,1)} %maximum_select_fusion), calls=%async_computation.1 | async-start | bytes 7077888 | tf_op jit(solution)/shard_map/all_to_all | solution.py:104
  35.6 16.7 %collective-permute-start.1 = (f32[2,512]{1,0:T(2,128)S(1)}, f32[2,512]{1,0:T(2,128)S(1)}, u32[]{:S(2)}, u32[]{:S(2)}) collective-permute-start(f32[2,512]{1,0:T(2,128)S(1)} %shard_map.92), channel_id=1, source_target_pairs={{0,2},{1,3},{2,0},{3,1},{4,6},{5,7},{6,4},{7,5},{8,10},{9,11},{10,... | collective-permute-start | bytes 12296 | tf_op jit(solution)/shard_map/ppermute | solution.py:488
  52.4 44.6 %collective-permute-start.8 = (bf16[768,1152]{1,0:T(8,128)(2,1)}, bf16[768,1152]{1,0:T(8,128)(2,1)}, u32[]{:S(2)}, u32[]{:S(2)}) collective-permute-start(bf16[768,1152]{1,0:T(8,128)(2,1)} %get-tuple-element.22), channel_id=1, source_target_pairs={{0,12},{4,8},{8,4},{12,0},{16,28},{20,24},{24,20},{28,16},{1,13},{... | collective-permute-start | bytes 5308424 | tf_op jit(solution)/shard_map/ppermute | solution.py:100
  52.5 44.6 %collective-permute-start.9 = (bf16[768,1152]{1,0:T(8,128)(2,1)}, bf16[768,1152]{1,0:T(8,128)(2,1)}, u32[]{:S(2)}, u32[]{:S(2)}) collective-permute-start(bf16[768,1152]{1,0:T(8,128)(2,1)} %get-tuple-element.23), channel_id=1, source_target_pairs={{0,16},{4,20},{8,24},{12,28},{16,0},{20,4},{24,8},{28,12},{1,17},{... | collective-permute-start | bytes 5308424 | tf_op jit(solution)/shard_map/ppermute | solution.py:100
  53.0 25.4 %collective-permute-start.6 = (bf16[512,1536]{1,0:T(8,128)(2,1)}, bf16[512,1536]{1,0:T(8,128)(2,1)}, u32[]{:S(2)}, u32[]{:S(2)}) collective-permute-start(bf16[512,1536]{1,0:T(8,128)(2,1)} %get-tuple-element.20.refs_1_.refs_0_), channel_id=1, source_target_pairs={{1,2},{2,3},{5,6},{6,7},{9,10},{10,11},{13,14},{14,15},{17,18},{18... | collective-permute-start | bytes 4718600 | tf_op jit(solution)/shard_map/ppermute | solution.py:471
  54.8 42.2 %collective-permute-start.7 = (bf16[512,1536]{1,0:T(8,128)(2,1)}, bf16[512,1536]{1,0:T(8,128)(2,1)}, u32[]{:S(2)}, u32[]{:S(2)}) collective-permute-start(bf16[512,1536]{1,0:T(8,128)(2,1)} %get-tuple-element.21.refs_2_), channel_id=1, source_target_pairs={{1,0},{2,1},{5,4},{6,5},{9,8},{10,9},{13,12},{14,13},{17,16},{18,1... | collective-permute-start | bytes 4718600 | tf_op jit(solution)/shard_map/ppermute | solution.py:474
  63.2 1.4 copy-start.1
  64.6 0.9 copy-start.2
  65.5 0.7 copy-start.3
  97.1 28.4 %collective-permute-start.10 = (bf16[512,1536]{1,0:T(8,128)(2,1)}, bf16[512,1536]{1,0:T(8,128)(2,1)S(1)}, u32[]{:S(2)}, u32[]{:S(2)}) collective-permute-start(bf16[512,1536]{1,0:T(8,128)(2,1)} %get-tuple-element.24.refs_1_.refs_0_), channel_id=1, source_target_pairs={{2,3},{6,7},{10,11},{14,15},{18,19},{22,23},{26,27},{30,31}} | collective-permute-start | bytes 4718600 | tf_op jit(solution)/shard_map/ppermute | solution.py:471
  97.8 37.9 %collective-permute-start.11 = (bf16[512,1536]{1,0:T(8,128)(2,1)}, bf16[512,1536]{1,0:T(8,128)(2,1)S(1)}, u32[]{:S(2)}, u32[]{:S(2)}) collective-permute-start(bf16[512,1536]{1,0:T(8,128)(2,1)} %get-tuple-element.25.refs_3_.refs_2_), channel_id=1, source_target_pairs={{1,0},{5,4},{9,8},{13,12},{17,16},{21,20},{25,24},{29,28}} | collective-permute-start | bytes 4718600 | tf_op jit(solution)/shard_map/ppermute | solution.py:474
  99.1 40.3 %collective-permute-start.13 = (bf16[768,1152]{1,0:T(8,128)(2,1)}, bf16[768,1152]{1,0:T(8,128)(2,1)S(1)}, u32[]{:S(2)}, u32[]{:S(2)}) collective-permute-start(bf16[768,1152]{1,0:T(8,128)(2,1)} %get-tuple-element.26.refs_3_), channel_id=1, source_target_pairs={{0,16},{4,20},{8,24},{12,28},{16,0},{20,4},{24,8},{28,12},{1,17},{... | collective-permute-start | bytes 5308424 | tf_op jit(solution)/shard_map/ppermute | solution.py:100
  100.8 40.0 %collective-permute-start.14 = (bf16[768,1152]{1,0:T(8,128)(2,1)}, bf16[768,1152]{1,0:T(8,128)(2,1)S(1)}, u32[]{:S(2)}, u32[]{:S(2)}) collective-permute-start(bf16[768,1152]{1,0:T(8,128)(2,1)} %get-tuple-element.27.refs_6_), channel_id=1, source_target_pairs={{0,8},{4,12},{8,0},{12,4},{16,24},{20,28},{24,16},{28,20},{1,9},{5... | collective-permute-start | bytes 5308424 | tf_op jit(solution)/shard_map/ppermute | solution.py:100
  135.7 5.3 %copy-start.4 = (f32[128]{0:T(128)S(1)}, f32[128]{0:T(128)}, u32[]{:S(2)}) copy-start(f32[128]{0:T(128)} %param.15) | copy-start | bytes 1540
  135.7 5.3 %copy-start.5 = (f32[128]{0:T(128)S(1)}, f32[128]{0:T(128)}, u32[]{:S(2)}) copy-start(f32[128]{0:T(128)} %param.16) | copy-start | bytes 1540
  137.6 3.5 %collective-permute-start.12 = (bf16[1,1,512,1536]{3,2,1,0:T(8,128)(2,1)S(1)}, bf16[1,1,512,1536]{3,2,1,0:T(8,128)(2,1)S(1)}, u32[]{:S(2)}, u32[]{:S(2)}) collective-permute-start(bf16[1,1,512,1536]{3,2,1,0:T(8,128)(2,1)S(1)} %shard_map.99.last_here), channel_id=1, source_target_pairs={{0,4},{4,0},{8,12},{12,8},{16,20},{20,16},{24,28},{28,24},{1,5},{5... | collective-permute-start | bytes 4718600 | tf_op jit(solution)/shard_map/ppermute | solution.py:100
  156.3 0.9 copy-start.6

commit v3 on v2

--- a/solution.py
+++ b/solution.py
@@ -181,23 +181,26 @@
             pltpu.make_async_copy(choice, target, sem).start()
 
 
-def norm_kernel(slots, numbers, plan_ref, mean_ref, scale_ref, gains_ref, *refs):
+def norm_kernel(slots, numbers, plan_ref, stats_ref, gains_ref, *refs):
     arrays = dict(zip(numbers, refs))
-    out_ref, raw, normed, in_sems, out_sems = refs[-5:]
-    rows = raw.shape[1]
+    out_ref, raw, normed, columns, in_sems, out_sems = refs[-6:]
+    _, rows, features = raw.shape
     step = 64
-
     for n, slot in enumerate(slots):
         fetch(plan_ref[ARRIVAL + slot], arrays, raw.at[n], in_sems.at[n])
+    stats = jnp.sum(stats_ref[...], axis=0) / (4 * features)
+    mean = stats[0:1]
+    scale = lax.rsqrt(stats[1:2] - mean * mean + EPS)
+    columns[...] = jnp.concatenate([mean, scale, jnp.zeros((6, rows), jnp.float32)], axis=0).T
     for n, slot in enumerate(slots):
-        gain = gains_ref[pl.ds(plan_ref[PLACE + slot], 1), :]
+        gain = gains_ref[:, pl.ds(pl.multiple_of(plan_ref[PLACE + slot] * features, features), features)]
         pltpu.make_async_copy(refs[0], raw.at[n], in_sems.at[n]).wait()
 
         @pl.loop(0, rows // step)
         def _(tile):
             at = pl.ds(pl.multiple_of(tile * step, step), step)
             values = raw[n, at, :].astype(jnp.float32)
-            normed[n, at, :] = ((values - mean_ref[at, :]) * scale_ref[at, :] * gain).astype(jnp.bfloat16)
+            normed[n, at, :] = ((values - columns[at, 0:1]) * columns[at, 1:2] * gain).astype(jnp.bfloat16)
 
         for copy in range(out_ref.shape[0]):
             pltpu.make_async_copy(normed.at[n], out_ref.at[copy, n], out_sems.at[copy, n]).start()
@@ -206,23 +209,24 @@
             pltpu.make_async_copy(normed.at[n], out_ref.at[copy, n], out_sems.at[copy, n]).wait()
 
 
-def norm(plan_here, slots, copies, mean, scale, gains, arrays, *others):
+def norm(plan_here, slots, copies, stats, gains, arrays, *others):
     rows, features = next(iter(arrays.values())).shape
     shape = (len(slots), rows, features)
     return pl.pallas_call(
         functools.partial(norm_kernel, slots, tuple(arrays)),
-        in_specs=[SMEM] + [VMEM] * 3 + [ANY] * len(arrays) + [ANY] * len(others),
+        in_specs=[SMEM] + [VMEM] * 2 + [ANY] * (len(arrays) + len(others)),
         out_specs=HBM,
         out_shape=jax.ShapeDtypeStruct((copies, *shape), jnp.bfloat16),
         scratch_shapes=[
             pltpu.VMEM(shape, jnp.bfloat16),
             pltpu.VMEM(shape, jnp.bfloat16),
+            pltpu.VMEM((rows, 8), jnp.float32),
             pltpu.SemaphoreType.DMA((len(slots),)),
             pltpu.SemaphoreType.DMA((copies, len(slots))),
         ],
         compiler_params=params(16),
         cost_estimate=FREE,
-    )(plan_here, mean, scale, gains, *arrays.values(), *others)
+    )(plan_here, stats, gains, *arrays.values(), *others)
 
 
 class Tokens:
@@ -375,25 +379,24 @@
 
 
 def finish_kernel(
+    side,
     plan_ref,
     mask_ref,
     total_ref,
     next_tokens,
     next_weights,
-    last_here,
-    last_there,
+    last_ref,
     diag_same,
     diag_cross,
     query_gain,
     key_gain,
-    out_ref,
-    near_tokens,
-    diag_tokens,
+    *refs,
 ):
+    out_ref, near_tokens, diag_tokens = refs[-3:]
     core = plan_ref[CORE_AT]
-    tiles, _, width = total_ref.shape
+    width = total_ref.shape[2]
     heads = width // (3 * DH)
-    half = tiles // 2
+    tiles = near_tokens.shape[0]
     depth = diag_same.shape[0]
 
     def place(tile, near, diag):
@@ -403,13 +406,12 @@
             diag_tokens[part, tile] = diag(pl.ds(first, depth))
 
     for tile in range(tiles):
-        at = pl.ds(tile % half * TPD, TPD)
-
-        def last(features, at=at, ref=last_here if tile < half else last_there):
-            return ref[0, 0, at, features]
+
+        def last(features, tile=tile):
+            return last_ref[0, 0, pl.ds(tile * TPD, TPD), features]
 
         def early(features, tile=tile):
-            return next_tokens[tile, :, features]
+            return next_tokens[side * tiles + tile, :, features]
 
         @pl.when(plan_ref[4] == 3)
         def _():
@@ -423,7 +425,7 @@
     for tile in range(tiles):
         sums = []
         for first, end in column_groups(width):
-            part = total_ref[tile, :, first:end]
+            part = total_ref[side * tiles + tile, :, first:end]
             for tokens, weights in (
                 (near_tokens[tile], next_weights),
                 (diag_tokens[0, tile], diag_same),
@@ -431,32 +433,31 @@
             ):
                 part = part + jnp.dot(tokens, weights[:, first:end], preferred_element_type=jnp.float32)
             sums += [part[:, at : at + DH] for at in range(0, end - first, DH)]
-        whose = core if tile < half else 1 - core
+        whose = core if side == 0 else 1 - core
         for h in range(heads):
             query = head_norm(sums[query_first[h] // DH], query_gain[...]).astype(jnp.bfloat16)
             key = head_norm(sums[key_first[h] // DH], key_gain[...]).astype(jnp.bfloat16)
             value = sums[value_first[h] // DH].astype(jnp.bfloat16)
-            out_ref[whose, h, pl.ds(tile % half * TPD, TPD), :] = attend(
-                query, key, value, mask_ref, whose * half + tile % half
+            out_ref[pl.ds(tile * TPD, TPD), h * DH : (h + 1) * DH] = attend(
+                query, key, value, mask_ref, whose * tiles + tile
             )
 
 
-def finish(plan_here, mask, total, next_tokens, next_weights, last, diag, query_gain, key_gain):
+def finish(side, plan_here, mask, total, next_tokens, next_weights, last, diag, query_gain, key_gain, *others):
     tiles, _, width = total.shape
     depth = diag[0].shape[0]
-    heads = width // (3 * DH)
     return pl.pallas_call(
-        finish_kernel,
-        in_specs=[SMEM] * 2 + [VMEM] * 9,
+        functools.partial(finish_kernel, side),
+        in_specs=[SMEM] * 2 + [VMEM] * 8 + [ANY] * len(others),
         out_specs=VMEM,
-        out_shape=jax.ShapeDtypeStruct((2, heads, tiles // 2 * TPD, DH), jnp.bfloat16),
+        out_shape=jax.ShapeDtypeStruct((tiles // 2 * TPD, width // 3), jnp.bfloat16),
         scratch_shapes=[
-            pltpu.VMEM((tiles, TPD, 2 * depth), jnp.bfloat16),
-            pltpu.VMEM((2, tiles, TPD, depth), jnp.bfloat16),
+            pltpu.VMEM((tiles // 2, TPD, 2 * depth), jnp.bfloat16),
+            pltpu.VMEM((2, tiles // 2, TPD, depth), jnp.bfloat16),
         ],
         compiler_params=params(18),
         cost_estimate=FREE,
-    )(plan_here, mask, total, next_tokens, next_weights, *last, *diag, query_gain, key_gain)
+    )(plan_here, mask, total, next_tokens, next_weights, last, *diag, query_gain, key_gain, *others)
 
 
 def per_device_8x4(tokens, block_mask, norm_gain, w_query, w_key, w_value, query_gain, key_gain):
@@ -474,56 +475,45 @@
         return lax.ppermute(array, "tensor", [(i + 1, i) for i in range(last)])
 
     mine, other = pack(w_query, w_key, w_value)
+    x_same, y_cross = swap(mine, X), swap(other, Y | CORE)
+    up1, down1 = up(tokens, 0), down(tokens, 3)
     values = tokens.astype(jnp.float32)
     stats = jnp.stack([jnp.sum(values, axis=1), jnp.sum(values * values, axis=1)])
-    stats = stats + lax.ppermute(stats, "tensor", [(i, i ^ 1) for i in range(4)])
-
-    x_same, y_cross = swap(mine, X), swap(other, Y | CORE)
-    (sent,) = gate((tokens,), (stats, mine))
-    up1, down1 = up(sent, 0), down(sent, 3)
     own = trade(jnp.where(core == 0, jnp.stack([mine, other]), jnp.stack([other, mine])))
     mask = block_mask.astype(jnp.float32).reshape(1, -1)
     mask = trade(jnp.concatenate([mask, mask])).reshape(-1)
     (stats,) = gate((stats,), (own, mask))
-    stats = stats + lax.ppermute(stats, "tensor", [(i, i ^ 2) for i in range(4)])
-
-    mine, other, up1, down1 = gate((mine, other, up1, down1), (x_same, y_cross, stats))
+    stats = lax.all_to_all(jnp.stack([stats] * 4), "tensor", 0, 0)
+    gains = norm_gain.reshape(1, -1)
+
+    mine, other, up1, down1, stats = gate((mine, other, up1, down1, stats), (x_same, y_cross))
     x_cross, y_same = swap(other, X | CORE), swap(mine, Y)
     up2, down2 = up(up1, 1), down(down1, 2)
 
-    means = stats / (4 * features)
-    mean = means[0][:, None]
-    scale = lax.rsqrt(means[1] - means[0] * means[0] + EPS)[:, None]
-    gains = norm_gain.reshape(4, features)
     arrived = {0: tokens, 1: up1, 4: down1}
-    normed = [trade(norm(plan_here, (0, 1), 2, mean, scale, gains, arrived))]
-
-    x_same, y_cross, up2, down2 = gate(
-        (x_same, y_cross, up2, down2), (x_cross, y_same, normed[0])
-    )
+    normed = [trade(norm(plan_here, (0, 1), 2, stats, gains, arrived))]
+
+    x_same, y_cross, up2, down2 = gate((x_same, y_cross, up2, down2), (x_cross, y_same, normed[0]))
     diag_same, diag_cross = swap(x_same, Y), swap(y_cross, X)
     up3, down3 = up(up2, 2), down(down2, 1)
     arrived = {1: up1, 2: up2, 4: down1, 5: down2}
-    normed.append(trade(norm(plan_here, (2,), 2, mean, scale, gains, arrived)))
+    normed.append(trade(norm(plan_here, (2,), 2, stats, gains, arrived)))
     near = [own, x_same, x_cross, y_same, y_cross]
     total, next_tokens, next_weights = project(plan_here, normed, near)
 
     arrived = {2: up2, 3: up3, 5: down2, 6: down3}
-    last = norm(plan_here, (3,), 1, mean, scale, gains, arrived, total)
-    last = (last, swap(last, CORE))
-    out = finish(
-        plan_here,
-        mask,
-        total,
-        next_tokens,
-        next_weights,
-        last,
-        (diag_same, diag_cross),
-        query_gain[None, :],
-        key_gain[None, :],
+    last = norm(plan_here, (3,), 1, stats, gains, arrived, total)
+    diag = (diag_same, diag_cross)
+    gain_pair = (query_gain[None, :], key_gain[None, :])
+    early = (plan_here, mask, total, next_tokens, next_weights)
+    theirs = finish(1, *early, swap(last, CORE), diag, *gain_pair)
+    here = finish(0, *early, last, diag, *gain_pair, theirs)
+    there = swap(theirs, CORE)
+    return jnp.where(
+        core == 0,
+        jnp.concatenate([here, there], axis=1),
+        jnp.concatenate([there, here], axis=1),
     )
-    out = trade(out)
-    return jnp.concatenate([out[i // heads, i % heads] for i in range(2 * heads)], axis=1)
 
 
 def solution(mesh):

time: 159 us -> 150 us (0.943)
  blocking collectives: 19.4 us -> 32.7 us
  local copies, waits for them, and re-layouts: 12.5 us -> 2.14 us
  waiting for transfers between devices: 49.1 us -> 39.9 us
  starting transfers between devices: 31 us -> 27.1 us
  Pallas kernels: 36.2 us -> 38.2 us
    all_to_all x0 -> x1, blocking collectives: none -> 17.7 us  [per_device_8x4(): stats = lax.all_to_all(jnp.stack([stats] * 4), 'tensor', 0, 0)]
    ppermute x2 -> x0, waiting for transfers between devices: 14.1 us -> none  [the longest x1 14.1 us: per_device_8x4(): lax.ppermute(stats, 'tensor', [(i, i ^ 2) for i in range(4)])]
    ppermute x3, waiting for transfers between devices: 28.9 us -> 35.9 us  [down(): return lax.ppermute(array, 'tensor', [(i + 1, i) for i in range(last)])]
    ppermute x2 -> x0, starting transfers between devices: 5.67 us -> none  [the longest x1 3.09 us: per_device_8x4(): lax.ppermute(stats, 'tensor', [(i, i ^ 1) for i in range(4)])]
    unnamed x22 -> x14, local copies, waits for them, and re-layouts: 5.28 us -> 0.76 us
    all_to_all x3 -> x2, blocking collectives: 19.4 us -> 15 us  [trade(): lax.all_to_all(array, 'dp', 0, 0, axis_index_groups=[[i, i + 1] for i in...]
    all_to_all x2, waiting for transfers between devices: 2.62 us -> 0.62 us  [trade(): lax.all_to_all(array, 'dp', 0, 0, axis_index_groups=[[i, i + 1] for i in...]
    ppermute x7 -> x8, starting transfers between devices: 6.03 us -> 7.75 us  [swap(): return lax.ppermute(array, 'dp', [(i, i ^ bits) for i in range(8)])]
  transfers between devices with their start and end apart: 17 -> 16, of which waited for: 7 -> 6; matrix products, arithmetic and copies ran while one was open for 10% -> 6% of each run, Pallas kernels for 16% -> 19%
where the time goes in v3:
time: 150 us
  waiting for transfers between devices  39.9 us (27%)
  Pallas kernels  38.2 us (25%)
  blocking collectives  32.7 us (22%)
  starting transfers between devices  27.1 us (18%)
  other arithmetic  9.4 us (6%)
  local copies, waits for them, and re-layouts  2.14 us (1%)
    ppermute x3, waiting for transfers between devices, down(): return lax.ppermute(array, 'tensor', [(i + 1, i) for i in range(last)])  35.9 us
    all_to_all x1, blocking collectives, per_device_8x4(): stats = lax.all_to_all(jnp.stack([stats] * 4), 'tensor', 0, 0)  17.7 us
    all_to_all x2, blocking collectives, trade(): lax.all_to_all(array, 'dp', 0, 0, axis_index_groups=[[i, i + 1] for i in...  15 us
    pallas_call x1, Pallas kernels, project(): pl.pallas_call(functools.partial(project_kernel, tokens), in_specs=[SMEM]...  13.7 us
    pallas_call x2, Pallas kernels, finish(): pl.pallas_call(functools.partial(finish_kernel, side), in_specs=[SMEM] *...  11.4 us
    pallas_call x3, Pallas kernels, norm(): pl.pallas_call(functools.partial(norm_kernel, slots, tuple(arrays)), in_s...  9.62 us
    ppermute x3, starting transfers between devices, up(): return lax.ppermute(array, 'tensor', [(i, i + 1) for i in range(first, 3)])  8.25 us
    ppermute x8, starting transfers between devices, swap(): return lax.ppermute(array, 'dp', [(i, i ^ bits) for i in range(8)])  7.75 us
  transfers between devices with their start and end apart: 16, of which 6 were waited for; matrix products, arithmetic and copies ran while one was open for 6% of the time, Pallas kernels for 19%

profile of v3, /device:TPU:0, one launch (start us, length us, event | category | flops | bytes accessed | tf_op | source)
XLA Modules:
  0.0 149.7 jit_solution(17690980841458543389)
XLA Ops:
  0.0 3.4 %shard_map.91 = (bf16[768,1152]{1,0:T(8,128)(2,1)}, bf16[768,1152]{1,0:T(8,128)(2,1)}) custom-call(bf16[768,768]{1,0:T(8,128)(2,1)} %refs_0_.2, bf16[768,768]{1,0:T(8,128)(2,1)} %refs_1_.1, bf16[768,768]{1,0:T(8,128)(2,1)} %refs_2_.1), custom_call_target="tpu_custom_call" | custom-call | tf_op jit(solution)/shard_map/pallas_call | solution.py:160
  3.4 3.0 %collective-permute-start.2 = (bf16[768,1152]{1,0:T(8,128)(2,1)}, bf16[768,1152]{1,0:T(8,128)(2,1)}, u32[]{:S(2)}, u32[]{:S(2)}) collective-permute-start(bf16[768,1152]{1,0:T(8,128)(2,1)} %get-tuple-element.19.refs_0_), channel_id=1, source_target_pairs={{0,8},{4,12},{8,0},{12,4},{16,24},{20,28},{24,16},{28,20},{1,9},{5... | collective-permute-start | bytes 5308424 | tf_op jit(solution)/shard_map/ppermute | solution.py:100
  6.4 0.7 collective-permute-start.3
  7.1 1.3 collective-permute-start.1
  8.4 5.7 %collective-permute-start = (bf16[512,1536]{1,0:T(8,128)(2,1)}, bf16[512,1536]{1,0:T(8,128)(2,1)}, u32[]{:S(2)}, u32[]{:S(2)}) collective-permute-start(bf16[512,1536]{1,0:T(8,128)(2,1)} %refs_0_.3), channel_id=1, source_target_pairs={{0,1},{1,2},{2,3},{4,5},{5,6},{6,7},{8,9},{9,10},{10,11},{12,13},{... | collective-permute-start | bytes 4718600 | tf_op jit(solution)/shard_map/ppermute | solution.py:472
  14.8 3.2 %all-to-all-start = ((f32[2,1,32]{2,1,0:T(1,128)}), f32[2,1,32]{2,1,0:T(1,128)S(1)}, u32[]{:S(2)}, u32[]{:S(2)}) async-start(f32[2,1,32]{2,1,0:T(1,128)} %bitcast.3), calls=%async_computation | async-start | bytes 2048 | tf_op jit(solution)/shard_map/all_to_all | solution.py:104
  18.0 5.0 %maximum_select_fusion = bf16[2,768,1152]{2,1,0:T(8,128)(2,1)} fusion(bf16[1,768,1152]{2,1,0:T(8,128)(2,1)} %bitcast.7, bf16[1,768,1152]{2,1,0:T(8,128)(2,1)} %bitcast.6, pred[]{:T(512)S(6)} %eq.6), kind=kLoop, calls=%fused_computation.2 | loop fusion | flops 5308416 | bytes 7077889 | tf_op jit(solution)/shard_map/jit(_where)/select_n | solution.py:482
  23.0 4.0 %all-to-all-start.1 = ((bf16[2,768,1152]{2,1,0:T(8,128)(2,1)}), bf16[2,768,1152]{2,1,0:T(8,128)(2,1)S(1)}, u32[]{:S(2)}, u32[]{:S(2)}) async-start(bf16[2,768,1152]{2,1,0:T(8,128)(2,1)} %maximum_select_fusion), calls=%async_computation.1 | async-start | bytes 7077888 | tf_op jit(solution)/shard_map/all_to_all | solution.py:104
  27.6 0.7 reduce.3
  28.3 2.0 %convert_reduce_fusion = (f32[512]{0:T(512)S(1)}, f32[512]{0:T(512)S(1)}) fusion(bf16[512,1536]{1,0:T(8,128)(2,1)} %refs_0_.3), kind=kLoop, calls=%fused_computation.1 | loop fusion | flops 3144704 | bytes 1576960 | tf_op jit(solution)/shard_map/reduce_sum | solution.py:481
  30.9 17.7 %all_to_all.29.refs_4_ = f32[4,2,512]{2,1,0:T(2,128)S(1)} all-to-all(f32[4,2,512]{2,1,0:T(2,128)S(1)} %stack.37), channel_id=1, replica_groups=mesh['dp'=8,'tensor'=4] {'tensor'}, dimensions={0} | all-to-all | bytes 32768 | tf_op jit(solution)/shard_map/all_to_all | solution.py:486
  49.4 1.8 %collective-permute-start.4 = (bf16[512,1536]{1,0:T(8,128)(2,1)}, bf16[512,1536]{1,0:T(8,128)(2,1)}, u32[]{:S(2)}, u32[]{:S(2)}) collective-permute-start(bf16[512,1536]{1,0:T(8,128)(2,1)} %get-tuple-element.22.refs_1_.refs_0_), channel_id=1, source_target_pairs={{1,2},{2,3},{5,6},{6,7},{9,10},{10,11},{13,14},{14,15},{17,18},{18... | collective-permute-start | bytes 4718600 | tf_op jit(solution)/shard_map/ppermute | solution.py:472
  51.1 1.3 collective-permute-start.5
  52.5 0.7 dynamic-slice_bitcast_fusion
  53.2 0.7 copy-done
  54.0 4.5 %shard_map.94 = bf16[2,2,512,1536]{3,2,1,0:T(8,128)(2,1)S(1)} custom-call(s32[17]{0:T(128)S(1)} %pad_add_fusion.plan_ref, f32[4,2,512]{2,1,0:T(2,128)S(1)} %get-tuple-element.21.stats_ref, f32[1,6144]{1,0:T(1,128)S(1)} %bitcast.13, bf16[512,1536]{1,0:T(8,128)(2,1)} %refs_0_.3, bf16[512,1536]{1,0:T(8,128)(2,1)} %get-tuple-element.22.refs_1_.refs_0_, ...), custom_call_target="tpu_custom_call" | custom-call | tf_op jit(solution)/shard_map/pallas_call | solution.py:215
  58.4 8.8 %all_to_all.30.refs_6_.refs_0_ = bf16[2,2,512,1536]{3,2,1,0:T(8,128)(2,1)S(1)} all-to-all(bf16[2,2,512,1536]{3,2,1,0:T(8,128)(2,1)S(1)} %shard_map.94), channel_id=1, replica_groups={{0,4},{8,12},{16,20},{24,28},{1,5},{9,13},{17,21},{25,29},{2,6},{10,14}..., dimensions={0} | all-to-all | bytes 12582912 | tf_op jit(solution)/shard_map/all_to_all | solution.py:104
  67.2 25.6 %collective-permute-done.5.refs_3_ = bf16[512,1536]{1,0:T(8,128)(2,1)} collective-permute-done((bf16[512,1536]{1,0:T(8,128)(2,1)}, bf16[512,1536]{1,0:T(8,128)(2,1)}, u32[]{:S(2)}, u32[]{:S(2)}) %collective-permute-start.5) | collective-permute-done | bytes 1572896 | tf_op jit(solution)/shard_map/ppermute | solution.py:475
  92.8 0.8 collective-permute-start.8
  93.6 1.3 collective-permute-start.9
  94.9 1.6 %collective-permute-start.10 = (bf16[768,1152]{1,0:T(8,128)(2,1)}, bf16[768,1152]{1,0:T(8,128)(2,1)S(1)}, u32[]{:S(2)}, u32[]{:S(2)}) collective-permute-start(bf16[768,1152]{1,0:T(8,128)(2,1)} %get-tuple-element.28.refs_3_), channel_id=1, source_target_pairs={{0,16},{4,20},{8,24},{12,28},{16,0},{20,4},{24,8},{28,12},{1,17},{... | collective-permute-start | bytes 5308424 | tf_op jit(solution)/shard_map/ppermute | solution.py:100
  96.5 1.5 collective-permute-start.11
  98.0 3.2 %shard_map.96 = bf16[2,1,512,1536]{3,2,1,0:T(8,128)(2,1)S(1)} custom-call(s32[17]{0:T(128)S(1)} %pad_add_fusion.plan_ref, f32[4,2,512]{2,1,0:T(2,128)S(1)} %get-tuple-element.21.stats_ref, f32[1,6144]{1,0:T(1,128)S(1)} %bitcast.14, bf16[512,1536]{1,0:T(8,128)(2,1)} %get-tuple-element.22.refs_1_.refs_0_, bf16[512,1536]{1,0:T(8,128)(2,1)} %get-tuple-element.26.refs_1_.refs_0_, ...), custom_call_target="tpu_custom_call" | custom-call | tf_op jit(solution)/shard_map/pallas_call | solution.py:215
  101.2 6.3 %all_to_all.31.refs_1_ = bf16[2,1,512,1536]{3,2,1,0:T(8,128)(2,1)S(1)} all-to-all(bf16[2,1,512,1536]{3,2,1,0:T(8,128)(2,1)S(1)} %shard_map.96), channel_id=1, replica_groups={{0,4},{8,12},{16,20},{24,28},{1,5},{9,13},{17,21},{25,29},{2,6},{10,14}..., dimensions={0} | all-to-all | bytes 6291456 | tf_op jit(solution)/shard_map/all_to_all | solution.py:104
  107.4 13.7 %shard_map.97 = (f32[4,256,1152]{2,1,0:T(8,128)S(1)}, bf16[4,256,1536]{2,1,0:T(8,128)(2,1)S(1)}, bf16[1536,1152]{1,0:T(8,128)(2,1)S(1)}) custom-call(s32[17]{0:T(128)S(1)} %pad_add_fusion.plan_ref, bf16[2,2,512,1536]{3,2,1,0:T(8,128)(2,1)S(1)} %all_to_all.30.refs_6_.refs_0_, bf16[2,1,512,1536]{3,2,1,0:T(8,128)(2,1)S(1)} %all_to_all.31.refs_1_, ...), custom_call_target="tpu_custom_call" | custom-call | tf_op jit(solution)/shard_map/pallas_call | solution.py:338
  121.2 10.3 %collective-permute-done.9.refs_3_ = bf16[512,1536]{1,0:T(8,128)(2,1)S(1)} collective-permute-done((bf16[512,1536]{1,0:T(8,128)(2,1)}, bf16[512,1536]{1,0:T(8,128)(2,1)S(1)}, u32[]{:S(2)}, u32[]{:S(2)}) %collective-permute-start.9) | collective-permute-done | bytes 1572896 | tf_op jit(solution)/shard_map/ppermute | solution.py:475
  131.5 2.0 %shard_map.98.last_ref = bf16[1,1,512,1536]{3,2,1,0:T(8,128)(2,1)S(1)} custom-call(s32[17]{0:T(128)S(1)} %pad_add_fusion.plan_ref, f32[4,2,512]{2,1,0:T(2,128)S(1)} %get-tuple-element.21.stats_ref, f32[1,6144]{1,0:T(1,128)S(1)} %bitcast.15, bf16[512,1536]{1,0:T(8,128)(2,1)} %get-tuple-element.26.refs_1_.refs_0_, ...), custom_call_target="tpu_custom_call" | custom-call | tf_op jit(solution)/shard_map/pallas_call | solution.py:215
  133.5 1.6 %collective-permute-done.10.diag_same = bf16[768,1152]{1,0:T(8,128)(2,1)S(1)} collective-permute-done((bf16[768,1152]{1,0:T(8,128)(2,1)}, bf16[768,1152]{1,0:T(8,128)(2,1)S(1)}, u32[]{:S(2)}, u32[]{:S(2)}) %collective-permute-start.10) | collective-permute-done | bytes 1769504 | tf_op jit(solution)/shard_map/ppermute | solution.py:100
  135.2 1.2 collective-permute-done.11.diag_cross
  136.9 5.7 %shard_map.99.refs_0_ = bf16[512,384]{1,0:T(8,128)(2,1)S(1)} custom-call(s32[17]{0:T(128)S(1)} %pad_add_fusion.plan_ref, f32[64]{0:T(128)S(1)} %copy-done.3, f32[4,256,1152]{2,1,0:T(8,128)S(1)} %get-tuple-element.30.refs_4_.total_ref, bf16[4,256,1536]{2,1,0:T(8,128)(2,1)S(1)} %get-tuple-element.31.next_tokens, ...), custom_call_target="tpu_custom_call" | custom-call | tf_op jit(solution)/shard_map/pallas_call | solution.py:449
  142.9 5.7 %shard_map.100 = bf16[512,384]{1,0:T(8,128)(2,1)S(1)} custom-call(s32[17]{0:T(128)S(1)} %pad_add_fusion.plan_ref, f32[64]{0:T(128)S(1)} %copy-done.3, f32[4,256,1152]{2,1,0:T(8,128)S(1)} %get-tuple-element.30.refs_4_.total_ref, bf16[4,256,1536]{2,1,0:T(8,128)(2,1)S(1)} %get-tuple-element.31.next_tokens, ...), custom_call_target="tpu_custom_call" | custom-call | tf_op jit(solution)/shard_map/pallas_call | solution.py:449
  148.6 1.1 maximum_select_fusion.1
  (40 shorter events, 3.6 us)
Async XLA Ops:
  0.0 14.1 %copy-start.6 = (s32[2,4,4]{2,1,0:T(4,128)S(1)}, s32[2,4,4]{2,1,0:T(4,128)}, u32[]{:S(2)}) copy-start(s32[2,4,4]{2,1,0:T(4,128)} %param.10) | copy-start | bytes 388
  3.4 45.2 %collective-permute-start.2 = (bf16[768,1152]{1,0:T(8,128)(2,1)}, bf16[768,1152]{1,0:T(8,128)(2,1)}, u32[]{:S(2)}, u32[]{:S(2)}) collective-permute-start(bf16[768,1152]{1,0:T(8,128)(2,1)} %get-tuple-element.19.refs_0_), channel_id=1, source_target_pairs={{0,8},{4,12},{8,0},{12,4},{16,24},{20,28},{24,16},{28,20},{1,9},{5... | collective-permute-start | bytes 5308424 | tf_op jit(solution)/shard_map/ppermute | solution.py:100
  6.4 42.2 %collective-permute-start.3 = (bf16[768,1152]{1,0:T(8,128)(2,1)}, bf16[768,1152]{1,0:T(8,128)(2,1)}, u32[]{:S(2)}, u32[]{:S(2)}) collective-permute-start(bf16[768,1152]{1,0:T(8,128)(2,1)} %get-tuple-element.20.refs_1_), channel_id=1, source_target_pairs={{0,20},{4,16},{8,28},{12,24},{16,4},{20,0},{24,12},{28,8},{1,21},{... | collective-permute-start | bytes 5308424 | tf_op jit(solution)/shard_map/ppermute | solution.py:100
  7.1 41.5 %collective-permute-start.1 = (bf16[512,1536]{1,0:T(8,128)(2,1)}, bf16[512,1536]{1,0:T(8,128)(2,1)}, u32[]{:S(2)}, u32[]{:S(2)}) collective-permute-start(bf16[512,1536]{1,0:T(8,128)(2,1)} %refs_0_.3), channel_id=1, source_target_pairs={{1,0},{2,1},{3,2},{5,4},{6,5},{7,6},{9,8},{10,9},{11,10},{13,12},{... | collective-permute-start | bytes 4718600 | tf_op jit(solution)/shard_map/ppermute | solution.py:475
  8.4 40.2 %collective-permute-start = (bf16[512,1536]{1,0:T(8,128)(2,1)}, bf16[512,1536]{1,0:T(8,128)(2,1)}, u32[]{:S(2)}, u32[]{:S(2)}) collective-permute-start(bf16[512,1536]{1,0:T(8,128)(2,1)} %refs_0_.3), channel_id=1, source_target_pairs={{0,1},{1,2},{2,3},{4,5},{5,6},{6,7},{8,9},{9,10},{10,11},{12,13},{... | collective-permute-start | bytes 4718600 | tf_op jit(solution)/shard_map/ppermute | solution.py:472
  14.8 8.2 %all-to-all-start = ((f32[2,1,32]{2,1,0:T(1,128)}), f32[2,1,32]{2,1,0:T(1,128)S(1)}, u32[]{:S(2)}, u32[]{:S(2)}) async-start(f32[2,1,32]{2,1,0:T(1,128)} %bitcast.3), calls=%async_computation | async-start | bytes 2048 | tf_op jit(solution)/shard_map/all_to_all | solution.py:104
  23.0 7.9 %all-to-all-start.1 = ((bf16[2,768,1152]{2,1,0:T(8,128)(2,1)}), bf16[2,768,1152]{2,1,0:T(8,128)(2,1)S(1)}, u32[]{:S(2)}, u32[]{:S(2)}) async-start(bf16[2,768,1152]{2,1,0:T(8,128)(2,1)} %maximum_select_fusion), calls=%async_computation.1 | async-start | bytes 7077888 | tf_op jit(solution)/shard_map/all_to_all | solution.py:104
  28.3 2.6 %copy-start.2 = (f32[64]{0:T(128)}, f32[64]{0:T(128)S(1)}, u32[]{:S(2)}) copy-start(f32[64]{0:T(128)S(1)} %reshape.15.refs_2_.mask_ref) | copy-start | bytes 772
  48.6 44.2 %collective-permute-start.6 = (bf16[768,1152]{1,0:T(8,128)(2,1)}, bf16[768,1152]{1,0:T(8,128)(2,1)}, u32[]{:S(2)}, u32[]{:S(2)}) collective-permute-start(bf16[768,1152]{1,0:T(8,128)(2,1)} %get-tuple-element.24), channel_id=1, source_target_pairs={{0,12},{4,8},{8,4},{12,0},{16,28},{20,24},{24,20},{28,16},{1,13},{... | collective-permute-start | bytes 5308424 | tf_op jit(solution)/shard_map/ppermute | solution.py:100
  48.9 43.9 %collective-permute-start.7 = (bf16[768,1152]{1,0:T(8,128)(2,1)}, bf16[768,1152]{1,0:T(8,128)(2,1)}, u32[]{:S(2)}, u32[]{:S(2)}) collective-permute-start(bf16[768,1152]{1,0:T(8,128)(2,1)} %get-tuple-element.25), channel_id=1, source_target_pairs={{0,16},{4,20},{8,24},{12,28},{16,0},{20,4},{24,8},{28,12},{1,17},{... | collective-permute-start | bytes 5308424 | tf_op jit(solution)/shard_map/ppermute | solution.py:100
  49.4 17.9 %collective-permute-start.4 = (bf16[512,1536]{1,0:T(8,128)(2,1)}, bf16[512,1536]{1,0:T(8,128)(2,1)}, u32[]{:S(2)}, u32[]{:S(2)}) collective-permute-start(bf16[512,1536]{1,0:T(8,128)(2,1)} %get-tuple-element.22.refs_1_.refs_0_), channel_id=1, source_target_pairs={{1,2},{2,3},{5,6},{6,7},{9,10},{10,11},{13,14},{14,15},{17,18},{18... | collective-permute-start | bytes 4718600 | tf_op jit(solution)/shard_map/ppermute | solution.py:472
  51.1 41.7 %collective-permute-start.5 = (bf16[512,1536]{1,0:T(8,128)(2,1)}, bf16[512,1536]{1,0:T(8,128)(2,1)}, u32[]{:S(2)}, u32[]{:S(2)}) collective-permute-start(bf16[512,1536]{1,0:T(8,128)(2,1)} %get-tuple-element.23.refs_2_), channel_id=1, source_target_pairs={{1,0},{2,1},{5,4},{6,5},{9,8},{10,9},{13,12},{14,13},{17,16},{18,1... | collective-permute-start | bytes 4718600 | tf_op jit(solution)/shard_map/ppermute | solution.py:475
  53.2 0.7 copy-start
  92.8 28.3 %collective-permute-start.8 = (bf16[512,1536]{1,0:T(8,128)(2,1)}, bf16[512,1536]{1,0:T(8,128)(2,1)S(1)}, u32[]{:S(2)}, u32[]{:S(2)}) collective-permute-start(bf16[512,1536]{1,0:T(8,128)(2,1)} %get-tuple-element.26.refs_1_.refs_0_), channel_id=1, source_target_pairs={{2,3},{6,7},{10,11},{14,15},{18,19},{22,23},{26,27},{30,31}} | collective-permute-start | bytes 4718600 | tf_op jit(solution)/shard_map/ppermute | solution.py:472
  93.6 37.9 %collective-permute-start.9 = (bf16[512,1536]{1,0:T(8,128)(2,1)}, bf16[512,1536]{1,0:T(8,128)(2,1)S(1)}, u32[]{:S(2)}, u32[]{:S(2)}) collective-permute-start(bf16[512,1536]{1,0:T(8,128)(2,1)} %get-tuple-element.27.refs_3_.refs_2_), channel_id=1, source_target_pairs={{1,0},{5,4},{9,8},{13,12},{17,16},{21,20},{25,24},{29,28}} | collective-permute-start | bytes 4718600 | tf_op jit(solution)/shard_map/ppermute | solution.py:475
  94.9 40.3 %collective-permute-start.10 = (bf16[768,1152]{1,0:T(8,128)(2,1)}, bf16[768,1152]{1,0:T(8,128)(2,1)S(1)}, u32[]{:S(2)}, u32[]{:S(2)}) collective-permute-start(bf16[768,1152]{1,0:T(8,128)(2,1)} %get-tuple-element.28.refs_3_), channel_id=1, source_target_pairs={{0,16},{4,20},{8,24},{12,28},{16,0},{20,4},{24,8},{28,12},{1,17},{... | collective-permute-start | bytes 5308424 | tf_op jit(solution)/shard_map/ppermute | solution.py:100
  96.5 39.9 %collective-permute-start.11 = (bf16[768,1152]{1,0:T(8,128)(2,1)}, bf16[768,1152]{1,0:T(8,128)(2,1)S(1)}, u32[]{:S(2)}, u32[]{:S(2)}) collective-permute-start(bf16[768,1152]{1,0:T(8,128)(2,1)} %get-tuple-element.29.refs_6_), channel_id=1, source_target_pairs={{0,8},{4,12},{8,0},{12,4},{16,24},{20,28},{24,16},{28,20},{1,9},{5... | collective-permute-start | bytes 5308424 | tf_op jit(solution)/shard_map/ppermute | solution.py:100
  107.4 24.0 %copy-start.1 = (f32[6144]{0:T(1024)S(1)}, f32[6144]{0:T(1024)}, u32[]{:S(2)}) copy-start(f32[6144]{0:T(1024)} %param.11) | copy-start | bytes 73732
  131.5 5.5 %copy-start.3 = (f32[64]{0:T(128)S(1)}, f32[64]{0:T(128)}, u32[]{:S(2)}) copy-start(f32[64]{0:T(128)} %copy-done.2) | copy-start | bytes 772
  131.5 5.5 %copy-start.4 = (f32[128]{0:T(128)S(1)}, f32[128]{0:T(128)}, u32[]{:S(2)}) copy-start(f32[128]{0:T(128)} %param.15) | copy-start | bytes 1540
  131.5 5.5 %copy-start.5 = (f32[128]{0:T(128)S(1)}, f32[128]{0:T(128)}, u32[]{:S(2)}) copy-start(f32[128]{0:T(128)} %param.16) | copy-start | bytes 1540
  133.4 3.5 %collective-permute-start.12 = (bf16[1,1,512,1536]{3,2,1,0:T(8,128)(2,1)S(1)}, bf16[1,1,512,1536]{3,2,1,0:T(8,128)(2,1)S(1)}, u32[]{:S(2)}, u32[]{:S(2)}) collective-permute-start(bf16[1,1,512,1536]{3,2,1,0:T(8,128)(2,1)S(1)} %shard_map.98.last_ref), channel_id=1, source_target_pairs={{0,4},{4,0},{8,12},{12,8},{16,20},{20,16},{24,28},{28,24},{1,5},{5... | collective-permute-start | bytes 4718600 | tf_op jit(solution)/shard_map/ppermute | solution.py:100
  142.7 5.9 %collective-permute-start.13 = (bf16[512,384]{1,0:T(8,128)(2,1)S(1)}, bf16[512,384]{1,0:T(8,128)(2,1)S(1)}, u32[]{:S(2)}, u32[]{:S(2)}) collective-permute-start(bf16[512,384]{1,0:T(8,128)(2,1)S(1)} %shard_map.99.refs_0_), channel_id=1, source_target_pairs={{0,4},{4,0},{8,12},{12,8},{16,20},{20,16},{24,28},{28,24},{1,5},{5... | collective-permute-start | bytes 1179656 | tf_op jit(solution)/shard_map/ppermute | solution.py:100

commit v4 on v3

--- a/solution.py
+++ b/solution.py
@@ -69,17 +69,20 @@
 CORE, X, Y = 1, 2, 4
 
 PLACES = ((0, 1, 2, 3), (1, 0, 2, 3), (2, 3, 1, 0), (3, 2, 1, 0))
-
-
-def arrival(z, place):
-    return z - place if place <= z else 3 + place - z
+OWN, PARTNER, MIDDLE, OUTWARD, MIDDLE_AGAIN, OUTWARD_AGAIN = range(6)
+AT_ENDS = (OWN, PARTNER, OUTWARD, OUTWARD_AGAIN)
+IN_MIDDLE = (OWN, PARTNER, MIDDLE, MIDDLE_AGAIN)
+ARRIVALS = (AT_ENDS, IN_MIDDLE, IN_MIDDLE, AT_ENDS)
+TO_PARTNER = ((0, 1), (1, 0), (2, 3), (3, 2))
+TO_MIDDLE = ((1, 2), (2, 1))
+TO_OUTSIDE = ((1, 0), (2, 3))
 
 
 def plan(z, chip):
     diagonal = chip ^ 3
     order = [place for place in PLACES[z] if place != diagonal] + [diagonal]
     pairs = [number for place in order for number in (PLACES[z].index(place), place ^ chip)]
-    return pairs + list(PLACES[z]) + [arrival(z, place) for place in PLACES[z]]
+    return pairs + list(PLACES[z]) + list(ARRIVALS[z])
 
 
 PLAN = [[plan(z, chip) for chip in range(4)] for z in range(4)]
@@ -126,51 +129,40 @@
     return [(first, min(first + 2 * DH, width)) for first in range(0, width, 2 * DH)]
 
 
-def pack_kernel(*refs):
-    weights, outs, (held, packed, in_sems, out_sems) = refs[:3], refs[3:5], refs[5:]
+def pack_kernel(theirs, *refs):
+    weights, out_ref, held, in_sems = refs[:3], *refs[-3:]
     core = lax.axis_index("dp") % 2
-    _, _, _, width = held.shape
+    width = held.shape[2]
     heads = width // DH
 
-    def load(number, kind):
-        first = pl.multiple_of((core if number == 0 else 1 - core) * width, DH)
+    def load(kind):
+        first = pl.multiple_of((1 - core if theirs else core) * width, DH)
         return pltpu.make_async_copy(
-            weights[kind].at[:, pl.ds(first, width)], held.at[number, kind], in_sems.at[number, kind]
+            weights[kind].at[:, pl.ds(first, width)], held.at[kind], in_sems.at[kind]
         )
 
-    def store(number):
-        return pltpu.make_async_copy(packed.at[number], outs[number], out_sems.at[number])
-
-    for number in range(2):
-        for kind in range(3):
-            load(number, kind).start()
-    for number in range(2):
-        for kind, firsts in enumerate(columns_of(heads)):
-            load(number, kind).wait()
-            for h, first in enumerate(firsts):
-                packed[number, :, first : first + DH] = held[number, kind, :, h * DH : (h + 1) * DH]
-        store(number).start()
-    for number in range(2):
-        store(number).wait()
-
-
-def pack(*weights):
+    for kind in range(3):
+        load(kind).start()
+    for kind, firsts in enumerate(columns_of(heads)):
+        load(kind).wait()
+        for h, first in enumerate(firsts):
+            out_ref[:, first : first + DH] = held[kind, :, h * DH : (h + 1) * DH]
+
+
+def pack(theirs, weights, *others):
     rows, columns = weights[0].shape
-    shape = (rows, 3 * columns // 2)
     return pl.pallas_call(
-        pack_kernel,
-        in_specs=[HBM] * 3,
-        out_specs=[HBM] * 2,
-        out_shape=[jax.ShapeDtypeStruct(shape, jnp.bfloat16)] * 2,
+        functools.partial(pack_kernel, theirs),
+        in_specs=[HBM] * 3 + [ANY] * len(others),
+        out_specs=VMEM,
+        out_shape=jax.ShapeDtypeStruct((rows, 3 * columns // 2), jnp.bfloat16),
         scratch_shapes=[
-            pltpu.VMEM((2, 3, rows, columns // 2), jnp.bfloat16),
-            pltpu.VMEM((2, *shape), jnp.bfloat16),
-            pltpu.SemaphoreType.DMA((2, 3)),
-            pltpu.SemaphoreType.DMA((2,)),
+            pltpu.VMEM((3, rows, columns // 2), jnp.bfloat16),
+            pltpu.SemaphoreType.DMA((3,)),
         ],
         compiler_params=params(56),
         cost_estimate=FREE,
-    )(*weights)
+    )(*weights, *others)
 
 
 def fetch(chosen, choices, target, sem):
@@ -378,13 +370,68 @@
     return (both[:, :DH] / both[:, DH:]).astype(jnp.bfloat16)
 
 
+def place(plan_ref, side, next_tokens, last_ref, near_tokens=None, diag_tokens=None):
+    core = plan_ref[CORE_AT]
+    tiles = last_ref.shape[2] // TPD
+
+    def copy(near, diag):
+        if near_tokens is not None:
+            near_tokens[...] = near(slice(None))
+        if diag_tokens is not None:
+            depth = diag_tokens.shape[2]
+            for part in range(2):
+                first = pl.multiple_of((core if part == 0 else 1 - core) * depth, depth)
+                diag_tokens[part] = diag(pl.ds(first, depth))
+
+    def last(features):
+        return last_ref[0, 0, :, features]
+
+    def early(features):
+        chunk = next_tokens[side * tiles : (side + 1) * tiles, :, features]
+        return chunk.reshape(tiles * TPD, chunk.shape[2])
+
+    @pl.when(plan_ref[4] == 3)
+    def _():
+        copy(last, early)
+
+    @pl.when(plan_ref[4] != 3)
+    def _():
+        copy(early, last)
+
+
+def near_kernel(side, plan_ref, total_ref, next_tokens, next_weights, last_ref, *refs):
+    out_ref, near_tokens = refs[-2:]
+    place(plan_ref, side, next_tokens, last_ref, near_tokens=near_tokens)
+    tiles, _, width = out_ref.shape
+    for tile in range(tiles):
+        rows = near_tokens[tile * TPD : (tile + 1) * TPD, :]
+        for first, end in column_groups(width):
+            out_ref[tile, :, first:end] = total_ref[side * tiles + tile, :, first:end] + jnp.dot(
+                rows, next_weights[:, first:end], preferred_element_type=jnp.float32
+            )
+
+
+def add_near(side, plan_here, total, next_tokens, next_weights, last):
+    tiles, _, width = total.shape
+    _, _, rows, features = last.shape
+    return pl.pallas_call(
+        functools.partial(near_kernel, side),
+        in_specs=[SMEM] + [VMEM] * 4,
+        out_specs=VMEM,
+        out_shape=jax.ShapeDtypeStruct((tiles // 2, TPD, width), jnp.float32),
+        scratch_shapes=[pltpu.VMEM((rows, features), jnp.bfloat16)],
+        compiler_params=params(18),
+        cost_estimate=FREE,
+    )(plan_here, total, next_tokens, next_weights, last)
+
+
 def finish_kernel(
     side,
+    first_tile,
     plan_ref,
     mask_ref,
     total_ref,
     next_tokens,
-    next_weights,
     last_ref,
     diag_same,
     diag_cross,
@@ -396,68 +443,45 @@
     core = plan_ref[CORE_AT]
     width = total_ref.shape[2]
     heads = width // (3 * DH)
-    tiles = near_tokens.shape[0]
-    depth = diag_same.shape[0]
-
-    def place(tile, near, diag):
-        near_tokens[tile] = near(slice(None))
-        for part in range(2):
-            first = pl.multiple_of((core if part == 0 else 1 - core) * depth, depth)
-            diag_tokens[part, tile] = diag(pl.ds(first, depth))
-
-    for tile in range(tiles):
-
-        def last(features, tile=tile):
-            return last_ref[0, 0, pl.ds(tile * TPD, TPD), features]
-
-        def early(features, tile=tile):
-            return next_tokens[side * tiles + tile, :, features]
-
-        @pl.when(plan_ref[4] == 3)
-        def _():
-            place(tile, last, early)
-
-        @pl.when(plan_ref[4] != 3)
-        def _():
-            place(tile, early, last)
-
+    tiles = last_ref.shape[2] // TPD
+    near = near_tokens.shape[0] > TPD
+    place(plan_ref, side, next_tokens, last_ref, near_tokens if near else None, diag_tokens)
     query_first, key_first, value_first = columns_of(heads)
     for tile in range(tiles):
         sums = []
+        at = slice(tile * TPD, (tile + 1) * TPD)
+        pairs = [(diag_tokens[0, at], diag_same), (diag_tokens[1, at], diag_cross)]
+        if near:
+            pairs.append((near_tokens[at, :], refs[0]))
         for first, end in column_groups(width):
-            part = total_ref[side * tiles + tile, :, first:end]
-            for tokens, weights in (
-                (near_tokens[tile], next_weights),
-                (diag_tokens[0, tile], diag_same),
-                (diag_tokens[1, tile], diag_cross),
-            ):
+            part = total_ref[first_tile + tile, :, first:end]
+            for tokens, weights in pairs:
                 part = part + jnp.dot(tokens, weights[:, first:end], preferred_element_type=jnp.float32)
-            sums += [part[:, at : at + DH] for at in range(0, end - first, DH)]
+            sums += [part[:, column : column + DH] for column in range(0, end - first, DH)]
         whose = core if side == 0 else 1 - core
         for h in range(heads):
             query = head_norm(sums[query_first[h] // DH], query_gain[...]).astype(jnp.bfloat16)
             key = head_norm(sums[key_first[h] // DH], key_gain[...]).astype(jnp.bfloat16)
             value = sums[value_first[h] // DH].astype(jnp.bfloat16)
-            out_ref[pl.ds(tile * TPD, TPD), h * DH : (h + 1) * DH] = attend(
-                query, key, value, mask_ref, whose * tiles + tile
-            )
-
-
-def finish(side, plan_here, mask, total, next_tokens, next_weights, last, diag, query_gain, key_gain, *others):
-    tiles, _, width = total.shape
-    depth = diag[0].shape[0]
+            out_ref[at, h * DH : (h + 1) * DH] = attend(query, key, value, mask_ref, whose * tiles + tile)
+
+
+def finish(side, plan_here, mask, total, next_tokens, last, diag, gains, next_weights=None, others=()):
+    width = total.shape[2]
+    _, _, rows, features = last.shape
+    near = next_weights is not None
     return pl.pallas_call(
-        functools.partial(finish_kernel, side),
-        in_specs=[SMEM] * 2 + [VMEM] * 8 + [ANY] * len(others),
+        functools.partial(finish_kernel, side, side * rows // TPD if near else 0),
+        in_specs=[SMEM] * 2 + [VMEM] * (8 if near else 7) + [ANY] * len(others),
         out_specs=VMEM,
-        out_shape=jax.ShapeDtypeStruct((tiles // 2 * TPD, width // 3), jnp.bfloat16),
+        out_shape=jax.ShapeDtypeStruct((rows, width // 3), jnp.bfloat16),
         scratch_shapes=[
-            pltpu.VMEM((tiles // 2, TPD, 2 * depth), jnp.bfloat16),
-            pltpu.VMEM((2, tiles // 2, TPD, depth), jnp.bfloat16),
+            pltpu.VMEM((rows if near else 16, features), jnp.bfloat16),
+            pltpu.VMEM((2, rows, diag[0].shape[0]), jnp.bfloat16),
         ],
         compiler_params=params(18),
         cost_estimate=FREE,
-    )(plan_here, mask, total, next_tokens, next_weights, last, *diag, query_gain, key_gain, *others)
+    )(plan_here, mask, total, next_tokens, last, *diag, *gains, *([next_weights] if near else []), *others)
 
 
 def per_device_8x4(tokens, block_mask, norm_gain, w_query, w_key, w_value, query_gain, key_gain):
@@ -468,17 +492,15 @@
     plan_here = jnp.asarray(PLAN, jnp.int32)[z, dp // 2]
     plan_here = jnp.concatenate([plan_here, core[None]])
 
-    def up(array, first):
-        return lax.ppermute(array, "tensor", [(i, i + 1) for i in range(first, 3)])
-
-    def down(array, last):
-        return lax.ppermute(array, "tensor", [(i + 1, i) for i in range(last)])
-
-    mine, other = pack(w_query, w_key, w_value)
-    x_same, y_cross = swap(mine, X), swap(other, Y | CORE)
-    up1, down1 = up(tokens, 0), down(tokens, 3)
+    def along(array, pairs):
+        return lax.ppermute(array, "tensor", pairs)
+
+    mine = pack(False, (w_query, w_key, w_value))
+    x_same, y_same = swap(mine, X), swap(mine, Y)
+    partner, middle = along(tokens, TO_PARTNER), along(tokens, TO_MIDDLE)
     values = tokens.astype(jnp.float32)
     stats = jnp.stack([jnp.sum(values, axis=1), jnp.sum(values * values, axis=1)])
+    other = pack(True, (w_query, w_key, w_value), mine)
     own = trade(jnp.where(core == 0, jnp.stack([mine, other]), jnp.stack([other, mine])))
     mask = block_mask.astype(jnp.float32).reshape(1, -1)
     mask = trade(jnp.concatenate([mask, mask])).reshape(-1)
@@ -486,28 +508,32 @@
     stats = lax.all_to_all(jnp.stack([stats] * 4), "tensor", 0, 0)
     gains = norm_gain.reshape(1, -1)
 
-    mine, other, up1, down1, stats = gate((mine, other, up1, down1, stats), (x_same, y_cross))
-    x_cross, y_same = swap(other, X | CORE), swap(mine, Y)
-    up2, down2 = up(up1, 1), down(down1, 2)
-
-    arrived = {0: tokens, 1: up1, 4: down1}
+    other, partner, middle, stats = gate((other, partner, middle, stats), (x_same, y_same))
+    x_cross, y_cross = swap(other, X | CORE), swap(other, Y | CORE)
+    outward, middle_again = along(middle, TO_OUTSIDE), along(partner, TO_MIDDLE)
+
+    arrived = {OWN: tokens, PARTNER: partner}
     normed = [trade(norm(plan_here, (0, 1), 2, stats, gains, arrived))]
 
-    x_same, y_cross, up2, down2 = gate((x_same, y_cross, up2, down2), (x_cross, y_same, normed[0]))
+    x_same, y_cross, outward, middle_again = gate(
+        (x_same, y_cross, outward, middle_again), (x_cross, normed[0])
+    )
     diag_same, diag_cross = swap(x_same, Y), swap(y_cross, X)
-    up3, down3 = up(up2, 2), down(down2, 1)
-    arrived = {1: up1, 2: up2, 4: down1, 5: down2}
+    outward_again = along(middle_again, TO_OUTSIDE)
+    arrived = {MIDDLE: middle, OUTWARD: outward}
     normed.append(trade(norm(plan_here, (2,), 2, stats, gains, arrived)))
     near = [own, x_same, x_cross, y_same, y_cross]
     total, next_tokens, next_weights = project(plan_here, normed, near)
 
-    arrived = {2: up2, 3: up3, 5: down2, 6: down3}
+    arrived = {MIDDLE_AGAIN: middle_again, OUTWARD_AGAIN: outward_again}
     last = norm(plan_here, (3,), 1, stats, gains, arrived, total)
     diag = (diag_same, diag_cross)
     gain_pair = (query_gain[None, :], key_gain[None, :])
-    early = (plan_here, mask, total, next_tokens, next_weights)
-    theirs = finish(1, *early, swap(last, CORE), diag, *gain_pair)
-    here = finish(0, *early, last, diag, *gain_pair, theirs)
+    last_there = swap(last, CORE)
+    total_here = add_near(0, plan_here, total, next_tokens, next_weights, last)
+    (last_there,) = gate((last_there,), (total_here,))
+    theirs = finish(1, plan_here, mask, total, next_tokens, last_there, diag, gain_pair, next_weights)
+    here = finish(0, plan_here, mask, total_here, next_tokens, last, diag, gain_pair, others=(theirs,))
     there = swap(theirs, CORE)
     return jnp.where(
         core == 0,

time: 150 us -> 144 us (0.960)
  waiting for transfers between devices: 39.9 us -> 35.6 us
  Pallas kernels: 38.2 us -> 41.1 us
  starting transfers between devices: 27.1 us -> 24.8 us
    ppermute x8, waiting for transfers between devices: 3.41 us -> 0.44 us  [swap(): return lax.ppermute(array, 'dp', [(i, i ^ bits) for i in range(8)])]
    pallas_call x3 -> x5, Pallas kernels: 14.9 us -> 17.8 us  [the longest x2 9.18 us: finish(): pl.pallas_call(functools.partial(finish_kernel, side, side * rows // TPD...]
    ppermute x6 -> x5, starting transfers between devices: 12.1 us -> 9.49 us  [along(): return lax.ppermute(array, 'tensor', pairs)]
    ppermute x6 -> x5, waiting for transfers between devices: 35.9 us -> 34.5 us  [along(): return lax.ppermute(array, 'tensor', pairs)]
  transfers between devices with their start and end apart: 16 -> 15, of which waited for: 6 -> 4; matrix products, arithmetic and copies ran while one was open for 6% -> 6% of each run, Pallas kernels for 19% -> 23%
where the time goes in v4:
time: 144 us
  Pallas kernels  41.1 us (29%)
  waiting for transfers between devices  35.6 us (25%)
  blocking collectives  31.3 us (22%)
  starting transfers between devices  24.8 us (17%)
  other arithmetic  8.33 us (6%)
  local copies, waits for them, and re-layouts  2.38 us (2%)
    ppermute x5, waiting for transfers between devices, along(): return lax.ppermute(array, 'tensor', pairs)  34.5 us
    all_to_all x1, blocking collectives, per_device_8x4(): stats = lax.all_to_all(jnp.stack([stats] * 4), 'tensor', 0, 0)  16.3 us
    all_to_all x2, blocking collectives, trade(): lax.all_to_all(array, 'dp', 0, 0, axis_index_groups=[[i, i + 1] for i in...  15 us
    pallas_call x1, Pallas kernels, project(): pl.pallas_call(functools.partial(project_kernel, tokens), in_specs=[SMEM]...  13.7 us
    pallas_call x3, Pallas kernels, norm(): pl.pallas_call(functools.partial(norm_kernel, slots, tuple(arrays)), in_s...  9.61 us
    ppermute x5, starting transfers between devices, along(): return lax.ppermute(array, 'tensor', pairs)  9.49 us
    pallas_call x2, Pallas kernels, finish(): pl.pallas_call(functools.partial(finish_kernel, side, side * rows // TPD...  9.18 us
    ppermute x8, starting transfers between devices, swap(): return lax.ppermute(array, 'dp', [(i, i ^ bits) for i in range(8)])  8.06 us
  transfers between devices with their start and end apart: 15, of which 4 were waited for; matrix products, arithmetic and copies ran while one was open for 6% of the time, Pallas kernels for 23%

profile of v4, /device:TPU:0, one launch (start us, length us, event | category | flops | bytes accessed | tf_op | source)
XLA Modules:
  0.0 143.7 jit_solution(11733214488387518335)
XLA Ops:
  0.0 2.7 %shard_map.91.refs_3_ = bf16[768,1152]{1,0:T(8,128)(2,1)} custom-call(bf16[768,768]{1,0:T(8,128)(2,1)} %refs_0_.4, bf16[768,768]{1,0:T(8,128)(2,1)} %refs_1_.3, bf16[768,768]{1,0:T(8,128)(2,1)} %refs_2_.3), custom_call_target="tpu_custom_call" | custom-call | tf_op jit(solution)/shard_map/pallas_call | solution.py:154
  2.8 3.0 %collective-permute-start.3 = (bf16[768,1152]{1,0:T(8,128)(2,1)}, bf16[768,1152]{1,0:T(8,128)(2,1)}, u32[]{:S(2)}, u32[]{:S(2)}) collective-permute-start(bf16[768,1152]{1,0:T(8,128)(2,1)} %shard_map.91.refs_3_), channel_id=1, source_target_pairs={{0,16},{4,20},{8,24},{12,28},{16,0},{20,4},{24,8},{28,12},{1,17},{... | collective-permute-start | bytes 5308424 | tf_op jit(solution)/shard_map/ppermute | solution.py:103
  5.8 1.5 %collective-permute-start.2 = (bf16[768,1152]{1,0:T(8,128)(2,1)}, bf16[768,1152]{1,0:T(8,128)(2,1)}, u32[]{:S(2)}, u32[]{:S(2)}) collective-permute-start(bf16[768,1152]{1,0:T(8,128)(2,1)} %shard_map.91.refs_3_), channel_id=1, source_target_pairs={{0,8},{4,12},{8,0},{12,4},{16,24},{20,28},{24,16},{28,20},{1,9},{5... | collective-permute-start | bytes 5308424 | tf_op jit(solution)/shard_map/ppermute | solution.py:103
  7.3 1.8 %collective-permute-start.1 = (bf16[512,1536]{1,0:T(8,128)(2,1)}, bf16[512,1536]{1,0:T(8,128)(2,1)}, u32[]{:S(2)}, u32[]{:S(2)}) collective-permute-start(bf16[512,1536]{1,0:T(8,128)(2,1)} %refs_0_.5), channel_id=1, source_target_pairs={{1,2},{2,1},{5,6},{6,5},{9,10},{10,9},{13,14},{14,13},{17,18},{18,... | collective-permute-start | bytes 4718600 | tf_op jit(solution)/shard_map/ppermute | solution.py:496
  9.1 3.3 %collective-permute-start = (bf16[512,1536]{1,0:T(8,128)(2,1)}, bf16[512,1536]{1,0:T(8,128)(2,1)}, u32[]{:S(2)}, u32[]{:S(2)}) collective-permute-start(bf16[512,1536]{1,0:T(8,128)(2,1)} %refs_0_.5), channel_id=1, source_target_pairs={{0,1},{1,0},{2,3},{3,2},{4,5},{5,4},{6,7},{7,6},{8,9},{9,8},{10,11... | collective-permute-start | bytes 4718600 | tf_op jit(solution)/shard_map/ppermute | solution.py:496
  13.1 3.2 %all-to-all-start = ((f32[2,1,32]{2,1,0:T(1,128)}), f32[2,1,32]{2,1,0:T(1,128)S(1)}, u32[]{:S(2)}, u32[]{:S(2)}) async-start(f32[2,1,32]{2,1,0:T(1,128)} %bitcast.3), calls=%async_computation | async-start | bytes 2048 | tf_op jit(solution)/shard_map/all_to_all | solution.py:107
  16.3 2.9 %shard_map.92.refs_0_ = bf16[768,1152]{1,0:T(8,128)(2,1)} custom-call(bf16[768,768]{1,0:T(8,128)(2,1)} %refs_0_.4, bf16[768,768]{1,0:T(8,128)(2,1)} %refs_1_.3, bf16[768,768]{1,0:T(8,128)(2,1)} %refs_2_.3, bf16[768,1152]{1,0:T(8,128)(2,1)} %shard_map.91.refs_3_), custom_call_target="tpu_custom_call" | custom-call | tf_op jit(solution)/shard_map/pallas_call | solution.py:154
  19.3 3.9 %maximum_select_fusion = bf16[2,768,1152]{2,1,0:T(8,128)(2,1)} fusion(bf16[1,768,1152]{2,1,0:T(8,128)(2,1)} %bitcast.7, bf16[1,768,1152]{2,1,0:T(8,128)(2,1)S(1)} %bitcast.20, pred[]{:T(512)S(6)} %eq.6), kind=kLoop, calls=%fused_computation.2 | loop fusion | flops 5308416 | bytes 7077889 | tf_op jit(solution)/shard_map/jit(_where)/select_n | solution.py:504
  23.2 4.0 %all-to-all-start.1 = ((bf16[2,768,1152]{2,1,0:T(8,128)(2,1)}), bf16[2,768,1152]{2,1,0:T(8,128)(2,1)S(1)}, u32[]{:S(2)}, u32[]{:S(2)}) async-start(bf16[2,768,1152]{2,1,0:T(8,128)(2,1)} %maximum_select_fusion), calls=%async_computation.1 | async-start | bytes 7077888 | tf_op jit(solution)/shard_map/all_to_all | solution.py:107
  27.8 0.7 reduce.3
  28.5 2.0 %convert_reduce_fusion = (f32[512]{0:T(512)S(1)}, f32[512]{0:T(512)S(1)}) fusion(bf16[512,1536]{1,0:T(8,128)(2,1)} %refs_0_.5), kind=kLoop, calls=%fused_computation.1 | loop fusion | flops 3144704 | bytes 1576960 | tf_op jit(solution)/shard_map/reduce_sum | solution.py:502
  31.1 16.3 %all_to_all.29.refs_3_ = f32[4,2,512]{2,1,0:T(2,128)S(1)} all-to-all(f32[4,2,512]{2,1,0:T(2,128)S(1)} %stack.37), channel_id=1, replica_groups=mesh['dp'=8,'tensor'=4] {'tensor'}, dimensions={0} | all-to-all | bytes 32768 | tf_op jit(solution)/shard_map/all_to_all | solution.py:508
  47.5 0.7 collective-permute-start.4
  48.3 1.8 %collective-permute-start.6 = (bf16[512,1536]{1,0:T(8,128)(2,1)}, bf16[512,1536]{1,0:T(8,128)(2,1)}, u32[]{:S(2)}, u32[]{:S(2)}) collective-permute-start(bf16[512,1536]{1,0:T(8,128)(2,1)} %get-tuple-element.17.refs_1_), channel_id=1, source_target_pairs={{1,2},{2,1},{5,6},{6,5},{9,10},{10,9},{13,14},{14,13},{17,18},{18,... | collective-permute-start | bytes 4718600 | tf_op jit(solution)/shard_map/ppermute | solution.py:496
  50.1 1.3 collective-permute-start.5
  51.4 0.7 dynamic-slice_bitcast_fusion
  52.2 0.7 copy-done
  52.9 4.5 %shard_map.95 = bf16[2,2,512,1536]{3,2,1,0:T(8,128)(2,1)S(1)} custom-call(s32[17]{0:T(128)S(1)} %pad_add_fusion.plan_ref, f32[4,2,512]{2,1,0:T(2,128)S(1)} %get-tuple-element.16.stats_ref, f32[1,6144]{1,0:T(1,128)S(1)} %bitcast.13, bf16[512,1536]{1,0:T(8,128)(2,1)} %refs_0_.5, bf16[512,1536]{1,0:T(8,128)(2,1)} %get-tuple-element.17.refs_1_), custom_call_target="tpu_custom_call" | custom-call | tf_op jit(solution)/shard_map/pallas_call | solution.py:207
  57.4 8.8 %all_to_all.30.refs_5_.refs_0_ = bf16[2,2,512,1536]{3,2,1,0:T(8,128)(2,1)S(1)} all-to-all(bf16[2,2,512,1536]{3,2,1,0:T(8,128)(2,1)S(1)} %shard_map.95), channel_id=1, replica_groups={{0,4},{8,12},{16,20},{24,28},{1,5},{9,13},{17,21},{25,29},{2,6},{10,14}..., dimensions={0} | all-to-all | bytes 12582912 | tf_op jit(solution)/shard_map/all_to_all | solution.py:107
  66.2 22.6 %collective-permute-done.5.refs_2_ = bf16[512,1536]{1,0:T(8,128)(2,1)} collective-permute-done((bf16[512,1536]{1,0:T(8,128)(2,1)}, bf16[512,1536]{1,0:T(8,128)(2,1)}, u32[]{:S(2)}, u32[]{:S(2)}) %collective-permute-start.5) | collective-permute-done | bytes 1572896 | tf_op jit(solution)/shard_map/ppermute | solution.py:496
  88.7 1.3 collective-permute-start.8
  90.0 1.4 collective-permute-start.9
  91.4 0.7 collective-permute-start.10
  92.1 3.2 %shard_map.97 = bf16[2,1,512,1536]{3,2,1,0:T(8,128)(2,1)S(1)} custom-call(s32[17]{0:T(128)S(1)} %pad_add_fusion.plan_ref, f32[4,2,512]{2,1,0:T(2,128)S(1)} %get-tuple-element.16.stats_ref, f32[1,6144]{1,0:T(1,128)S(1)} %bitcast.14, bf16[512,1536]{1,0:T(8,128)(2,1)} %get-tuple-element.18.refs_0_, bf16[512,1536]{1,0:T(8,128)(2,1)} %get-tuple-element.20.refs_1_), custom_call_target="tpu_custom_call" | custom-call | tf_op jit(solution)/shard_map/pallas_call | solution.py:207
  95.3 6.3 %all_to_all.31.refs_1_ = bf16[2,1,512,1536]{3,2,1,0:T(8,128)(2,1)S(1)} all-to-all(bf16[2,1,512,1536]{3,2,1,0:T(8,128)(2,1)S(1)} %shard_map.97), channel_id=1, replica_groups={{0,4},{8,12},{16,20},{24,28},{1,5},{9,13},{17,21},{25,29},{2,6},{10,14}..., dimensions={0} | all-to-all | bytes 6291456 | tf_op jit(solution)/shard_map/all_to_all | solution.py:107
  101.6 13.7 %shard_map.98 = (f32[4,256,1152]{2,1,0:T(8,128)S(1)}, bf16[4,256,1536]{2,1,0:T(8,128)(2,1)S(1)}, bf16[1536,1152]{1,0:T(8,128)(2,1)S(1)}) custom-call(s32[17]{0:T(128)S(1)} %pad_add_fusion.plan_ref, bf16[2,2,512,1536]{3,2,1,0:T(8,128)(2,1)S(1)} %all_to_all.30.refs_5_.refs_0_, bf16[2,1,512,1536]{3,2,1,0:T(8,128)(2,1)S(1)} %all_to_all.31.refs_1_, ...), custom_call_target="tpu_custom_call" | custom-call | tf_op jit(solution)/shard_map/pallas_call | solution.py:330
  115.3 11.9 %collective-permute-done.8.refs_1_ = bf16[512,1536]{1,0:T(8,128)(2,1)S(1)} collective-permute-done((bf16[512,1536]{1,0:T(8,128)(2,1)}, bf16[512,1536]{1,0:T(8,128)(2,1)S(1)}, u32[]{:S(2)}, u32[]{:S(2)}) %collective-permute-start.8) | collective-permute-done | bytes 1572896 | tf_op jit(solution)/shard_map/ppermute | solution.py:496
  127.2 1.9 %shard_map.99.last_ref = bf16[1,1,512,1536]{3,2,1,0:T(8,128)(2,1)S(1)} custom-call(s32[17]{0:T(128)S(1)} %pad_add_fusion.plan_ref, f32[4,2,512]{2,1,0:T(2,128)S(1)} %get-tuple-element.16.stats_ref, f32[1,6144]{1,0:T(1,128)S(1)} %bitcast.15, bf16[512,1536]{1,0:T(8,128)(2,1)} %get-tuple-element.26.refs_0_, ...), custom_call_target="tpu_custom_call" | custom-call | tf_op jit(solution)/shard_map/pallas_call | solution.py:207
  129.3 2.9 %shard_map.100.refs_1_.total_ref = f32[2,256,1152]{2,1,0:T(8,128)S(1)} custom-call(s32[17]{0:T(128)S(1)} %pad_add_fusion.plan_ref, f32[4,256,1152]{2,1,0:T(8,128)S(1)} %get-tuple-element.23.refs_2_.total_ref, bf16[4,256,1536]{2,1,0:T(8,128)(2,1)S(1)} %get-tuple-element.24.next_tokens, bf16[1536,1152]{1,0:T(8,128)(2,1)S(1)} %get-tuple-element.25.next_weights.refs_0_, ...), custom_call_target="tpu_custom_call" | custom-call | tf_op jit(solution)/shard_map/pallas_call | solution.py:417
  132.9 5.7 %shard_map.102.refs_0_ = bf16[512,384]{1,0:T(8,128)(2,1)S(1)} custom-call(s32[17]{0:T(128)S(1)} %pad_add_fusion.plan_ref, f32[64]{0:T(128)S(1)} %copy-done.3, f32[4,256,1152]{2,1,0:T(8,128)S(1)} %get-tuple-element.23.refs_2_.total_ref, bf16[4,256,1536]{2,1,0:T(8,128)(2,1)S(1)} %get-tuple-element.24.next_tokens, ...), custom_call_target="tpu_custom_call" | custom-call | tf_op jit(solution)/shard_map/pallas_call | solution.py:473
  139.1 3.5 %shard_map.103 = bf16[512,384]{1,0:T(8,128)(2,1)S(1)} custom-call(s32[17]{0:T(128)S(1)} %pad_add_fusion.plan_ref, f32[64]{0:T(128)S(1)} %copy-done.3, f32[2,256,1152]{2,1,0:T(8,128)S(1)} %shard_map.100.refs_1_.total_ref, bf16[4,256,1536]{2,1,0:T(8,128)(2,1)S(1)} %get-tuple-element.24.next_tokens, bf16[1,1,512,1536]{3,2,1,0:T(8,128)(2,1)S(1)} %shard_map.99.last_ref, ...), custom_call_target="tpu_custom_call" | custom-call | tf_op jit(solution)/shard_map/pallas_call | solution.py:473
  142.7 1.1 maximum_select_fusion.1
  (43 shorter events, 3.4 us)
Async XLA Ops:
  0.0 12.4 %copy-start.7 = (s32[2,4,4]{2,1,0:T(4,128)S(1)}, s32[2,4,4]{2,1,0:T(4,128)}, u32[]{:S(2)}) copy-start(s32[2,4,4]{2,1,0:T(4,128)} %param.10) | copy-start | bytes 388
  2.8 44.7 %collective-permute-start.3 = (bf16[768,1152]{1,0:T(8,128)(2,1)}, bf16[768,1152]{1,0:T(8,128)(2,1)}, u32[]{:S(2)}, u32[]{:S(2)}) collective-permute-start(bf16[768,1152]{1,0:T(8,128)(2,1)} %shard_map.91.refs_3_), channel_id=1, source_target_pairs={{0,16},{4,20},{8,24},{12,28},{16,0},{20,4},{24,8},{28,12},{1,17},{... | collective-permute-start | bytes 5308424 | tf_op jit(solution)/shard_map/ppermute | solution.py:103
  5.8 41.6 %collective-permute-start.2 = (bf16[768,1152]{1,0:T(8,128)(2,1)}, bf16[768,1152]{1,0:T(8,128)(2,1)}, u32[]{:S(2)}, u32[]{:S(2)}) collective-permute-start(bf16[768,1152]{1,0:T(8,128)(2,1)} %shard_map.91.refs_3_), channel_id=1, source_target_pairs={{0,8},{4,12},{8,0},{12,4},{16,24},{20,28},{24,16},{28,20},{1,9},{5... | collective-permute-start | bytes 5308424 | tf_op jit(solution)/shard_map/ppermute | solution.py:103
  7.3 40.1 %collective-permute-start.1 = (bf16[512,1536]{1,0:T(8,128)(2,1)}, bf16[512,1536]{1,0:T(8,128)(2,1)}, u32[]{:S(2)}, u32[]{:S(2)}) collective-permute-start(bf16[512,1536]{1,0:T(8,128)(2,1)} %refs_0_.5), channel_id=1, source_target_pairs={{1,2},{2,1},{5,6},{6,5},{9,10},{10,9},{13,14},{14,13},{17,18},{18,... | collective-permute-start | bytes 4718600 | tf_op jit(solution)/shard_map/ppermute | solution.py:496
  9.1 38.3 %collective-permute-start = (bf16[512,1536]{1,0:T(8,128)(2,1)}, bf16[512,1536]{1,0:T(8,128)(2,1)}, u32[]{:S(2)}, u32[]{:S(2)}) collective-permute-start(bf16[512,1536]{1,0:T(8,128)(2,1)} %refs_0_.5), channel_id=1, source_target_pairs={{0,1},{1,0},{2,3},{3,2},{4,5},{5,4},{6,7},{7,6},{8,9},{9,8},{10,11... | collective-permute-start | bytes 4718600 | tf_op jit(solution)/shard_map/ppermute | solution.py:496
  13.1 10.2 %all-to-all-start = ((f32[2,1,32]{2,1,0:T(1,128)}), f32[2,1,32]{2,1,0:T(1,128)S(1)}, u32[]{:S(2)}, u32[]{:S(2)}) async-start(f32[2,1,32]{2,1,0:T(1,128)} %bitcast.3), calls=%async_computation | async-start | bytes 2048 | tf_op jit(solution)/shard_map/all_to_all | solution.py:107
  16.3 3.0 %copy-start.6 = (bf16[768,1152]{1,0:T(8,128)(2,1)S(1)}, bf16[768,1152]{1,0:T(8,128)(2,1)}, u32[]{:S(2)}) copy-start(bf16[768,1152]{1,0:T(8,128)(2,1)} %shard_map.91.refs_3_) | copy-start | bytes 5308420
  23.2 7.9 %all-to-all-start.1 = ((bf16[2,768,1152]{2,1,0:T(8,128)(2,1)}), bf16[2,768,1152]{2,1,0:T(8,128)(2,1)S(1)}, u32[]{:S(2)}, u32[]{:S(2)}) async-start(bf16[2,768,1152]{2,1,0:T(8,128)(2,1)} %maximum_select_fusion), calls=%async_computation.1 | async-start | bytes 7077888 | tf_op jit(solution)/shard_map/all_to_all | solution.py:107
  28.5 2.6 %copy-start.2 = (f32[64]{0:T(128)}, f32[64]{0:T(128)S(1)}, u32[]{:S(2)}) copy-start(f32[64]{0:T(128)S(1)} %reshape.15.refs_2_.mask_ref) | copy-start | bytes 772
  47.4 41.3 %collective-permute-start.7 = (bf16[768,1152]{1,0:T(8,128)(2,1)}, bf16[768,1152]{1,0:T(8,128)(2,1)}, u32[]{:S(2)}, u32[]{:S(2)}) collective-permute-start(bf16[768,1152]{1,0:T(8,128)(2,1)} %get-tuple-element.19), channel_id=1, source_target_pairs={{0,12},{4,8},{8,4},{12,0},{16,28},{20,24},{24,20},{28,16},{1,13},{... | collective-permute-start | bytes 5308424 | tf_op jit(solution)/shard_map/ppermute | solution.py:103
  47.5 41.2 %collective-permute-start.4 = (bf16[768,1152]{1,0:T(8,128)(2,1)}, bf16[768,1152]{1,0:T(8,128)(2,1)}, u32[]{:S(2)}, u32[]{:S(2)}) collective-permute-start(bf16[768,1152]{1,0:T(8,128)(2,1)} %get-tuple-element.19), channel_id=1, source_target_pairs={{0,20},{4,16},{8,28},{12,24},{16,4},{20,0},{24,12},{28,8},{1,21},{... | collective-permute-start | bytes 5308424 | tf_op jit(solution)/shard_map/ppermute | solution.py:103
  48.3 17.9 %collective-permute-start.6 = (bf16[512,1536]{1,0:T(8,128)(2,1)}, bf16[512,1536]{1,0:T(8,128)(2,1)}, u32[]{:S(2)}, u32[]{:S(2)}) collective-permute-start(bf16[512,1536]{1,0:T(8,128)(2,1)} %get-tuple-element.17.refs_1_), channel_id=1, source_target_pairs={{1,2},{2,1},{5,6},{6,5},{9,10},{10,9},{13,14},{14,13},{17,18},{18,... | collective-permute-start | bytes 4718600 | tf_op jit(solution)/shard_map/ppermute | solution.py:496
  50.1 38.6 %collective-permute-start.5 = (bf16[512,1536]{1,0:T(8,128)(2,1)}, bf16[512,1536]{1,0:T(8,128)(2,1)}, u32[]{:S(2)}, u32[]{:S(2)}) collective-permute-start(bf16[512,1536]{1,0:T(8,128)(2,1)} %get-tuple-element.18.refs_0_), channel_id=1, source_target_pairs={{1,0},{2,3},{5,4},{6,7},{9,8},{10,11},{13,12},{14,15},{17,16},{18,... | collective-permute-start | bytes 4718600 | tf_op jit(solution)/shard_map/ppermute | solution.py:496
  52.2 0.7 copy-start
  88.7 38.5 %collective-permute-start.8 = (bf16[512,1536]{1,0:T(8,128)(2,1)}, bf16[512,1536]{1,0:T(8,128)(2,1)S(1)}, u32[]{:S(2)}, u32[]{:S(2)}) collective-permute-start(bf16[512,1536]{1,0:T(8,128)(2,1)} %get-tuple-element.26.refs_0_), channel_id=1, source_target_pairs={{1,0},{2,3},{5,4},{6,7},{9,8},{10,11},{13,12},{14,15},{17,16},{18,... | collective-permute-start | bytes 4718600 | tf_op jit(solution)/shard_map/ppermute | solution.py:496
  90.0 42.6 %collective-permute-start.9 = (bf16[768,1152]{1,0:T(8,128)(2,1)}, bf16[768,1152]{1,0:T(8,128)(2,1)S(1)}, u32[]{:S(2)}, u32[]{:S(2)}) collective-permute-start(bf16[768,1152]{1,0:T(8,128)(2,1)} %get-tuple-element.21.refs_3_), channel_id=1, source_target_pairs={{0,16},{4,20},{8,24},{12,28},{16,0},{20,4},{24,8},{28,12},{1,17},{... | collective-permute-start | bytes 5308424 | tf_op jit(solution)/shard_map/ppermute | solution.py:103
  91.4 41.3 %collective-permute-start.10 = (bf16[768,1152]{1,0:T(8,128)(2,1)}, bf16[768,1152]{1,0:T(8,128)(2,1)S(1)}, u32[]{:S(2)}, u32[]{:S(2)}) collective-permute-start(bf16[768,1152]{1,0:T(8,128)(2,1)} %get-tuple-element.22.refs_6_), channel_id=1, source_target_pairs={{0,8},{4,12},{8,0},{12,4},{16,24},{20,28},{24,16},{28,20},{1,9},{5... | collective-permute-start | bytes 5308424 | tf_op jit(solution)/shard_map/ppermute | solution.py:103
  101.6 25.6 %copy-start.1 = (f32[6144]{0:T(1024)S(1)}, f32[6144]{0:T(1024)}, u32[]{:S(2)}) copy-start(f32[6144]{0:T(1024)} %param.11) | copy-start | bytes 73732
  129.2 3.5 %collective-permute-start.11 = (bf16[1,1,512,1536]{3,2,1,0:T(8,128)(2,1)S(1)}, bf16[1,1,512,1536]{3,2,1,0:T(8,128)(2,1)S(1)}, u32[]{:S(2)}, u32[]{:S(2)}) collective-permute-start(bf16[1,1,512,1536]{3,2,1,0:T(8,128)(2,1)S(1)} %shard_map.99.last_ref), channel_id=1, source_target_pairs={{0,4},{4,0},{8,12},{12,8},{16,20},{20,16},{24,28},{28,24},{1,5},{5... | collective-permute-start | bytes 4718600 | tf_op jit(solution)/shard_map/ppermute | solution.py:103
  132.2 0.7 copy-start.3
  132.2 0.7 copy-start.4
  132.2 0.7 copy-start.5
  138.6 4.1 %collective-permute-start.12 = (bf16[512,384]{1,0:T(8,128)(2,1)S(1)}, bf16[512,384]{1,0:T(8,128)(2,1)S(1)}, u32[]{:S(2)}, u32[]{:S(2)}) collective-permute-start(bf16[512,384]{1,0:T(8,128)(2,1)S(1)} %shard_map.102.refs_0_), channel_id=1, source_target_pairs={{0,4},{4,0},{8,12},{12,8},{16,20},{20,16},{24,28},{28,24},{1,5},{5... | collective-permute-start | bytes 1179656 | tf_op jit(solution)/shard_map/ppermute | solution.py:103

commit v5 on v4

--- a/solution.py
+++ b/solution.py
@@ -175,9 +175,11 @@
 
 def norm_kernel(slots, numbers, plan_ref, stats_ref, gains_ref, *refs):
     arrays = dict(zip(numbers, refs))
-    out_ref, raw, normed, columns, in_sems, out_sems = refs[-6:]
+    out_ref, raw, scratch, columns, in_sems, out_sems = refs[-6:]
     _, rows, features = raw.shape
     step = 64
+    copies = out_ref.shape[0]
+    normed = out_ref.at[0] if copies == 1 else scratch
     for n, slot in enumerate(slots):
         fetch(plan_ref[ARRIVAL + slot], arrays, raw.at[n], in_sems.at[n])
     stats = jnp.sum(stats_ref[...], axis=0) / (4 * features)
@@ -194,10 +196,10 @@
             values = raw[n, at, :].astype(jnp.float32)
             normed[n, at, :] = ((values - columns[at, 0:1]) * columns[at, 1:2] * gain).astype(jnp.bfloat16)
 
-        for copy in range(out_ref.shape[0]):
+        for copy in range(copies if copies > 1 else 0):
             pltpu.make_async_copy(normed.at[n], out_ref.at[copy, n], out_sems.at[copy, n]).start()
     for n in range(len(slots)):
-        for copy in range(out_ref.shape[0]):
+        for copy in range(copies if copies > 1 else 0):
             pltpu.make_async_copy(normed.at[n], out_ref.at[copy, n], out_sems.at[copy, n]).wait()
 
 
@@ -207,11 +209,11 @@
     return pl.pallas_call(
         functools.partial(norm_kernel, slots, tuple(arrays)),
         in_specs=[SMEM] + [VMEM] * 2 + [ANY] * (len(arrays) + len(others)),
-        out_specs=HBM,
+        out_specs=VMEM if copies == 1 else HBM,
         out_shape=jax.ShapeDtypeStruct((copies, *shape), jnp.bfloat16),
         scratch_shapes=[
             pltpu.VMEM(shape, jnp.bfloat16),
-            pltpu.VMEM(shape, jnp.bfloat16),
+            pltpu.VMEM(shape if copies > 1 else (1, 16, 128), jnp.bfloat16),
             pltpu.VMEM((rows, 8), jnp.float32),
             pltpu.SemaphoreType.DMA((len(slots),)),
             pltpu.SemaphoreType.DMA((copies, len(slots))),

time: 144 us -> 144 us (level)
  no operation moved by 1% of the time
where the time goes in v5:
time: 144 us
  Pallas kernels  41 us (28%)
  waiting for transfers between devices  35.6 us (25%)
  blocking collectives  31.3 us (22%)
  starting transfers between devices  24.8 us (17%)
  other arithmetic  8.33 us (6%)
  local copies, waits for them, and re-layouts  2.38 us (2%)
    ppermute x5, waiting for transfers between devices, along(): return lax.ppermute(array, 'tensor', pairs)  34.5 us
    all_to_all x1, blocking collectives, per_device_8x4(): stats = lax.all_to_all(jnp.stack([stats] * 4), 'tensor', 0, 0)  16.3 us
    all_to_all x2, blocking collectives, trade(): lax.all_to_all(array, 'dp', 0, 0, axis_index_groups=[[i, i + 1] for i in...  15 us
    pallas_call x1, Pallas kernels, project(): pl.pallas_call(functools.partial(project_kernel, tokens), in_specs=[SMEM]...  13.7 us
    ppermute x5, starting transfers between devices, along(): return lax.ppermute(array, 'tensor', pairs)  9.49 us
    pallas_call x3, Pallas kernels, norm(): pl.pallas_call(functools.partial(norm_kernel, slots, tuple(arrays)), in_s...  9.49 us
    pallas_call x2, Pallas kernels, finish(): pl.pallas_call(functools.partial(finish_kernel, side, side * rows // TPD...  9.18 us
    ppermute x8, starting transfers between devices, swap(): return lax.ppermute(array, 'dp', [(i, i ^ bits) for i in range(8)])  8.06 us
  transfers between devices with their start and end apart: 15, of which 4 were waited for; matrix products, arithmetic and copies ran while one was open for 6% of the time, Pallas kernels for 23%

profile of v5, /device:TPU:0, one launch (start us, length us, event | category | flops | bytes accessed | tf_op | source)
XLA Modules:
  0.0 143.6 jit_solution(17302376011100330155)
XLA Ops:
  0.0 2.7 %shard_map.91.refs_3_ = bf16[768,1152]{1,0:T(8,128)(2,1)} custom-call(bf16[768,768]{1,0:T(8,128)(2,1)} %refs_0_.4, bf16[768,768]{1,0:T(8,128)(2,1)} %refs_1_.3, bf16[768,768]{1,0:T(8,128)(2,1)} %refs_2_.3), custom_call_target="tpu_custom_call" | custom-call | tf_op jit(solution)/shard_map/pallas_call | solution.py:154
  2.8 3.0 %collective-permute-start.3 = (bf16[768,1152]{1,0:T(8,128)(2,1)}, bf16[768,1152]{1,0:T(8,128)(2,1)}, u32[]{:S(2)}, u32[]{:S(2)}) collective-permute-start(bf16[768,1152]{1,0:T(8,128)(2,1)} %shard_map.91.refs_3_), channel_id=1, source_target_pairs={{0,16},{4,20},{8,24},{12,28},{16,0},{20,4},{24,8},{28,12},{1,17},{... | collective-permute-start | bytes 5308424 | tf_op jit(solution)/shard_map/ppermute | solution.py:103
  5.8 1.5 %collective-permute-start.2 = (bf16[768,1152]{1,0:T(8,128)(2,1)}, bf16[768,1152]{1,0:T(8,128)(2,1)}, u32[]{:S(2)}, u32[]{:S(2)}) collective-permute-start(bf16[768,1152]{1,0:T(8,128)(2,1)} %shard_map.91.refs_3_), channel_id=1, source_target_pairs={{0,8},{4,12},{8,0},{12,4},{16,24},{20,28},{24,16},{28,20},{1,9},{5... | collective-permute-start | bytes 5308424 | tf_op jit(solution)/shard_map/ppermute | solution.py:103
  7.3 1.8 %collective-permute-start.1 = (bf16[512,1536]{1,0:T(8,128)(2,1)}, bf16[512,1536]{1,0:T(8,128)(2,1)}, u32[]{:S(2)}, u32[]{:S(2)}) collective-permute-start(bf16[512,1536]{1,0:T(8,128)(2,1)} %refs_0_.5), channel_id=1, source_target_pairs={{1,2},{2,1},{5,6},{6,5},{9,10},{10,9},{13,14},{14,13},{17,18},{18,... | collective-permute-start | bytes 4718600 | tf_op jit(solution)/shard_map/ppermute | solution.py:498
  9.1 3.3 %collective-permute-start = (bf16[512,1536]{1,0:T(8,128)(2,1)}, bf16[512,1536]{1,0:T(8,128)(2,1)}, u32[]{:S(2)}, u32[]{:S(2)}) collective-permute-start(bf16[512,1536]{1,0:T(8,128)(2,1)} %refs_0_.5), channel_id=1, source_target_pairs={{0,1},{1,0},{2,3},{3,2},{4,5},{5,4},{6,7},{7,6},{8,9},{9,8},{10,11... | collective-permute-start | bytes 4718600 | tf_op jit(solution)/shard_map/ppermute | solution.py:498
  13.1 3.2 %all-to-all-start = ((f32[2,1,32]{2,1,0:T(1,128)}), f32[2,1,32]{2,1,0:T(1,128)S(1)}, u32[]{:S(2)}, u32[]{:S(2)}) async-start(f32[2,1,32]{2,1,0:T(1,128)} %bitcast.3), calls=%async_computation | async-start | bytes 2048 | tf_op jit(solution)/shard_map/all_to_all | solution.py:107
  16.3 2.9 %shard_map.92.refs_0_ = bf16[768,1152]{1,0:T(8,128)(2,1)} custom-call(bf16[768,768]{1,0:T(8,128)(2,1)} %refs_0_.4, bf16[768,768]{1,0:T(8,128)(2,1)} %refs_1_.3, bf16[768,768]{1,0:T(8,128)(2,1)} %refs_2_.3, bf16[768,1152]{1,0:T(8,128)(2,1)} %shard_map.91.refs_3_), custom_call_target="tpu_custom_call" | custom-call | tf_op jit(solution)/shard_map/pallas_call | solution.py:154
  19.3 3.9 %maximum_select_fusion = bf16[2,768,1152]{2,1,0:T(8,128)(2,1)} fusion(bf16[1,768,1152]{2,1,0:T(8,128)(2,1)} %bitcast.7, bf16[1,768,1152]{2,1,0:T(8,128)(2,1)S(1)} %bitcast.20, pred[]{:T(512)S(6)} %eq.6), kind=kLoop, calls=%fused_computation.2 | loop fusion | flops 5308416 | bytes 7077889 | tf_op jit(solution)/shard_map/jit(_where)/select_n | solution.py:506
  23.2 4.0 %all-to-all-start.1 = ((bf16[2,768,1152]{2,1,0:T(8,128)(2,1)}), bf16[2,768,1152]{2,1,0:T(8,128)(2,1)S(1)}, u32[]{:S(2)}, u32[]{:S(2)}) async-start(bf16[2,768,1152]{2,1,0:T(8,128)(2,1)} %maximum_select_fusion), calls=%async_computation.1 | async-start | bytes 7077888 | tf_op jit(solution)/shard_map/all_to_all | solution.py:107
  27.8 0.7 reduce.3
  28.5 2.0 %convert_reduce_fusion = (f32[512]{0:T(512)S(1)}, f32[512]{0:T(512)S(1)}) fusion(bf16[512,1536]{1,0:T(8,128)(2,1)} %refs_0_.5), kind=kLoop, calls=%fused_computation.1 | loop fusion | flops 3144704 | bytes 1576960 | tf_op jit(solution)/shard_map/reduce_sum | solution.py:504
  31.1 16.3 %all_to_all.29.refs_3_ = f32[4,2,512]{2,1,0:T(2,128)S(1)} all-to-all(f32[4,2,512]{2,1,0:T(2,128)S(1)} %stack.37), channel_id=1, replica_groups=mesh['dp'=8,'tensor'=4] {'tensor'}, dimensions={0} | all-to-all | bytes 32768 | tf_op jit(solution)/shard_map/all_to_all | solution.py:510
  47.5 0.7 collective-permute-start.4
  48.3 1.8 %collective-permute-start.6 = (bf16[512,1536]{1,0:T(8,128)(2,1)}, bf16[512,1536]{1,0:T(8,128)(2,1)}, u32[]{:S(2)}, u32[]{:S(2)}) collective-permute-start(bf16[512,1536]{1,0:T(8,128)(2,1)} %get-tuple-element.17.refs_1_), channel_id=1, source_target_pairs={{1,2},{2,1},{5,6},{6,5},{9,10},{10,9},{13,14},{14,13},{17,18},{18,... | collective-permute-start | bytes 4718600 | tf_op jit(solution)/shard_map/ppermute | solution.py:498
  50.1 1.3 collective-permute-start.5
  51.4 0.7 dynamic-slice_bitcast_fusion
  52.2 0.7 copy-done
  52.9 4.5 %shard_map.95 = bf16[2,2,512,1536]{3,2,1,0:T(8,128)(2,1)S(1)} custom-call(s32[17]{0:T(128)S(1)} %pad_add_fusion.plan_ref, f32[4,2,512]{2,1,0:T(2,128)S(1)} %get-tuple-element.16.stats_ref, f32[1,6144]{1,0:T(1,128)S(1)} %bitcast.13, bf16[512,1536]{1,0:T(8,128)(2,1)} %refs_0_.5, bf16[512,1536]{1,0:T(8,128)(2,1)} %get-tuple-element.17.refs_1_), custom_call_target="tpu_custom_call" | custom-call | tf_op jit(solution)/shard_map/pallas_call | solution.py:209
  57.4 8.8 %all_to_all.30.refs_5_.refs_0_ = bf16[2,2,512,1536]{3,2,1,0:T(8,128)(2,1)S(1)} all-to-all(bf16[2,2,512,1536]{3,2,1,0:T(8,128)(2,1)S(1)} %shard_map.95), channel_id=1, replica_groups={{0,4},{8,12},{16,20},{24,28},{1,5},{9,13},{17,21},{25,29},{2,6},{10,14}..., dimensions={0} | all-to-all | bytes 12582912 | tf_op jit(solution)/shard_map/all_to_all | solution.py:107
  66.2 22.6 %collective-permute-done.5.refs_2_ = bf16[512,1536]{1,0:T(8,128)(2,1)} collective-permute-done((bf16[512,1536]{1,0:T(8,128)(2,1)}, bf16[512,1536]{1,0:T(8,128)(2,1)}, u32[]{:S(2)}, u32[]{:S(2)}) %collective-permute-start.5) | collective-permute-done | bytes 1572896 | tf_op jit(solution)/shard_map/ppermute | solution.py:498
  88.7 1.3 collective-permute-start.8
  90.0 1.4 collective-permute-start.9
  91.4 0.7 collective-permute-start.10
  92.1 3.2 %shard_map.97 = bf16[2,1,512,1536]{3,2,1,0:T(8,128)(2,1)S(1)} custom-call(s32[17]{0:T(128)S(1)} %pad_add_fusion.plan_ref, f32[4,2,512]{2,1,0:T(2,128)S(1)} %get-tuple-element.16.stats_ref, f32[1,6144]{1,0:T(1,128)S(1)} %bitcast.14, bf16[512,1536]{1,0:T(8,128)(2,1)} %get-tuple-element.18.refs_0_, bf16[512,1536]{1,0:T(8,128)(2,1)} %get-tuple-element.20.refs_1_), custom_call_target="tpu_custom_call" | custom-call | tf_op jit(solution)/shard_map/pallas_call | solution.py:209
  95.3 6.3 %all_to_all.31.refs_1_ = bf16[2,1,512,1536]{3,2,1,0:T(8,128)(2,1)S(1)} all-to-all(bf16[2,1,512,1536]{3,2,1,0:T(8,128)(2,1)S(1)} %shard_map.97), channel_id=1, replica_groups={{0,4},{8,12},{16,20},{24,28},{1,5},{9,13},{17,21},{25,29},{2,6},{10,14}..., dimensions={0} | all-to-all | bytes 6291456 | tf_op jit(solution)/shard_map/all_to_all | solution.py:107
  101.6 13.7 %shard_map.98 = (f32[4,256,1152]{2,1,0:T(8,128)S(1)}, bf16[4,256,1536]{2,1,0:T(8,128)(2,1)S(1)}, bf16[1536,1152]{1,0:T(8,128)(2,1)S(1)}) custom-call(s32[17]{0:T(128)S(1)} %pad_add_fusion.plan_ref, bf16[2,2,512,1536]{3,2,1,0:T(8,128)(2,1)S(1)} %all_to_all.30.refs_5_.refs_0_, bf16[2,1,512,1536]{3,2,1,0:T(8,128)(2,1)S(1)} %all_to_all.31.refs_1_, ...), custom_call_target="tpu_custom_call" | custom-call | tf_op jit(solution)/shard_map/pallas_call | solution.py:332
  115.3 11.9 %collective-permute-done.8.refs_1_ = bf16[512,1536]{1,0:T(8,128)(2,1)S(1)} collective-permute-done((bf16[512,1536]{1,0:T(8,128)(2,1)}, bf16[512,1536]{1,0:T(8,128)(2,1)S(1)}, u32[]{:S(2)}, u32[]{:S(2)}) %collective-permute-start.8) | collective-permute-done | bytes 1572896 | tf_op jit(solution)/shard_map/ppermute | solution.py:498
  127.2 1.8 %shard_map.99.last_ref = bf16[1,1,512,1536]{3,2,1,0:T(8,128)(2,1)S(1)} custom-call(s32[17]{0:T(128)S(1)} %pad_add_fusion.plan_ref, f32[4,2,512]{2,1,0:T(2,128)S(1)} %get-tuple-element.16.stats_ref, f32[1,6144]{1,0:T(1,128)S(1)} %bitcast.15, bf16[512,1536]{1,0:T(8,128)(2,1)} %get-tuple-element.26.refs_0_, ...), custom_call_target="tpu_custom_call" | custom-call | tf_op jit(solution)/shard_map/pallas_call | solution.py:209
  129.1 2.9 %shard_map.100.refs_1_.total_ref = f32[2,256,1152]{2,1,0:T(8,128)S(1)} custom-call(s32[17]{0:T(128)S(1)} %pad_add_fusion.plan_ref, f32[4,256,1152]{2,1,0:T(8,128)S(1)} %get-tuple-element.23.refs_2_.total_ref, bf16[4,256,1536]{2,1,0:T(8,128)(2,1)S(1)} %get-tuple-element.24.next_tokens, bf16[1536,1152]{1,0:T(8,128)(2,1)S(1)} %get-tuple-element.25.next_weights.refs_0_, ...), custom_call_target="tpu_custom_call" | custom-call | tf_op jit(solution)/shard_map/pallas_call | solution.py:419
  132.8 5.7 %shard_map.102.refs_0_ = bf16[512,384]{1,0:T(8,128)(2,1)S(1)} custom-call(s32[17]{0:T(128)S(1)} %pad_add_fusion.plan_ref, f32[64]{0:T(128)S(1)} %copy-done.3, f32[4,256,1152]{2,1,0:T(8,128)S(1)} %get-tuple-element.23.refs_2_.total_ref, bf16[4,256,1536]{2,1,0:T(8,128)(2,1)S(1)} %get-tuple-element.24.next_tokens, ...), custom_call_target="tpu_custom_call" | custom-call | tf_op jit(solution)/shard_map/pallas_call | solution.py:475
  139.0 3.5 %shard_map.103 = bf16[512,384]{1,0:T(8,128)(2,1)S(1)} custom-call(s32[17]{0:T(128)S(1)} %pad_add_fusion.plan_ref, f32[64]{0:T(128)S(1)} %copy-done.3, f32[2,256,1152]{2,1,0:T(8,128)S(1)} %shard_map.100.refs_1_.total_ref, bf16[4,256,1536]{2,1,0:T(8,128)(2,1)S(1)} %get-tuple-element.24.next_tokens, bf16[1,1,512,1536]{3,2,1,0:T(8,128)(2,1)S(1)} %shard_map.99.last_ref, ...), custom_call_target="tpu_custom_call" | custom-call | tf_op jit(solution)/shard_map/pallas_call | solution.py:475
  142.5 1.1 maximum_select_fusion.1
  (43 shorter events, 3.4 us)
Async XLA Ops:
  0.0 12.4 %copy-start.7 = (s32[2,4,4]{2,1,0:T(4,128)S(1)}, s32[2,4,4]{2,1,0:T(4,128)}, u32[]{:S(2)}) copy-start(s32[2,4,4]{2,1,0:T(4,128)} %param.10) | copy-start | bytes 388
  2.8 44.7 %collective-permute-start.3 = (bf16[768,1152]{1,0:T(8,128)(2,1)}, bf16[768,1152]{1,0:T(8,128)(2,1)}, u32[]{:S(2)}, u32[]{:S(2)}) collective-permute-start(bf16[768,1152]{1,0:T(8,128)(2,1)} %shard_map.91.refs_3_), channel_id=1, source_target_pairs={{0,16},{4,20},{8,24},{12,28},{16,0},{20,4},{24,8},{28,12},{1,17},{... | collective-permute-start | bytes 5308424 | tf_op jit(solution)/shard_map/ppermute | solution.py:103
  5.8 41.6 %collective-permute-start.2 = (bf16[768,1152]{1,0:T(8,128)(2,1)}, bf16[768,1152]{1,0:T(8,128)(2,1)}, u32[]{:S(2)}, u32[]{:S(2)}) collective-permute-start(bf16[768,1152]{1,0:T(8,128)(2,1)} %shard_map.91.refs_3_), channel_id=1, source_target_pairs={{0,8},{4,12},{8,0},{12,4},{16,24},{20,28},{24,16},{28,20},{1,9},{5... | collective-permute-start | bytes 5308424 | tf_op jit(solution)/shard_map/ppermute | solution.py:103
  7.3 40.1 %collective-permute-start.1 = (bf16[512,1536]{1,0:T(8,128)(2,1)}, bf16[512,1536]{1,0:T(8,128)(2,1)}, u32[]{:S(2)}, u32[]{:S(2)}) collective-permute-start(bf16[512,1536]{1,0:T(8,128)(2,1)} %refs_0_.5), channel_id=1, source_target_pairs={{1,2},{2,1},{5,6},{6,5},{9,10},{10,9},{13,14},{14,13},{17,18},{18,... | collective-permute-start | bytes 4718600 | tf_op jit(solution)/shard_map/ppermute | solution.py:498
  9.1 38.3 %collective-permute-start = (bf16[512,1536]{1,0:T(8,128)(2,1)}, bf16[512,1536]{1,0:T(8,128)(2,1)}, u32[]{:S(2)}, u32[]{:S(2)}) collective-permute-start(bf16[512,1536]{1,0:T(8,128)(2,1)} %refs_0_.5), channel_id=1, source_target_pairs={{0,1},{1,0},{2,3},{3,2},{4,5},{5,4},{6,7},{7,6},{8,9},{9,8},{10,11... | collective-permute-start | bytes 4718600 | tf_op jit(solution)/shard_map/ppermute | solution.py:498
  13.1 10.2 %all-to-all-start = ((f32[2,1,32]{2,1,0:T(1,128)}), f32[2,1,32]{2,1,0:T(1,128)S(1)}, u32[]{:S(2)}, u32[]{:S(2)}) async-start(f32[2,1,32]{2,1,0:T(1,128)} %bitcast.3), calls=%async_computation | async-start | bytes 2048 | tf_op jit(solution)/shard_map/all_to_all | solution.py:107
  16.3 3.0 %copy-start.6 = (bf16[768,1152]{1,0:T(8,128)(2,1)S(1)}, bf16[768,1152]{1,0:T(8,128)(2,1)}, u32[]{:S(2)}) copy-start(bf16[768,1152]{1,0:T(8,128)(2,1)} %shard_map.91.refs_3_) | copy-start | bytes 5308420
  23.2 7.9 %all-to-all-start.1 = ((bf16[2,768,1152]{2,1,0:T(8,128)(2,1)}), bf16[2,768,1152]{2,1,0:T(8,128)(2,1)S(1)}, u32[]{:S(2)}, u32[]{:S(2)}) async-start(bf16[2,768,1152]{2,1,0:T(8,128)(2,1)} %maximum_select_fusion), calls=%async_computation.1 | async-start | bytes 7077888 | tf_op jit(solution)/shard_map/all_to_all | solution.py:107
  28.5 2.6 %copy-start.2 = (f32[64]{0:T(128)}, f32[64]{0:T(128)S(1)}, u32[]{:S(2)}) copy-start(f32[64]{0:T(128)S(1)} %reshape.15.refs_2_.mask_ref) | copy-start | bytes 772
  47.4 41.3 %collective-permute-start.7 = (bf16[768,1152]{1,0:T(8,128)(2,1)}, bf16[768,1152]{1,0:T(8,128)(2,1)}, u32[]{:S(2)}, u32[]{:S(2)}) collective-permute-start(bf16[768,1152]{1,0:T(8,128)(2,1)} %get-tuple-element.19), channel_id=1, source_target_pairs={{0,12},{4,8},{8,4},{12,0},{16,28},{20,24},{24,20},{28,16},{1,13},{... | collective-permute-start | bytes 5308424 | tf_op jit(solution)/shard_map/ppermute | solution.py:103
  47.5 41.2 %collective-permute-start.4 = (bf16[768,1152]{1,0:T(8,128)(2,1)}, bf16[768,1152]{1,0:T(8,128)(2,1)}, u32[]{:S(2)}, u32[]{:S(2)}) collective-permute-start(bf16[768,1152]{1,0:T(8,128)(2,1)} %get-tuple-element.19), channel_id=1, source_target_pairs={{0,20},{4,16},{8,28},{12,24},{16,4},{20,0},{24,12},{28,8},{1,21},{... | collective-permute-start | bytes 5308424 | tf_op jit(solution)/shard_map/ppermute | solution.py:103
  48.3 17.9 %collective-permute-start.6 = (bf16[512,1536]{1,0:T(8,128)(2,1)}, bf16[512,1536]{1,0:T(8,128)(2,1)}, u32[]{:S(2)}, u32[]{:S(2)}) collective-permute-start(bf16[512,1536]{1,0:T(8,128)(2,1)} %get-tuple-element.17.refs_1_), channel_id=1, source_target_pairs={{1,2},{2,1},{5,6},{6,5},{9,10},{10,9},{13,14},{14,13},{17,18},{18,... | collective-permute-start | bytes 4718600 | tf_op jit(solution)/shard_map/ppermute | solution.py:498
  50.1 38.6 %collective-permute-start.5 = (bf16[512,1536]{1,0:T(8,128)(2,1)}, bf16[512,1536]{1,0:T(8,128)(2,1)}, u32[]{:S(2)}, u32[]{:S(2)}) collective-permute-start(bf16[512,1536]{1,0:T(8,128)(2,1)} %get-tuple-element.18.refs_0_), channel_id=1, source_target_pairs={{1,0},{2,3},{5,4},{6,7},{9,8},{10,11},{13,12},{14,15},{17,16},{18,... | collective-permute-start | bytes 4718600 | tf_op jit(solution)/shard_map/ppermute | solution.py:498
  52.2 0.7 copy-start
  88.7 38.5 %collective-permute-start.8 = (bf16[512,1536]{1,0:T(8,128)(2,1)}, bf16[512,1536]{1,0:T(8,128)(2,1)S(1)}, u32[]{:S(2)}, u32[]{:S(2)}) collective-permute-start(bf16[512,1536]{1,0:T(8,128)(2,1)} %get-tuple-element.26.refs_0_), channel_id=1, source_target_pairs={{1,0},{2,3},{5,4},{6,7},{9,8},{10,11},{13,12},{14,15},{17,16},{18,... | collective-permute-start | bytes 4718600 | tf_op jit(solution)/shard_map/ppermute | solution.py:498
  90.0 42.5 %collective-permute-start.9 = (bf16[768,1152]{1,0:T(8,128)(2,1)}, bf16[768,1152]{1,0:T(8,128)(2,1)S(1)}, u32[]{:S(2)}, u32[]{:S(2)}) collective-permute-start(bf16[768,1152]{1,0:T(8,128)(2,1)} %get-tuple-element.21.refs_3_), channel_id=1, source_target_pairs={{0,16},{4,20},{8,24},{12,28},{16,0},{20,4},{24,8},{28,12},{1,17},{... | collective-permute-start | bytes 5308424 | tf_op jit(solution)/shard_map/ppermute | solution.py:103
  91.4 41.1 %collective-permute-start.10 = (bf16[768,1152]{1,0:T(8,128)(2,1)}, bf16[768,1152]{1,0:T(8,128)(2,1)S(1)}, u32[]{:S(2)}, u32[]{:S(2)}) collective-permute-start(bf16[768,1152]{1,0:T(8,128)(2,1)} %get-tuple-element.22.refs_6_), channel_id=1, source_target_pairs={{0,8},{4,12},{8,0},{12,4},{16,24},{20,28},{24,16},{28,20},{1,9},{5... | collective-permute-start | bytes 5308424 | tf_op jit(solution)/shard_map/ppermute | solution.py:103
  101.6 25.6 %copy-start.1 = (f32[6144]{0:T(1024)S(1)}, f32[6144]{0:T(1024)}, u32[]{:S(2)}) copy-start(f32[6144]{0:T(1024)} %param.11) | copy-start | bytes 73732
  129.0 3.5 %collective-permute-start.11 = (bf16[1,1,512,1536]{3,2,1,0:T(8,128)(2,1)S(1)}, bf16[1,1,512,1536]{3,2,1,0:T(8,128)(2,1)S(1)}, u32[]{:S(2)}, u32[]{:S(2)}) collective-permute-start(bf16[1,1,512,1536]{3,2,1,0:T(8,128)(2,1)S(1)} %shard_map.99.last_ref), channel_id=1, source_target_pairs={{0,4},{4,0},{8,12},{12,8},{16,20},{20,16},{24,28},{28,24},{1,5},{5... | collective-permute-start | bytes 4718600 | tf_op jit(solution)/shard_map/ppermute | solution.py:103
  132.1 0.7 copy-start.3
  132.1 0.7 copy-start.4
  132.1 0.7 copy-start.5
  138.4 4.1 %collective-permute-start.12 = (bf16[512,384]{1,0:T(8,128)(2,1)S(1)}, bf16[512,384]{1,0:T(8,128)(2,1)S(1)}, u32[]{:S(2)}, u32[]{:S(2)}) collective-permute-start(bf16[512,384]{1,0:T(8,128)(2,1)S(1)} %shard_map.102.refs_0_), channel_id=1, source_target_pairs={{0,4},{4,0},{8,12},{12,8},{16,20},{20,16},{24,28},{28,24},{1,5},{5... | collective-permute-start | bytes 1179656 | tf_op jit(solution)/shard_map/ppermute | solution.py:103

commit v6 on v5

--- a/solution.py
+++ b/solution.py
@@ -130,7 +130,7 @@
 
 
 def pack_kernel(theirs, *refs):
-    weights, out_ref, held, in_sems = refs[:3], *refs[-3:]
+    weights, out_ref, held, packed, in_sems, out_sems = refs[:3], *refs[-5:]
     core = lax.axis_index("dp") % 2
     width = held.shape[2]
     heads = width // DH
@@ -141,24 +141,35 @@
             weights[kind].at[:, pl.ds(first, width)], held.at[kind], in_sems.at[kind]
         )
 
+    def store(number):
+        at = pl.ds(0, 2 * width) if number == 0 else pl.ds(2 * width, width)
+        return pltpu.make_async_copy(packed.at[:, at], out_ref.at[:, at], out_sems.at[number])
+
     for kind in range(3):
         load(kind).start()
     for kind, firsts in enumerate(columns_of(heads)):
         load(kind).wait()
         for h, first in enumerate(firsts):
-            out_ref[:, first : first + DH] = held[kind, :, h * DH : (h + 1) * DH]
+            packed[:, first : first + DH] = held[kind, :, h * DH : (h + 1) * DH]
+        if kind > 0:
+            store(kind - 1).start()
+    for number in range(2):
+        store(number).wait()
 
 
 def pack(theirs, weights, *others):
     rows, columns = weights[0].shape
+    shape = (rows, 3 * columns // 2)
     return pl.pallas_call(
         functools.partial(pack_kernel, theirs),
         in_specs=[HBM] * 3 + [ANY] * len(others),
-        out_specs=VMEM,
-        out_shape=jax.ShapeDtypeStruct((rows, 3 * columns // 2), jnp.bfloat16),
+        out_specs=HBM,
+        out_shape=jax.ShapeDtypeStruct(shape, jnp.bfloat16),
         scratch_shapes=[
             pltpu.VMEM((3, rows, columns // 2), jnp.bfloat16),
+            pltpu.VMEM(shape, jnp.bfloat16),
             pltpu.SemaphoreType.DMA((3,)),
+            pltpu.SemaphoreType.DMA((2,)),
         ],
         compiler_params=params(56),
         cost_estimate=FREE,

time: 144 us -> 144 us (level)
  no operation moved by 1% of the time
where the time goes in v6:
time: 144 us; the launch traced here: 143 us
  Pallas kernels  40.8 us (28%)
  waiting for transfers between devices  35.6 us (25%)
  blocking collectives  31.4 us (22%)
  starting transfers between devices  24.8 us (17%)
  other arithmetic  8.33 us (6%)
  local copies, waits for them, and re-layouts  2.38 us (2%)
    ppermute x5, waiting for transfers between devices, along(): return lax.ppermute(array, 'tensor', pairs)  34.5 us
    all_to_all x1, blocking collectives, per_device_8x4(): stats = lax.all_to_all(jnp.stack([stats] * 4), 'tensor', 0, 0)  16.4 us
    all_to_all x2, blocking collectives, trade(): lax.all_to_all(array, 'dp', 0, 0, axis_index_groups=[[i, i + 1] for i in...  15 us
    pallas_call x1, Pallas kernels, project(): pl.pallas_call(functools.partial(project_kernel, tokens), in_specs=[SMEM]...  13.7 us
    ppermute x5, starting transfers between devices, along(): return lax.ppermute(array, 'tensor', pairs)  9.49 us
    pallas_call x3, Pallas kernels, norm(): pl.pallas_call(functools.partial(norm_kernel, slots, tuple(arrays)), in_s...  9.49 us
    pallas_call x2, Pallas kernels, finish(): pl.pallas_call(functools.partial(finish_kernel, side, side * rows // TPD...  9.18 us
    ppermute x8, starting transfers between devices, swap(): return lax.ppermute(array, 'dp', [(i, i ^ bits) for i in range(8)])  8.06 us
  transfers between devices with their start and end apart: 15, of which 4 were waited for; matrix products, arithmetic and copies ran while one was open for 6% of the time, Pallas kernels for 23%

profile of v6, /device:TPU:0, one launch (start us, length us, event | category | flops | bytes accessed | tf_op | source)
XLA Modules:
  0.0 143.5 jit_solution(6306445837535792390)
XLA Ops:
  0.0 2.6 %shard_map.91.refs_3_ = bf16[768,1152]{1,0:T(8,128)(2,1)} custom-call(bf16[768,768]{1,0:T(8,128)(2,1)} %refs_0_.4, bf16[768,768]{1,0:T(8,128)(2,1)} %refs_1_.3, bf16[768,768]{1,0:T(8,128)(2,1)} %refs_2_.3), custom_call_target="tpu_custom_call" | custom-call | tf_op jit(solution)/shard_map/pallas_call | solution.py:163
  2.6 3.0 %collective-permute-start.3 = (bf16[768,1152]{1,0:T(8,128)(2,1)}, bf16[768,1152]{1,0:T(8,128)(2,1)}, u32[]{:S(2)}, u32[]{:S(2)}) collective-permute-start(bf16[768,1152]{1,0:T(8,128)(2,1)} %shard_map.91.refs_3_), channel_id=1, source_target_pairs={{0,16},{4,20},{8,24},{12,28},{16,0},{20,4},{24,8},{28,12},{1,17},{... | collective-permute-start | bytes 5308424 | tf_op jit(solution)/shard_map/ppermute | solution.py:103
  5.7 1.5 %collective-permute-start.2 = (bf16[768,1152]{1,0:T(8,128)(2,1)}, bf16[768,1152]{1,0:T(8,128)(2,1)}, u32[]{:S(2)}, u32[]{:S(2)}) collective-permute-start(bf16[768,1152]{1,0:T(8,128)(2,1)} %shard_map.91.refs_3_), channel_id=1, source_target_pairs={{0,8},{4,12},{8,0},{12,4},{16,24},{20,28},{24,16},{28,20},{1,9},{5... | collective-permute-start | bytes 5308424 | tf_op jit(solution)/shard_map/ppermute | solution.py:103
  7.2 1.8 %collective-permute-start.1 = (bf16[512,1536]{1,0:T(8,128)(2,1)}, bf16[512,1536]{1,0:T(8,128)(2,1)}, u32[]{:S(2)}, u32[]{:S(2)}) collective-permute-start(bf16[512,1536]{1,0:T(8,128)(2,1)} %refs_0_.5), channel_id=1, source_target_pairs={{1,2},{2,1},{5,6},{6,5},{9,10},{10,9},{13,14},{14,13},{17,18},{18,... | collective-permute-start | bytes 4718600 | tf_op jit(solution)/shard_map/ppermute | solution.py:509
  9.0 3.3 %collective-permute-start = (bf16[512,1536]{1,0:T(8,128)(2,1)}, bf16[512,1536]{1,0:T(8,128)(2,1)}, u32[]{:S(2)}, u32[]{:S(2)}) collective-permute-start(bf16[512,1536]{1,0:T(8,128)(2,1)} %refs_0_.5), channel_id=1, source_target_pairs={{0,1},{1,0},{2,3},{3,2},{4,5},{5,4},{6,7},{7,6},{8,9},{9,8},{10,11... | collective-permute-start | bytes 4718600 | tf_op jit(solution)/shard_map/ppermute | solution.py:509
  13.0 3.2 %all-to-all-start = ((f32[2,1,32]{2,1,0:T(1,128)}), f32[2,1,32]{2,1,0:T(1,128)S(1)}, u32[]{:S(2)}, u32[]{:S(2)}) async-start(f32[2,1,32]{2,1,0:T(1,128)} %bitcast.3), calls=%async_computation | async-start | bytes 2048 | tf_op jit(solution)/shard_map/all_to_all | solution.py:107
  16.2 2.8 %shard_map.92.refs_0_ = bf16[768,1152]{1,0:T(8,128)(2,1)} custom-call(bf16[768,768]{1,0:T(8,128)(2,1)} %refs_0_.4, bf16[768,768]{1,0:T(8,128)(2,1)} %refs_1_.3, bf16[768,768]{1,0:T(8,128)(2,1)} %refs_2_.3, bf16[768,1152]{1,0:T(8,128)(2,1)} %shard_map.91.refs_3_), custom_call_target="tpu_custom_call" | custom-call | tf_op jit(solution)/shard_map/pallas_call | solution.py:163
  19.0 3.9 %maximum_select_fusion = bf16[2,768,1152]{2,1,0:T(8,128)(2,1)} fusion(bf16[1,768,1152]{2,1,0:T(8,128)(2,1)} %bitcast.7, bf16[1,768,1152]{2,1,0:T(8,128)(2,1)S(1)} %bitcast.20, pred[]{:T(512)S(6)} %eq.6), kind=kLoop, calls=%fused_computation.2 | loop fusion | flops 5308416 | bytes 7077889 | tf_op jit(solution)/shard_map/jit(_where)/select_n | solution.py:517
  23.0 4.0 %all-to-all-start.1 = ((bf16[2,768,1152]{2,1,0:T(8,128)(2,1)}), bf16[2,768,1152]{2,1,0:T(8,128)(2,1)S(1)}, u32[]{:S(2)}, u32[]{:S(2)}) async-start(bf16[2,768,1152]{2,1,0:T(8,128)(2,1)} %maximum_select_fusion), calls=%async_computation.1 | async-start | bytes 7077888 | tf_op jit(solution)/shard_map/all_to_all | solution.py:107
  27.5 0.7 reduce.3
  28.3 2.0 %convert_reduce_fusion = (f32[512]{0:T(512)S(1)}, f32[512]{0:T(512)S(1)}) fusion(bf16[512,1536]{1,0:T(8,128)(2,1)} %refs_0_.5), kind=kLoop, calls=%fused_computation.1 | loop fusion | flops 3144704 | bytes 1576960 | tf_op jit(solution)/shard_map/reduce_sum | solution.py:515
  30.9 16.4 %all_to_all.29.refs_3_ = f32[4,2,512]{2,1,0:T(2,128)S(1)} all-to-all(f32[4,2,512]{2,1,0:T(2,128)S(1)} %stack.37), channel_id=1, replica_groups=mesh['dp'=8,'tensor'=4] {'tensor'}, dimensions={0} | all-to-all | bytes 32768 | tf_op jit(solution)/shard_map/all_to_all | solution.py:521
  47.4 0.7 collective-permute-start.4
  48.1 1.8 %collective-permute-start.6 = (bf16[512,1536]{1,0:T(8,128)(2,1)}, bf16[512,1536]{1,0:T(8,128)(2,1)}, u32[]{:S(2)}, u32[]{:S(2)}) collective-permute-start(bf16[512,1536]{1,0:T(8,128)(2,1)} %get-tuple-element.17.refs_1_), channel_id=1, source_target_pairs={{1,2},{2,1},{5,6},{6,5},{9,10},{10,9},{13,14},{14,13},{17,18},{18,... | collective-permute-start | bytes 4718600 | tf_op jit(solution)/shard_map/ppermute | solution.py:509
  49.9 1.3 collective-permute-start.5
  51.3 0.7 dynamic-slice_bitcast_fusion
  52.0 0.7 copy-done
  52.8 4.5 %shard_map.95 = bf16[2,2,512,1536]{3,2,1,0:T(8,128)(2,1)S(1)} custom-call(s32[17]{0:T(128)S(1)} %pad_add_fusion.plan_ref, f32[4,2,512]{2,1,0:T(2,128)S(1)} %get-tuple-element.16.stats_ref, f32[1,6144]{1,0:T(1,128)S(1)} %bitcast.13, bf16[512,1536]{1,0:T(8,128)(2,1)} %refs_0_.5, bf16[512,1536]{1,0:T(8,128)(2,1)} %get-tuple-element.17.refs_1_), custom_call_target="tpu_custom_call" | custom-call | tf_op jit(solution)/shard_map/pallas_call | solution.py:220
  57.2 8.8 %all_to_all.30.refs_5_.refs_0_ = bf16[2,2,512,1536]{3,2,1,0:T(8,128)(2,1)S(1)} all-to-all(bf16[2,2,512,1536]{3,2,1,0:T(8,128)(2,1)S(1)} %shard_map.95), channel_id=1, replica_groups={{0,4},{8,12},{16,20},{24,28},{1,5},{9,13},{17,21},{25,29},{2,6},{10,14}..., dimensions={0} | all-to-all | bytes 12582912 | tf_op jit(solution)/shard_map/all_to_all | solution.py:107
  66.0 22.6 %collective-permute-done.5.refs_2_ = bf16[512,1536]{1,0:T(8,128)(2,1)} collective-permute-done((bf16[512,1536]{1,0:T(8,128)(2,1)}, bf16[512,1536]{1,0:T(8,128)(2,1)}, u32[]{:S(2)}, u32[]{:S(2)}) %collective-permute-start.5) | collective-permute-done | bytes 1572896 | tf_op jit(solution)/shard_map/ppermute | solution.py:509
  88.6 1.3 collective-permute-start.8
  89.9 1.4 collective-permute-start.9
  91.3 0.7 collective-permute-start.10
  92.0 3.2 %shard_map.97 = bf16[2,1,512,1536]{3,2,1,0:T(8,128)(2,1)S(1)} custom-call(s32[17]{0:T(128)S(1)} %pad_add_fusion.plan_ref, f32[4,2,512]{2,1,0:T(2,128)S(1)} %get-tuple-element.16.stats_ref, f32[1,6144]{1,0:T(1,128)S(1)} %bitcast.14, bf16[512,1536]{1,0:T(8,128)(2,1)} %get-tuple-element.18.refs_0_, bf16[512,1536]{1,0:T(8,128)(2,1)} %get-tuple-element.20.refs_1_), custom_call_target="tpu_custom_call" | custom-call | tf_op jit(solution)/shard_map/pallas_call | solution.py:220
  95.2 6.3 %all_to_all.31.refs_1_ = bf16[2,1,512,1536]{3,2,1,0:T(8,128)(2,1)S(1)} all-to-all(bf16[2,1,512,1536]{3,2,1,0:T(8,128)(2,1)S(1)} %shard_map.97), channel_id=1, replica_groups={{0,4},{8,12},{16,20},{24,28},{1,5},{9,13},{17,21},{25,29},{2,6},{10,14}..., dimensions={0} | all-to-all | bytes 6291456 | tf_op jit(solution)/shard_map/all_to_all | solution.py:107
  101.5 13.7 %shard_map.98 = (f32[4,256,1152]{2,1,0:T(8,128)S(1)}, bf16[4,256,1536]{2,1,0:T(8,128)(2,1)S(1)}, bf16[1536,1152]{1,0:T(8,128)(2,1)S(1)}) custom-call(s32[17]{0:T(128)S(1)} %pad_add_fusion.plan_ref, bf16[2,2,512,1536]{3,2,1,0:T(8,128)(2,1)S(1)} %all_to_all.30.refs_5_.refs_0_, bf16[2,1,512,1536]{3,2,1,0:T(8,128)(2,1)S(1)} %all_to_all.31.refs_1_, ...), custom_call_target="tpu_custom_call" | custom-call | tf_op jit(solution)/shard_map/pallas_call | solution.py:343
  115.2 11.9 %collective-permute-done.8.refs_1_ = bf16[512,1536]{1,0:T(8,128)(2,1)S(1)} collective-permute-done((bf16[512,1536]{1,0:T(8,128)(2,1)}, bf16[512,1536]{1,0:T(8,128)(2,1)S(1)}, u32[]{:S(2)}, u32[]{:S(2)}) %collective-permute-start.8) | collective-permute-done | bytes 1572896 | tf_op jit(solution)/shard_map/ppermute | solution.py:509
  127.1 1.8 %shard_map.99.last_ref = bf16[1,1,512,1536]{3,2,1,0:T(8,128)(2,1)S(1)} custom-call(s32[17]{0:T(128)S(1)} %pad_add_fusion.plan_ref, f32[4,2,512]{2,1,0:T(2,128)S(1)} %get-tuple-element.16.stats_ref, f32[1,6144]{1,0:T(1,128)S(1)} %bitcast.15, bf16[512,1536]{1,0:T(8,128)(2,1)} %get-tuple-element.26.refs_0_, ...), custom_call_target="tpu_custom_call" | custom-call | tf_op jit(solution)/shard_map/pallas_call | solution.py:220
  129.0 2.9 %shard_map.100.refs_1_.total_ref = f32[2,256,1152]{2,1,0:T(8,128)S(1)} custom-call(s32[17]{0:T(128)S(1)} %pad_add_fusion.plan_ref, f32[4,256,1152]{2,1,0:T(8,128)S(1)} %get-tuple-element.23.refs_2_.total_ref, bf16[4,256,1536]{2,1,0:T(8,128)(2,1)S(1)} %get-tuple-element.24.next_tokens, bf16[1536,1152]{1,0:T(8,128)(2,1)S(1)} %get-tuple-element.25.next_weights.refs_0_, ...), custom_call_target="tpu_custom_call" | custom-call | tf_op jit(solution)/shard_map/pallas_call | solution.py:430
  132.6 5.7 %shard_map.102.refs_0_ = bf16[512,384]{1,0:T(8,128)(2,1)S(1)} custom-call(s32[17]{0:T(128)S(1)} %pad_add_fusion.plan_ref, f32[64]{0:T(128)S(1)} %copy-done.3, f32[4,256,1152]{2,1,0:T(8,128)S(1)} %get-tuple-element.23.refs_2_.total_ref, bf16[4,256,1536]{2,1,0:T(8,128)(2,1)S(1)} %get-tuple-element.24.next_tokens, ...), custom_call_target="tpu_custom_call" | custom-call | tf_op jit(solution)/shard_map/pallas_call | solution.py:486
  138.9 3.5 %shard_map.103 = bf16[512,384]{1,0:T(8,128)(2,1)S(1)} custom-call(s32[17]{0:T(128)S(1)} %pad_add_fusion.plan_ref, f32[64]{0:T(128)S(1)} %copy-done.3, f32[2,256,1152]{2,1,0:T(8,128)S(1)} %shard_map.100.refs_1_.total_ref, bf16[4,256,1536]{2,1,0:T(8,128)(2,1)S(1)} %get-tuple-element.24.next_tokens, bf16[1,1,512,1536]{3,2,1,0:T(8,128)(2,1)S(1)} %shard_map.99.last_ref, ...), custom_call_target="tpu_custom_call" | custom-call | tf_op jit(solution)/shard_map/pallas_call | solution.py:486
  142.4 1.1 maximum_select_fusion.1
  (43 shorter events, 3.4 us)
Async XLA Ops:
  0.0 12.3 %copy-start.7 = (s32[2,4,4]{2,1,0:T(4,128)S(1)}, s32[2,4,4]{2,1,0:T(4,128)}, u32[]{:S(2)}) copy-start(s32[2,4,4]{2,1,0:T(4,128)} %param.10) | copy-start | bytes 388
  2.6 44.7 %collective-permute-start.3 = (bf16[768,1152]{1,0:T(8,128)(2,1)}, bf16[768,1152]{1,0:T(8,128)(2,1)}, u32[]{:S(2)}, u32[]{:S(2)}) collective-permute-start(bf16[768,1152]{1,0:T(8,128)(2,1)} %shard_map.91.refs_3_), channel_id=1, source_target_pairs={{0,16},{4,20},{8,24},{12,28},{16,0},{20,4},{24,8},{28,12},{1,17},{... | collective-permute-start | bytes 5308424 | tf_op jit(solution)/shard_map/ppermute | solution.py:103
  5.7 41.6 %collective-permute-start.2 = (bf16[768,1152]{1,0:T(8,128)(2,1)}, bf16[768,1152]{1,0:T(8,128)(2,1)}, u32[]{:S(2)}, u32[]{:S(2)}) collective-permute-start(bf16[768,1152]{1,0:T(8,128)(2,1)} %shard_map.91.refs_3_), channel_id=1, source_target_pairs={{0,8},{4,12},{8,0},{12,4},{16,24},{20,28},{24,16},{28,20},{1,9},{5... | collective-permute-start | bytes 5308424 | tf_op jit(solution)/shard_map/ppermute | solution.py:103
  7.2 40.1 %collective-permute-start.1 = (bf16[512,1536]{1,0:T(8,128)(2,1)}, bf16[512,1536]{1,0:T(8,128)(2,1)}, u32[]{:S(2)}, u32[]{:S(2)}) collective-permute-start(bf16[512,1536]{1,0:T(8,128)(2,1)} %refs_0_.5), channel_id=1, source_target_pairs={{1,2},{2,1},{5,6},{6,5},{9,10},{10,9},{13,14},{14,13},{17,18},{18,... | collective-permute-start | bytes 4718600 | tf_op jit(solution)/shard_map/ppermute | solution.py:509
  9.0 38.3 %collective-permute-start = (bf16[512,1536]{1,0:T(8,128)(2,1)}, bf16[512,1536]{1,0:T(8,128)(2,1)}, u32[]{:S(2)}, u32[]{:S(2)}) collective-permute-start(bf16[512,1536]{1,0:T(8,128)(2,1)} %refs_0_.5), channel_id=1, source_target_pairs={{0,1},{1,0},{2,3},{3,2},{4,5},{5,4},{6,7},{7,6},{8,9},{9,8},{10,11... | collective-permute-start | bytes 4718600 | tf_op jit(solution)/shard_map/ppermute | solution.py:509
  13.0 10.0 %all-to-all-start = ((f32[2,1,32]{2,1,0:T(1,128)}), f32[2,1,32]{2,1,0:T(1,128)S(1)}, u32[]{:S(2)}, u32[]{:S(2)}) async-start(f32[2,1,32]{2,1,0:T(1,128)} %bitcast.3), calls=%async_computation | async-start | bytes 2048 | tf_op jit(solution)/shard_map/all_to_all | solution.py:107
  16.2 2.8 %copy-start.6 = (bf16[768,1152]{1,0:T(8,128)(2,1)S(1)}, bf16[768,1152]{1,0:T(8,128)(2,1)}, u32[]{:S(2)}) copy-start(bf16[768,1152]{1,0:T(8,128)(2,1)} %shard_map.91.refs_3_) | copy-start | bytes 5308420
  23.0 7.9 %all-to-all-start.1 = ((bf16[2,768,1152]{2,1,0:T(8,128)(2,1)}), bf16[2,768,1152]{2,1,0:T(8,128)(2,1)S(1)}, u32[]{:S(2)}, u32[]{:S(2)}) async-start(bf16[2,768,1152]{2,1,0:T(8,128)(2,1)} %maximum_select_fusion), calls=%async_computation.1 | async-start | bytes 7077888 | tf_op jit(solution)/shard_map/all_to_all | solution.py:107
  28.3 2.6 %copy-start.2 = (f32[64]{0:T(128)}, f32[64]{0:T(128)S(1)}, u32[]{:S(2)}) copy-start(f32[64]{0:T(128)S(1)} %reshape.15.refs_2_.mask_ref) | copy-start | bytes 772
  47.3 41.3 %collective-permute-start.7 = (bf16[768,1152]{1,0:T(8,128)(2,1)}, bf16[768,1152]{1,0:T(8,128)(2,1)}, u32[]{:S(2)}, u32[]{:S(2)}) collective-permute-start(bf16[768,1152]{1,0:T(8,128)(2,1)} %get-tuple-element.19), channel_id=1, source_target_pairs={{0,12},{4,8},{8,4},{12,0},{16,28},{20,24},{24,20},{28,16},{1,13},{... | collective-permute-start | bytes 5308424 | tf_op jit(solution)/shard_map/ppermute | solution.py:103
  47.4 41.2 %collective-permute-start.4 = (bf16[768,1152]{1,0:T(8,128)(2,1)}, bf16[768,1152]{1,0:T(8,128)(2,1)}, u32[]{:S(2)}, u32[]{:S(2)}) collective-permute-start(bf16[768,1152]{1,0:T(8,128)(2,1)} %get-tuple-element.19), channel_id=1, source_target_pairs={{0,20},{4,16},{8,28},{12,24},{16,4},{20,0},{24,12},{28,8},{1,21},{... | collective-permute-start | bytes 5308424 | tf_op jit(solution)/shard_map/ppermute | solution.py:103
  48.1 17.9 %collective-permute-start.6 = (bf16[512,1536]{1,0:T(8,128)(2,1)}, bf16[512,1536]{1,0:T(8,128)(2,1)}, u32[]{:S(2)}, u32[]{:S(2)}) collective-permute-start(bf16[512,1536]{1,0:T(8,128)(2,1)} %get-tuple-element.17.refs_1_), channel_id=1, source_target_pairs={{1,2},{2,1},{5,6},{6,5},{9,10},{10,9},{13,14},{14,13},{17,18},{18,... | collective-permute-start | bytes 4718600 | tf_op jit(solution)/shard_map/ppermute | solution.py:509
  49.9 38.6 %collective-permute-start.5 = (bf16[512,1536]{1,0:T(8,128)(2,1)}, bf16[512,1536]{1,0:T(8,128)(2,1)}, u32[]{:S(2)}, u32[]{:S(2)}) collective-permute-start(bf16[512,1536]{1,0:T(8,128)(2,1)} %get-tuple-element.18.refs_0_), channel_id=1, source_target_pairs={{1,0},{2,3},{5,4},{6,7},{9,8},{10,11},{13,12},{14,15},{17,16},{18,... | collective-permute-start | bytes 4718600 | tf_op jit(solution)/shard_map/ppermute | solution.py:509
  52.0 0.7 copy-start
  88.6 38.5 %collective-permute-start.8 = (bf16[512,1536]{1,0:T(8,128)(2,1)}, bf16[512,1536]{1,0:T(8,128)(2,1)S(1)}, u32[]{:S(2)}, u32[]{:S(2)}) collective-permute-start(bf16[512,1536]{1,0:T(8,128)(2,1)} %get-tuple-element.26.refs_0_), channel_id=1, source_target_pairs={{1,0},{2,3},{5,4},{6,7},{9,8},{10,11},{13,12},{14,15},{17,16},{18,... | collective-permute-start | bytes 4718600 | tf_op jit(solution)/shard_map/ppermute | solution.py:509
  89.9 42.5 %collective-permute-start.9 = (bf16[768,1152]{1,0:T(8,128)(2,1)}, bf16[768,1152]{1,0:T(8,128)(2,1)S(1)}, u32[]{:S(2)}, u32[]{:S(2)}) collective-permute-start(bf16[768,1152]{1,0:T(8,128)(2,1)} %get-tuple-element.21.refs_3_), channel_id=1, source_target_pairs={{0,16},{4,20},{8,24},{12,28},{16,0},{20,4},{24,8},{28,12},{1,17},{... | collective-permute-start | bytes 5308424 | tf_op jit(solution)/shard_map/ppermute | solution.py:103
  91.3 41.1 %collective-permute-start.10 = (bf16[768,1152]{1,0:T(8,128)(2,1)}, bf16[768,1152]{1,0:T(8,128)(2,1)S(1)}, u32[]{:S(2)}, u32[]{:S(2)}) collective-permute-start(bf16[768,1152]{1,0:T(8,128)(2,1)} %get-tuple-element.22.refs_6_), channel_id=1, source_target_pairs={{0,8},{4,12},{8,0},{12,4},{16,24},{20,28},{24,16},{28,20},{1,9},{5... | collective-permute-start | bytes 5308424 | tf_op jit(solution)/shard_map/ppermute | solution.py:103
  101.5 25.6 %copy-start.1 = (f32[6144]{0:T(1024)S(1)}, f32[6144]{0:T(1024)}, u32[]{:S(2)}) copy-start(f32[6144]{0:T(1024)} %param.11) | copy-start | bytes 73732
  128.9 3.5 %collective-permute-start.11 = (bf16[1,1,512,1536]{3,2,1,0:T(8,128)(2,1)S(1)}, bf16[1,1,512,1536]{3,2,1,0:T(8,128)(2,1)S(1)}, u32[]{:S(2)}, u32[]{:S(2)}) collective-permute-start(bf16[1,1,512,1536]{3,2,1,0:T(8,128)(2,1)S(1)} %shard_map.99.last_ref), channel_id=1, source_target_pairs={{0,4},{4,0},{8,12},{12,8},{16,20},{20,16},{24,28},{28,24},{1,5},{5... | collective-permute-start | bytes 4718600 | tf_op jit(solution)/shard_map/ppermute | solution.py:103
  131.9 0.7 copy-start.3
  132.0 0.7 copy-start.4
  132.0 0.7 copy-start.5
  138.3 4.1 %collective-permute-start.12 = (bf16[512,384]{1,0:T(8,128)(2,1)S(1)}, bf16[512,384]{1,0:T(8,128)(2,1)S(1)}, u32[]{:S(2)}, u32[]{:S(2)}) collective-permute-start(bf16[512,384]{1,0:T(8,128)(2,1)S(1)} %shard_map.102.refs_0_), channel_id=1, source_target_pairs={{0,4},{4,0},{8,12},{12,8},{16,20},{20,16},{24,28},{28,24},{1,5},{5... | collective-permute-start | bytes 1179656 | tf_op jit(solution)/shard_map/ppermute | solution.py:103
